TPU v7x, 32 devices: a whole 2x2x4 slice. The times are simulated.
32 devices in a mesh: groups: 2 (over y), expert: 8 (over z, core), dp: 2 (over x).
Axes of the slice: x: 2, y: 2, z: 4, core: 2. Of those that a mesh axis runs over, the one named last changes fastest.
Arguments:
- tokens: bfloat16 [256, 4096], P(('groups', 'expert', 'dp')), parts along dimension 0, may hold values from -6 to 6
- expert_ids: int32 [256, 8], P(('groups', 'expert', 'dp')), parts along dimension 0, may hold values from 0 to 15, all different within a row; in each aligned block of 8 rows (0 to 7, 8 to 15, ...) at most 8 rows name the same one
- gate_codes: bfloat16 [16, 4096, 1536], P('expert', None, 'dp'), may hold values from -8 to 7, as said below
- up_codes: bfloat16 [16, 4096, 1536], P('expert', None, 'dp'), may hold values from -8 to 7, as said below
- gate_scales: float32 [16, 32, 1536], P('expert', None, 'dp'), may hold values from 0.0015 to 0.006
- up_scales: float32 [16, 32, 1536], P('expert', None, 'dp'), may hold values from 0.0015 to 0.006
Outputs:
- hessian: float32 [32, 1536, 1536], P(('groups', 'expert'), 'dp'), parts along dimension 0
There are 2 independent parts, one for each index of `groups`. A program takes and returns all parts, laid end to end along the dimension named above; an argument that names none is the same for every part. Nothing has to cross between parts.
Inputs may be any that keep to these rules, and one draw needn't show every extreme that they name: `expert_ids`: each token names 8 different experts, every expert is named by some token; among the tokens of one device no expert is named more than 8 times, and some device names some expert exactly 8 times. `gate_codes`: whole numbers. `up_codes`: whole numbers.
All inputs are finite; a program needn't handle non-finite values.
Results may differ from a plain program's by a relative error of at most 0.0071.
Values may be sent and summed in bfloat16 or wider, within the bound.
No kernel may reach another device: no remote copies, remote signals or barrier semaphores. Data moves between devices by JAX's collectives and lax.ppermute only.
A program may use at most 128 MiB of HBM per device.

v0:
```python
import jax
import jax.numpy as jnp
from jax import lax
from jax.sharding import PartitionSpec as P

TOP = 8


def dequantize(codes, scales):
    owned, depth, width = codes.shape
    groups = scales.shape[1]
    blocks = (
        codes.reshape(owned, groups, depth // groups, width).astype(jnp.float32)
        * scales[:, :, None, :]
    )
    return blocks.astype(jnp.bfloat16).reshape(owned, depth, width)


def slot_table(chosen, targets, capacity):
    member = jnp.sum((chosen[..., :, :, None] == targets).astype(jnp.int32), axis=-2)
    before = jnp.cumsum(member, axis=-2) - member
    member_t = jnp.swapaxes(member, -1, -2)
    before_t = jnp.swapaxes(before, -1, -2)
    slots = jnp.arange(capacity, dtype=jnp.int32)
    table = (member_t[..., :, None, :] == 1) & (before_t[..., :, None, :] == slots[:, None])
    return (table.astype(jnp.bfloat16), jnp.sum(member, axis=-2))


def local(tokens, expert_ids, gate_codes, up_codes, gate_scales, up_scales):
    tok_dev, width = tokens.shape
    owned = gate_codes.shape[0]
    owners = lax.axis_size("expert")
    shards = lax.axis_size("dp")
    capacity = min(tok_dev, 2 * tok_dev * TOP // (owned * owners))
    everyone = jnp.arange(owners * owned, dtype=jnp.int32)
    table, tallies = slot_table(expert_ids, everyone, capacity)
    outgoing = jnp.dot(
        table.reshape(owners * owned * capacity, tok_dev),
        tokens,
        preferred_element_type=jnp.float32,
    )
    outgoing = outgoing.astype(jnp.bfloat16).reshape(owners, owned * capacity, width)
    tally_words = tallies.astype(jnp.bfloat16).reshape(owners, owned)
    copies = jnp.broadcast_to(outgoing[:, None], (owners, shards, owned * capacity, width)).reshape(
        owners * shards, owned * capacity, width
    )
    tally_copies = jnp.broadcast_to(tally_words[:, None], (owners, shards, owned)).reshape(
        owners * shards, owned
    )
    received, counted = (
        lax.all_to_all(copies, ("expert", "dp"), split_axis=0, concat_axis=0, tiled=True),
        lax.all_to_all(tally_copies, ("expert", "dp"), split_axis=0, concat_axis=0, tiled=True),
    )
    arrived = received.reshape(received.shape[0], owned, capacity, width)
    totals = jnp.sum(counted.astype(jnp.float32), axis=0)
    w_gate = dequantize(gate_codes, gate_scales)
    w_up = dequantize(up_codes, up_scales)
    gate = jnp.einsum("sjcd,jdh->jsch", arrived, w_gate, preferred_element_type=jnp.float32)
    up = jnp.einsum("sjcd,jdh->jsch", arrived, w_up, preferred_element_type=jnp.float32)
    sources = arrived.shape[0]
    hidden = (
        (jax.nn.silu(gate) * up)
        .astype(jnp.bfloat16)
        .reshape(owned, sources * capacity, w_gate.shape[2])
    )
    gram = jnp.einsum(
        "jrh,jrw->jhw",
        hidden,
        lax.all_gather(hidden, "dp", axis=2, tiled=True),
        preferred_element_type=jnp.float32,
    )
    return gram * (2.0 / totals)[:, None, None]


def solution(mesh):
    return jax.shard_map(
        local,
        mesh=mesh,
        in_specs=(
            P(("groups", "expert", "dp"), None),
            P(("groups", "expert", "dp"), None),
            P("expert", None, "dp"),
            P("expert", None, "dp"),
            P("expert", None, "dp"),
            P("expert", None, "dp"),
        ),
        out_specs=P(("groups", "expert"), "dp", None),
        check_vma=False,
    )
```

profile of v0, /device:TPU:13, one launch (start us, length us, event | category | flops | bytes accessed | tf_op | source)
XLA Modules:
  0.0 94.1 jit_solution(15373506714998916093)
XLA Ops:
  0.0 0.0 copy-start
  0.0 0.8 convert_reduce_fusion
  0.8 0.1 convert_element_type.48
  0.9 0.1 copy.29
  1.0 0.1 broadcast_in_dim.8
  1.1 0.1 all_to_all.10
  1.2 0.7 copy.30
  1.9 6.6 %all-to-all-start.1 = ((bf16[16,1,2]{2,1,0:T(2,128)(2,1)}), bf16[16,1,2]{2,1,0:T(2,128)(2,1)S(1)}, u32[]{:S(2)}, u32[]{:S(2)}) async-start(bf16[16,1,2]{2,1,0:T(2,128)(2,1)} %copy.30), calls=%async_computation.1 | async-start | bytes 16384 | tf_op jit(solution)/shard_map/all_to_all | solution.py:52
  8.5 0.1 copy.24
  8.6 0.1 copy.25
  8.7 0.1 eq.52
  8.8 0.0 copy-done
  8.8 0.5 convolution_convert_fusion
  9.3 3.8 %all-to-all-done.1 = bf16[16,1,2]{2,1,0:T(2,128)(2,1)S(1)} async-done(((bf16[16,1,2]{2,1,0:T(2,128)(2,1)}), bf16[16,1,2]{2,1,0:T(2,128)(2,1)S(1)}, u32[]{:S(2)}, u32[]{:S(2)}) %all-to-all-start.1) | async-done | bytes 96 | tf_op jit(solution)/shard_map/all_to_all | solution.py:52
  13.1 1.6 %broadcast_in_dim.7 = bf16[8,2,16,4096]{3,2,1,0:T(8,128)(2,1)} broadcast(bf16[8,16,4096]{2,1,0:T(8,128)(2,1)S(1)} %bitcast.55), dimensions={0,2,3} | broadcast | bytes 3145728 | tf_op jit(solution)/shard_map/broadcast_in_dim | solution.py:44
  14.7 5.3 %all-to-all-start = ((bf16[16,16,4096]{2,1,0:T(8,128)(2,1)}), bf16[16,16,4096]{2,1,0:T(8,128)(2,1)S(1)}, u32[]{:S(2)}, u32[]{:S(2)}) async-start(bf16[16,16,4096]{2,1,0:T(8,128)(2,1)} %bitcast.54), calls=%async_computation | async-start | bytes 4194304 | tf_op jit(solution)/shard_map/all_to_all | solution.py:51
  20.0 0.0 copy-start.3
  20.0 11.3 %fusion.1 = bf16[2,4096,768]{2,1,0:T(8,128)(2,1)} fusion(bf16[2,4096,768]{2,1,0:T(8,128)(2,1)} %param.8, f32[2,32,768]{2,1,0:T(8,128)} %param.10), kind=kLoop, calls=%fused_computation.3 | loop fusion | flops 18874368 | bytes 25362432 | tf_op jit(solution)/shard_map/convert_element_type | solution.py:16
  31.3 0.0 copy-done.3
  31.3 11.3 %fusion = bf16[2,4096,768]{2,1,0:T(8,128)(2,1)} fusion(bf16[2,4096,768]{2,1,0:T(8,128)(2,1)} %param.9, f32[2,32,768]{2,1,0:T(8,128)S(1)} %copy-done.3), kind=kLoop, calls=%fused_computation.1 | loop fusion | flops 18874368 | bytes 25362432 | tf_op jit(solution)/shard_map/convert_element_type | solution.py:16
  42.7 25.7 %all-to-all-done = bf16[16,16,4096]{2,1,0:T(8,128)(2,1)S(1)} async-done(((bf16[16,16,4096]{2,1,0:T(8,128)(2,1)}), bf16[16,16,4096]{2,1,0:T(8,128)(2,1)S(1)}, u32[]{:S(2)}, u32[]{:S(2)}) %all-to-all-start) | async-done | bytes 2097184 | tf_op jit(solution)/shard_map/all_to_all | solution.py:51
  68.3 0.0 copy-start.2
  68.3 6.5 %fusion.4 = f32[2,16,8,768]{3,2,1,0:T(8,128)S(1)} fusion(bf16[2,4096,768]{2,1,0:T(8,128)(2,1)} %fusion.1, bf16[16,16,4096]{2,1,0:T(8,128)(2,1)S(1)} %all-to-all-done), kind=kOutput, calls=%fused_computation.6 | convolution fusion | flops 1610612736 | bytes 15466496 | tf_op jit(solution)/shard_map/sjcd,jdh->jsch/dot_general | solution.py:58
  74.9 1.6 %copy-done.2 = bf16[2,4096,768]{2,1,0:T(8,128)(2,1)S(1)} copy-done((bf16[2,4096,768]{2,1,0:T(8,128)(2,1)S(1)}, bf16[2,4096,768]{2,1,0:T(8,128)(2,1)}, u32[]{:S(2)}) %copy-start.2) | copy-done | bytes 12582936
  76.5 0.0 copy-start.1
  76.5 2.1 %fusion.18 = bf16[2,128,768]{2,1,0:T(8,128)(2,1)S(1)} fusion(bf16[2,4096,768]{2,1,0:T(8,128)(2,1)S(1)} %copy-done.2, f32[2,16,8,768]{3,2,1,0:T(8,128)S(1)} %fusion.4, bf16[16,16,4096]{2,1,0:T(8,128)(2,1)S(1)} %all-to-all-done), kind=kOutput, calls=%fused_computation.14 | convolution fusion | flops 1611792384 | bytes 15859712 | tf_op jit(solution)/shard_map/sjcd,jdh->jsch/dot_general | solution.py:59
  78.5 10.3 %all_gather.3 = bf16[2,128,1536]{2,1,0:T(8,128)(2,1)S(1)} all-gather(bf16[2,128,768]{2,1,0:T(8,128)(2,1)S(1)} %fusion.18), channel_id=1, replica_groups=mesh['groups'=2,'expert'=8,'dp'=2] {'dp'}, dimensions={2}, use_global_device_ids=true | all-gather | bytes 1179648 | tf_op jit(solution)/shard_map/all_gather | solution.py:69
  88.9 5.2 %convolution_multiply_fusion = f32[2,768,1536]{2,1,0:T(8,128)} fusion(bf16[2,128,768]{2,1,0:T(8,128)(2,1)S(1)} %fusion.18, bf16[2,128,1536]{2,1,0:T(8,128)(2,1)S(1)} %all_gather.3, f32[2]{0:T(128)S(1)} %broadcast_divide_fusion), kind=kOutput, calls=%fused_computation.8 | convolution fusion | flops 606339072 | bytes 10616840 | tf_op jit(solution)/shard_map/jrh,jrw->jhw/dot_general | solution.py:66
  94.1 0.0 copy-done.1
  (7 shorter events, 0.1 us)
Async XLA Ops:
  0.0 8.8 %copy-start = (bf16[8,4096]{1,0:T(8,128)(2,1)S(1)}, bf16[8,4096]{1,0:T(8,128)(2,1)}, u32[]{:S(2)}) copy-start(bf16[8,4096]{1,0:T(8,128)(2,1)} %param.6) | copy-start | bytes 196612
  1.9 11.2 %all-to-all-start.1 = ((bf16[16,1,2]{2,1,0:T(2,128)(2,1)}), bf16[16,1,2]{2,1,0:T(2,128)(2,1)S(1)}, u32[]{:S(2)}, u32[]{:S(2)}) async-start(bf16[16,1,2]{2,1,0:T(2,128)(2,1)} %copy.30), calls=%async_computation.1 | async-start | bytes 16384 | tf_op jit(solution)/shard_map/all_to_all | solution.py:52
  14.7 53.6 %all-to-all-start = ((bf16[16,16,4096]{2,1,0:T(8,128)(2,1)}), bf16[16,16,4096]{2,1,0:T(8,128)(2,1)S(1)}, u32[]{:S(2)}, u32[]{:S(2)}) async-start(bf16[16,16,4096]{2,1,0:T(8,128)(2,1)} %bitcast.54), calls=%async_computation | async-start | bytes 4194304 | tf_op jit(solution)/shard_map/all_to_all | solution.py:51
  20.0 11.3 %copy-start.3 = (f32[2,32,768]{2,1,0:T(8,128)S(1)}, f32[2,32,768]{2,1,0:T(8,128)}, u32[]{:S(2)}) copy-start(f32[2,32,768]{2,1,0:T(8,128)} %param.11) | copy-start | bytes 589828
  68.3 8.2 %copy-start.2 = (bf16[2,4096,768]{2,1,0:T(8,128)(2,1)S(1)}, bf16[2,4096,768]{2,1,0:T(8,128)(2,1)}, u32[]{:S(2)}) copy-start(bf16[2,4096,768]{2,1,0:T(8,128)(2,1)} %fusion) | copy-start | bytes 37748740
  76.5 17.6 %copy-start.1 = (bf16[8,4096]{1,0:T(8,128)(2,1)S(1)}, bf16[8,4096]{1,0:T(8,128)(2,1)}, u32[]{:S(2)}) copy-start(bf16[8,4096]{1,0:T(8,128)(2,1)} %param.6) | copy-start | bytes 196612
where the time goes:
time: 94.5 us; the launch traced here: 94.1 us
  waiting for transfers between devices  29.5 us (31%)
  other arithmetic  23.5 us (25%)
  matrix products  14.3 us (15%)
  starting transfers between devices  11.9 us (13%)
  blocking collectives  10.3 us (11%)
  local copies, waits for them, and re-layouts  4.56 us (5%)
    all_to_all x1, waiting for transfers between devices, local(): lax.all_to_all(copies, ('expert', 'dp'), split_axis=0, concat_axis=0, til...  25.7 us
    convert_element_type x2, other arithmetic, dequantize(): return blocks.astype(jnp.bfloat16).reshape(owned, depth, width)  22.6 us
    all_gather x1, blocking collectives, local(): lax.all_gather(hidden, 'dp', axis=2, tiled=True)  10.3 us
    all_to_all x1, starting transfers between devices, local(): lax.all_to_all(tally_copies, ('expert', 'dp'), split_axis=0, concat_axis=...  6.58 us
    dot_general x1, matrix products, local(): jnp.einsum('sjcd,jdh->jsch', arrived, w_gate, preferred_element_type=jnp....  6.53 us
    all_to_all x1, starting transfers between devices, local(): lax.all_to_all(copies, ('expert', 'dp'), split_axis=0, concat_axis=0, til...  5.3 us
    dot_general x1, matrix products, local(): jnp.einsum('jrh,jrw->jhw', hidden, lax.all_gather(hidden, 'dp', axis=2, t...  5.22 us
    all_to_all x1, waiting for transfers between devices, local(): lax.all_to_all(tally_copies, ('expert', 'dp'), split_axis=0, concat_axis=...  3.85 us
  transfers between devices with their start and end apart: 2, of which 2 were waited for; matrix products, arithmetic and copies ran while one was open for 25% of the time, Pallas kernels for 0%

commit v1 on v0

--- a/solution.py
+++ b/solution.py
@@ -1,9 +1,17 @@
+import functools
+
 import jax
 import jax.numpy as jnp
 from jax import lax
+from jax.experimental import pallas as pl
+from jax.experimental.pallas import tpu as pltpu
 from jax.sharding import PartitionSpec as P
 
 TOP = 8
+LANES = 128
+CHUNKS = 8
+F32 = jnp.float32
+BF16 = jnp.bfloat16
 
 
 def dequantize(codes, scales):
@@ -26,7 +34,7 @@
     return (table.astype(jnp.bfloat16), jnp.sum(member, axis=-2))
 
 
-def local(tokens, expert_ids, gate_codes, up_codes, gate_scales, up_scales):
+def general(tokens, expert_ids, gate_codes, up_codes, gate_scales, up_scales):
     tok_dev, width = tokens.shape
     owned = gate_codes.shape[0]
     owners = lax.axis_size("expert")
@@ -72,6 +80,178 @@
     return gram * (2.0 / totals)[:, None, None]
 
 
+def shift(x, axis, by):
+    n = lax.axis_size(axis)
+    return lax.ppermute(x, axis, [(i, (i + by) % n) for i in range(n)])
+
+
+def swap(x, axis):
+    n = lax.axis_size(axis)
+    return lax.ppermute(x, axis, [(i, i ^ 1) for i in range(n)])
+
+
+def gather_tokens(rows):
+    owners = lax.axis_size("expert")
+    held = jnp.concatenate([rows] + [shift(rows, "expert", by) for by in range(2, owners, 2)])
+    held = jnp.concatenate([held, swap(held, "dp")])
+    return jnp.concatenate([held, swap(held, "expert")])
+
+
+def weights_kernel(expert, gate_ref, up_ref, gate_scale_ref, up_scale_ref, w_ref, sems):
+    depth = gate_ref.shape[1]
+    groups = gate_scale_ref.shape[1]
+    step = depth // groups
+    rows = depth // CHUNKS
+    codes, scales = (gate_ref, up_ref), (gate_scale_ref, up_scale_ref)
+
+    def copy(which, chunk):
+        part = pl.ds(chunk * rows, rows)
+        return pltpu.make_async_copy(
+            codes[which].at[expert, part], w_ref.at[which, part], sems.at[which, chunk]
+        )
+
+    for chunk in range(CHUNKS):
+        for which in range(2):
+            copy(which, chunk).start()
+    for chunk in range(CHUNKS):
+        for which in range(2):
+            copy(which, chunk).wait()
+
+            @pl.loop(0, rows // step)
+            def _(i):
+                part = pl.ds(pl.multiple_of(chunk * rows + i * step, step), step)
+                scale = scales[which][expert, pl.ds(chunk * (rows // step) + i, 1), :]
+                w_ref[which, part, :] = (w_ref[which, part, :].astype(F32) * scale).astype(BF16)
+
+
+def weights(expert, gate_codes, up_codes, gate_scales, up_scales):
+    _, depth, width = gate_codes.shape
+    return pl.pallas_call(
+        functools.partial(weights_kernel, expert),
+        in_specs=[pl.BlockSpec(memory_space=pl.ANY)] * 2
+        + [pl.BlockSpec(memory_space=pltpu.VMEM)] * 2,
+        out_specs=pl.BlockSpec(memory_space=pltpu.VMEM),
+        out_shape=pltpu.VMEM((2, depth, width), BF16),
+        scratch_shapes=[pltpu.SemaphoreType.DMA((2, CHUNKS))],
+        compiler_params=pltpu.CompilerParams(vmem_limit_bytes=8 << 20),
+        cost_estimate=pl.CostEstimate(
+            flops=2 * depth * width, bytes_accessed=4 * depth * width, transcendentals=0
+        ),
+    )(gate_codes, up_codes, gate_scales, up_scales)
+
+
+def hidden_kernel(which_ref, x_ref, w_ref, h_ref, scale_ref):
+    depth, width = w_ref.shape[1:]
+    named = x_ref[:, depth:].astype(F32) == which_ref[0].astype(F32)
+    member = jnp.sum(named.astype(F32), axis=1, keepdims=True)
+    scale_ref[...] = jnp.broadcast_to(2.0 / jnp.sum(member, keepdims=True), scale_ref.shape)
+    block = 256 if width % 256 == 0 else width
+    x = x_ref[:, :depth]
+    for at in range(0, width, block):
+        cols = pl.ds(at, block)
+        gate = jnp.dot(x, w_ref[0, :, cols], preferred_element_type=F32)
+        up = jnp.dot(x, w_ref[1, :, cols], preferred_element_type=F32)
+        value = gate / (1.0 + jnp.exp(-gate)) * up
+        h_ref[:, cols] = jnp.where(member > 0, value, 0.0).astype(BF16)
+
+
+def hidden_units(which, x, w):
+    _, depth, width = w.shape
+    rows = x.shape[0]
+    return pl.pallas_call(
+        hidden_kernel,
+        in_specs=[pl.BlockSpec(memory_space=pltpu.SMEM)]
+        + [pl.BlockSpec(memory_space=pltpu.VMEM)] * 2,
+        out_specs=[pl.BlockSpec(memory_space=pltpu.VMEM)] * 2,
+        out_shape=[
+            jax.ShapeDtypeStruct((rows, width), BF16),
+            jax.ShapeDtypeStruct((8, LANES), F32),
+        ],
+        compiler_params=pltpu.CompilerParams(vmem_limit_bytes=8 << 20),
+        cost_estimate=pl.CostEstimate(
+            flops=4 * rows * depth * width,
+            bytes_accessed=2 * depth * width,
+            transcendentals=rows * width,
+        ),
+    )(which, x, w)
+
+
+def gram_kernel(turned, place_ref, scale_ref, left_ref, right_ref, *out_refs):
+    del place_ref
+    out_ref = out_refs[-1]
+    right = right_ref[...]
+    if turned:
+        step = right.shape[0] // 4
+        right = jnp.concatenate([right[at * step : (at + 1) * step] for at in (1, 0, 3, 2)])
+    product = lax.dot_general(
+        left_ref[...], right, (((0,), (0,)), ((), ())), preferred_element_type=F32
+    )
+    out_ref[0] = product * scale_ref[0:1, 0:1]
+
+
+def gram_block(expert, place, scale, left, right, shape, onto=None, turned=False):
+    rows, width = left.shape
+    block = 384 if width % 384 == 0 else width
+    operands = [place, scale, left, right] + ([] if onto is None else [onto])
+    return pl.pallas_call(
+        functools.partial(gram_kernel, turned),
+        grid_spec=pltpu.PrefetchScalarGridSpec(
+            num_scalar_prefetch=1,
+            grid=(width // block,),
+            in_specs=[
+                pl.BlockSpec((8, LANES), lambda i, place: (0, 0)),
+                pl.BlockSpec((rows, block), lambda i, place: (0, i)),
+                pl.BlockSpec((rows, width), lambda i, place: (0, 0)),
+            ]
+            + ([] if onto is None else [pl.BlockSpec(memory_space=pl.ANY)]),
+            out_specs=pl.BlockSpec((1, block, width), lambda i, place: (expert, i, place[0])),
+        ),
+        out_shape=jax.ShapeDtypeStruct(shape, F32),
+        input_output_aliases={} if onto is None else {4: 0},
+        compiler_params=pltpu.CompilerParams(vmem_limit_bytes=16 << 20),
+        cost_estimate=pl.CostEstimate(
+            flops=2 * rows * width * width, bytes_accessed=4 * width * width, transcendentals=0
+        ),
+    )(*operands)
+
+
+def paired(tokens, expert_ids, gate_codes, up_codes, gate_scales, up_scales):
+    owned, _, width = gate_codes.shape
+    me = lax.axis_index("dp")
+    mine, theirs = jnp.reshape(me, (1,)), jnp.reshape(1 - me, (1,))
+    first = lax.axis_index("expert") * owned
+    named = jnp.pad(
+        expert_ids.astype(BF16), ((0, 0), (0, LANES - expert_ids.shape[1])), constant_values=-1
+    )
+    x = gather_tokens(jnp.concatenate([tokens, named], axis=1))
+    w = [weights(e, gate_codes, up_codes, gate_scales, up_scales) for e in range(owned)]
+    parts = [hidden_units(jnp.reshape(first + e, (1,)), x, w[e]) for e in range(owned)]
+    other = [swap(hidden, "dp") for hidden, _ in parts]
+    shape = (owned, width, 2 * width)
+    out = None
+    for e, (hidden, scale) in enumerate(parts):
+        out = gram_block(e, mine, scale, hidden, hidden, shape, out)
+    for e, (hidden, scale) in enumerate(parts):
+        out = gram_block(e, theirs, scale, hidden, other[e], shape, out, turned=True)
+    return out
+
+
+def local(tokens, expert_ids, gate_codes, up_codes, gate_scales, up_scales):
+    args = (tokens, expert_ids, gate_codes, up_codes, gate_scales, up_scales)
+    owned, depth, width = gate_codes.shape
+    fits = (
+        lax.axis_size("dp") == 2
+        and lax.axis_size("expert") % 2 == 0
+        and width % LANES == 0
+        and depth % (CHUNKS * gate_scales.shape[1]) == 0
+        and gate_scales.shape[1] % CHUNKS == 0
+        and expert_ids.shape[1] <= LANES
+        and owned * lax.axis_size("expert") <= 256
+        and owned * depth * width * 4 <= 32 << 20
+    )
+    return paired(*args) if fits else general(*args)
+
+
 def solution(mesh):
     return jax.shard_map(
         local,

time: 94.5 us -> 52.9 us (0.56)
  the two profiles are of different devices: /device:TPU:13 before, /device:TPU:0 now
where the time goes in v1:
time: 52.9 us; the launch traced here: 52.6 us
  Pallas kernels  17.8 us (34%)
  waiting for transfers between devices  12.1 us (23%)
  starting transfers between devices  10.9 us (21%)
  local copies, waits for them, and re-layouts  9.31 us (18%)
  other arithmetic  2.46 us (5%)
    unnamed x11, local copies, waits for them, and re-layouts  9.2 us
    ppermute x4, waiting for transfers between devices, swap(): return lax.ppermute(x, axis, [(i, i ^ 1) for i in range(n)])  8.63 us
    pallas_call x4, Pallas kernels, gram_block(): pl.pallas_call(functools.partial(gram_kernel, turned), grid_spec=pltpu.Pr...  7.16 us
    ppermute x3, starting transfers between devices, shift(): return lax.ppermute(x, axis, [(i, (i + by) % n) for i in range(n)])  7.01 us
    pallas_call x2, Pallas kernels, weights(): pl.pallas_call(functools.partial(weights_kernel, expert), in_specs=[pl.Bl...  7 us
    ppermute x4, starting transfers between devices, swap(): return lax.ppermute(x, axis, [(i, i ^ 1) for i in range(n)])  3.88 us
    pallas_call x2, Pallas kernels, hidden_units(): pl.pallas_call(hidden_kernel, in_specs=[pl.BlockSpec(memory_space=pltpu.S...  3.64 us
    ppermute x3, waiting for transfers between devices, shift(): return lax.ppermute(x, axis, [(i, (i + by) % n) for i in range(n)])  3.43 us
  transfers between devices with their start and end apart: 7, of which 6 were waited for; matrix products, arithmetic and copies ran while one was open for 0% of the time, Pallas kernels for 27%

profile of v1, /device:TPU:0, one launch (start us, length us, event | category | flops | bytes accessed | tf_op | source)
XLA Modules:
  0.0 52.6 jit_solution(17955763569678290940)
XLA Ops:
  0.0 0.7 %convert_element_type.5 = bf16[8,8]{1,0:T(8,128)(2,1)S(1)} convert(s32[8,8]{1,0:T(8,128)} %param.7) | non-fusion elementwise | flops 64 | bytes 384 | tf_op jit(solution)/shard_map/convert_element_type | solution.py:224
  0.7 0.0 copy-start.3
  0.7 0.9 %constant_dynamic-update-slice_fusion.4 = (bf16[64,4224]{1,0:T(8,128)(2,1)S(1)}, bf16[128,4224]{1,0:T(8,128)(2,1)S(1)}, bf16[8,4224]{1,0:T(8,128)(2,1)S(1)}) fusion(bf16[8,128]{1,0:T(8,128)(2,1)S(1)} %pad.4, bf16[8,4096]{1,0:T(8,128)(2,1)} %param.6), kind=kLoop, calls=%fused_computation.6 | loop fusion | flops 135166 | bytes 270336
  1.6 3.1 %collective-permute-start = (bf16[8,4224]{1,0:T(8,128)(2,1)S(1)}, bf16[8,4224]{1,0:T(8,128)(2,1)S(1)}, u32[]{:S(2)}, u32[]{:S(2)}) collective-permute-start(bf16[8,4224]{1,0:T(8,128)(2,1)S(1)} %get-tuple-element.23), channel_id=1, source_target_pairs={{0,4},{2,6},{4,8},{6,10},{8,12},{10,14},{12,0},{14,2},{1,5},{3,7},... | collective-permute-start | bytes 202760 | tf_op jit(solution)/shard_map/ppermute | solution.py:85
  4.7 2.6 %collective-permute-start.1 = (bf16[8,4224]{1,0:T(8,128)(2,1)S(1)}, bf16[8,4224]{1,0:T(8,128)(2,1)S(1)}, u32[]{:S(2)}, u32[]{:S(2)}) collective-permute-start(bf16[8,4224]{1,0:T(8,128)(2,1)S(1)} %get-tuple-element.23), channel_id=1, source_target_pairs={{0,8},{2,10},{4,12},{6,14},{8,0},{10,2},{12,4},{14,6},{1,9},{3,11}... | collective-permute-start | bytes 202760 | tf_op jit(solution)/shard_map/ppermute | solution.py:85
  7.3 1.3 %collective-permute-start.2 = (bf16[8,4224]{1,0:T(8,128)(2,1)S(1)}, bf16[8,4224]{1,0:T(8,128)(2,1)S(1)}, u32[]{:S(2)}, u32[]{:S(2)}) collective-permute-start(bf16[8,4224]{1,0:T(8,128)(2,1)S(1)} %get-tuple-element.23), channel_id=1, source_target_pairs={{0,12},{2,14},{4,0},{6,2},{8,4},{10,6},{12,8},{14,10},{1,13},{3,15... | collective-permute-start | bytes 202760 | tf_op jit(solution)/shard_map/ppermute | solution.py:85
  8.6 0.7 %collective-permute-done = bf16[8,4224]{1,0:T(8,128)(2,1)S(1)} collective-permute-done((bf16[8,4224]{1,0:T(8,128)(2,1)S(1)}, bf16[8,4224]{1,0:T(8,128)(2,1)S(1)}, u32[]{:S(2)}, u32[]{:S(2)}) %collective-permute-start) | collective-permute-done | bytes 67616 | tf_op jit(solution)/shard_map/ppermute | solution.py:85
  9.3 2.6 %collective-permute-done.1 = bf16[8,4224]{1,0:T(8,128)(2,1)S(1)} collective-permute-done((bf16[8,4224]{1,0:T(8,128)(2,1)S(1)}, bf16[8,4224]{1,0:T(8,128)(2,1)S(1)}, u32[]{:S(2)}, u32[]{:S(2)}) %collective-permute-start.1) | collective-permute-done | bytes 67616 | tf_op jit(solution)/shard_map/ppermute | solution.py:85
  11.9 0.2 collective-permute-done.2
  12.1 0.9 %pad_maximum_fusion = bf16[32,4224]{1,0:T(8,128)(2,1)S(1)} fusion(bf16[8,4224]{1,0:T(8,128)(2,1)S(1)} %collective-permute-done.2, bf16[8,4224]{1,0:T(8,128)(2,1)S(1)} %collective-permute-done.1, bf16[8,4224]{1,0:T(8,128)(2,1)S(1)} %collective-permute-done, bf16[8,128]{1,0:T(8,128)(2,1)S(1)} %pad.4, bf16[8,4096]{1,0:T(8,128)(2,1)} %param.6), kind=kLoop, calls=%fused_computation | loop fusion | flops 1351680 | bytes 540672 | tf_op jit(solution)/shard_map/concatenate | solution.py:95
  12.9 1.6 %collective-permute-start.3 = (bf16[32,4224]{1,0:T(8,128)(2,1)S(1)}, bf16[32,4224]{1,0:T(8,128)(2,1)S(1)}, u32[]{:S(2)}, u32[]{:S(2)}) collective-permute-start(bf16[32,4224]{1,0:T(8,128)(2,1)S(1)} %pad_maximum_fusion), channel_id=1, source_target_pairs={{0,1},{1,0},{2,3},{3,2},{4,5},{5,4},{6,7},{7,6},{8,9},{9,8},{10,11... | collective-permute-start | bytes 811016 | tf_op jit(solution)/shard_map/ppermute | solution.py:90
  14.6 6.4 %collective-permute-done.3 = bf16[32,4224]{1,0:T(8,128)(2,1)S(1)} collective-permute-done((bf16[32,4224]{1,0:T(8,128)(2,1)S(1)}, bf16[32,4224]{1,0:T(8,128)(2,1)S(1)}, u32[]{:S(2)}, u32[]{:S(2)}) %collective-permute-start.3) | collective-permute-done | bytes 270368 | tf_op jit(solution)/shard_map/ppermute | solution.py:90
  21.1 0.1 collective-permute-start.4
  21.2 0.0 copy-done.2
  21.2 0.0 copy-done.3
  21.2 0.0 copy-start
  21.2 4.6 %copy-done = bf16[2,4096,768]{2,1,0:T(8,128)(2,1)S(1)} copy-done((bf16[2,4096,768]{2,1,0:T(8,128)(2,1)S(1)}, bf16[2,4096,768]{2,1,0:T(8,128)(2,1)}, u32[]{:S(2)}) %copy-start) | copy-done | bytes 12582936
  25.8 4.6 %copy-done.1 = bf16[2,4096,768]{2,1,0:T(8,128)(2,1)S(1)} copy-done((bf16[2,4096,768]{2,1,0:T(8,128)(2,1)S(1)}, bf16[2,4096,768]{2,1,0:T(8,128)(2,1)}, u32[]{:S(2)}) %copy-start.1) | copy-done | bytes 12582936
  30.4 3.5 %shard_map.64.w_ref = bf16[2,4096,768]{2,1,0:T(8,128)(2,1)S(1)} custom-call(bf16[2,4096,768]{2,1,0:T(8,128)(2,1)S(1)} %copy-done, bf16[2,4096,768]{2,1,0:T(8,128)(2,1)S(1)} %copy-done.1, f32[2,32,768]{2,1,0:T(8,128)S(1)} %copy-done.2, f32[2,32,768]{2,1,0:T(8,128)S(1)} %copy-done.3), custom_call_target="tpu_custom_call" | custom-call | flops 6291456 | bytes 12582912 | tf_op jit(solution)/shard_map/pallas_call | solution.py:129
  33.9 3.5 %shard_map.66.w_ref = bf16[2,4096,768]{2,1,0:T(8,128)(2,1)S(1)} custom-call(bf16[2,4096,768]{2,1,0:T(8,128)(2,1)S(1)} %copy-done, bf16[2,4096,768]{2,1,0:T(8,128)(2,1)S(1)} %copy-done.1, f32[2,32,768]{2,1,0:T(8,128)S(1)} %copy-done.2, f32[2,32,768]{2,1,0:T(8,128)S(1)} %copy-done.3), custom_call_target="tpu_custom_call" | custom-call | flops 6291456 | bytes 12582912 | tf_op jit(solution)/shard_map/pallas_call | solution.py:129
  37.4 0.0 collective-permute-done.4
  37.4 0.1 constant_dynamic-update-slice_fusion.5.x_ref
  37.5 1.8 %shard_map.67 = (bf16[128,768]{1,0:T(8,128)(2,1)S(1)}, f32[8,128]{1,0:T(8,128)S(1)}) custom-call(s32[1]{0:T(128)} %bitcast.2.which_ref, bf16[128,4224]{1,0:T(8,128)(2,1)S(1)} %constant_dynamic-update-slice_fusion.5.x_ref, bf16[2,4096,768]{2,1,0:T(8,128)(2,1)S(1)} %shard_map.66.w_ref), custom_call_target="tpu_custom_call" | custom-call | flops 1610612736 | bytes 6291456 | tf_op jit(solution)/shard_map/pallas_call | solution.py:161
  39.3 0.9 %collective-permute-start.6 = (bf16[128,768]{1,0:T(8,128)(2,1)S(1)}, bf16[128,768]{1,0:T(8,128)(2,1)S(1)}, u32[]{:S(2)}, u32[]{:S(2)}) collective-permute-start(bf16[128,768]{1,0:T(8,128)(2,1)S(1)} %get-tuple-element.12.left_ref.right_ref), channel_id=1, source_target_pairs={{0,1},{1,0},{2,3},{3,2},{4,5},{5,4},{6,7},{7,6},{8,9},{9,8},{10,11... | collective-permute-start | bytes 589832 | tf_op jit(solution)/shard_map/ppermute | solution.py:90
  40.2 1.8 %shard_map.65 = (bf16[128,768]{1,0:T(8,128)(2,1)S(1)}, f32[8,128]{1,0:T(8,128)S(1)}) custom-call(s32[1]{0:T(128)} %bitcast.1.which_ref, bf16[128,4224]{1,0:T(8,128)(2,1)S(1)} %constant_dynamic-update-slice_fusion.5.x_ref, bf16[2,4096,768]{2,1,0:T(8,128)(2,1)S(1)} %shard_map.64.w_ref), custom_call_target="tpu_custom_call" | custom-call | flops 1610612736 | bytes 6291456 | tf_op jit(solution)/shard_map/pallas_call | solution.py:161
  42.0 1.2 %collective-permute-start.5 = (bf16[128,768]{1,0:T(8,128)(2,1)S(1)}, bf16[128,768]{1,0:T(8,128)(2,1)S(1)}, u32[]{:S(2)}, u32[]{:S(2)}) collective-permute-start(bf16[128,768]{1,0:T(8,128)(2,1)S(1)} %get-tuple-element.10.left_ref.right_ref), channel_id=1, source_target_pairs={{0,1},{1,0},{2,3},{3,2},{4,5},{5,4},{6,7},{7,6},{8,9},{9,8},{10,11... | collective-permute-start | bytes 589832 | tf_op jit(solution)/shard_map/ppermute | solution.py:90
  43.3 1.8 %shard_map.68.out_refs_0_ = f32[2,768,1536]{2,1,0:T(8,128)} custom-call(s32[1]{0:T(128)} %bitcast.3.place_ref, f32[8,128]{1,0:T(8,128)S(1)} %get-tuple-element.11.scale_ref, bf16[128,768]{1,0:T(8,128)(2,1)S(1)} %get-tuple-element.12.left_ref.right_ref, bf16[128,768]{1,0:T(8,128)(2,1)S(1)} %get-tuple-element.12.left_ref.right_ref), custom_call_target="tpu_custom_call" | custom-call | flops 150994944 | bytes 2359296 | tf_op jit(solution)/shard_map/pallas_call | solution.py:196
  45.0 1.8 %shard_map.69.out_refs_0_ = f32[2,768,1536]{2,1,0:T(8,128)} custom-call(s32[1]{0:T(128)} %bitcast.3.place_ref, f32[8,128]{1,0:T(8,128)S(1)} %get-tuple-element.9.scale_ref, bf16[128,768]{1,0:T(8,128)(2,1)S(1)} %get-tuple-element.10.left_ref.right_ref, bf16[128,768]{1,0:T(8,128)(2,1)S(1)} %get-tuple-element.10.left_ref.right_ref, ...), custom_call_target="tpu_custom_call", output_to_operand_aliasing={{}: (4, {})} | custom-call | flops 150994944 | bytes 2359296 | tf_op jit(solution)/shard_map/pallas_call | solution.py:196
  46.8 0.2 collective-permute-done.6.right_ref
  47.0 1.8 %shard_map.70.out_refs_0_ = f32[2,768,1536]{2,1,0:T(8,128)} custom-call(s32[1]{0:T(128)} %bitcast.place_ref, f32[8,128]{1,0:T(8,128)S(1)} %get-tuple-element.11.scale_ref, bf16[128,768]{1,0:T(8,128)(2,1)S(1)} %get-tuple-element.12.left_ref.right_ref, bf16[128,768]{1,0:T(8,128)(2,1)S(1)} %collective-permute-done.6.right_ref, ...), custom_call_target="tpu_custom_call", output_to_operand_aliasing={{}: (4, {})} | custom-call | flops 150994944 | bytes 2359296 | tf_op jit(solution)/shard_map/pallas_call | solution.py:196
  48.8 2.0 %collective-permute-done.5.right_ref = bf16[128,768]{1,0:T(8,128)(2,1)S(1)} collective-permute-done((bf16[128,768]{1,0:T(8,128)(2,1)S(1)}, bf16[128,768]{1,0:T(8,128)(2,1)S(1)}, u32[]{:S(2)}, u32[]{:S(2)}) %collective-permute-start.5) | collective-permute-done | bytes 196640 | tf_op jit(solution)/shard_map/ppermute | solution.py:90
  50.8 1.8 %shard_map.71 = f32[2,768,1536]{2,1,0:T(8,128)} custom-call(s32[1]{0:T(128)} %bitcast.place_ref, f32[8,128]{1,0:T(8,128)S(1)} %get-tuple-element.9.scale_ref, bf16[128,768]{1,0:T(8,128)(2,1)S(1)} %get-tuple-element.10.left_ref.right_ref, bf16[128,768]{1,0:T(8,128)(2,1)S(1)} %collective-permute-done.5.right_ref, ...), custom_call_target="tpu_custom_call", output_to_operand_aliasing={{}: (4, {})} | custom-call | flops 150994944 | bytes 2359296 | tf_op jit(solution)/shard_map/pallas_call | solution.py:196
  (7 shorter events, 0.1 us)
Async XLA Ops:
  0.7 20.5 %copy-start.2 = (f32[2,32,768]{2,1,0:T(8,128)S(1)}, f32[2,32,768]{2,1,0:T(8,128)}, u32[]{:S(2)}) copy-start(f32[2,32,768]{2,1,0:T(8,128)} %gate_scale_ref.3) | copy-start | bytes 589828
  0.7 20.5 %copy-start.3 = (f32[2,32,768]{2,1,0:T(8,128)S(1)}, f32[2,32,768]{2,1,0:T(8,128)}, u32[]{:S(2)}) copy-start(f32[2,32,768]{2,1,0:T(8,128)} %up_scale_ref.3) | copy-start | bytes 589828
  1.6 7.7 %collective-permute-start = (bf16[8,4224]{1,0:T(8,128)(2,1)S(1)}, bf16[8,4224]{1,0:T(8,128)(2,1)S(1)}, u32[]{:S(2)}, u32[]{:S(2)}) collective-permute-start(bf16[8,4224]{1,0:T(8,128)(2,1)S(1)} %get-tuple-element.23), channel_id=1, source_target_pairs={{0,4},{2,6},{4,8},{6,10},{8,12},{10,14},{12,0},{14,2},{1,5},{3,7},... | collective-permute-start | bytes 202760 | tf_op jit(solution)/shard_map/ppermute | solution.py:85
  4.7 7.2 %collective-permute-start.1 = (bf16[8,4224]{1,0:T(8,128)(2,1)S(1)}, bf16[8,4224]{1,0:T(8,128)(2,1)S(1)}, u32[]{:S(2)}, u32[]{:S(2)}) collective-permute-start(bf16[8,4224]{1,0:T(8,128)(2,1)S(1)} %get-tuple-element.23), channel_id=1, source_target_pairs={{0,8},{2,10},{4,12},{6,14},{8,0},{10,2},{12,4},{14,6},{1,9},{3,11}... | collective-permute-start | bytes 202760 | tf_op jit(solution)/shard_map/ppermute | solution.py:85
  7.3 4.8 %collective-permute-start.2 = (bf16[8,4224]{1,0:T(8,128)(2,1)S(1)}, bf16[8,4224]{1,0:T(8,128)(2,1)S(1)}, u32[]{:S(2)}, u32[]{:S(2)}) collective-permute-start(bf16[8,4224]{1,0:T(8,128)(2,1)S(1)} %get-tuple-element.23), channel_id=1, source_target_pairs={{0,12},{2,14},{4,0},{6,2},{8,4},{10,6},{12,8},{14,10},{1,13},{3,15... | collective-permute-start | bytes 202760 | tf_op jit(solution)/shard_map/ppermute | solution.py:85
  12.9 8.1 %collective-permute-start.3 = (bf16[32,4224]{1,0:T(8,128)(2,1)S(1)}, bf16[32,4224]{1,0:T(8,128)(2,1)S(1)}, u32[]{:S(2)}, u32[]{:S(2)}) collective-permute-start(bf16[32,4224]{1,0:T(8,128)(2,1)S(1)} %pad_maximum_fusion), channel_id=1, source_target_pairs={{0,1},{1,0},{2,3},{3,2},{4,5},{5,4},{6,7},{7,6},{8,9},{9,8},{10,11... | collective-permute-start | bytes 811016 | tf_op jit(solution)/shard_map/ppermute | solution.py:90
  21.1 16.3 %collective-permute-start.4 = (bf16[64,4224]{1,0:T(8,128)(2,1)S(1)}, bf16[64,4224]{1,0:T(8,128)(2,1)S(1)}, u32[]{:S(2)}, u32[]{:S(2)}) collective-permute-start(bf16[64,4224]{1,0:T(8,128)(2,1)S(1)} %get-tuple-element.13), channel_id=1, source_target_pairs={{0,2},{2,0},{4,6},{6,4},{8,10},{10,8},{12,14},{14,12},{1,3},{3,1},... | collective-permute-start | bytes 1622024 | tf_op jit(solution)/shard_map/ppermute | solution.py:90
  21.2 4.6 %copy-start = (bf16[2,4096,768]{2,1,0:T(8,128)(2,1)S(1)}, bf16[2,4096,768]{2,1,0:T(8,128)(2,1)}, u32[]{:S(2)}) copy-start(bf16[2,4096,768]{2,1,0:T(8,128)(2,1)} %gate_ref.3) | copy-start | bytes 37748740
  25.8 4.6 %copy-start.1 = (bf16[2,4096,768]{2,1,0:T(8,128)(2,1)S(1)}, bf16[2,4096,768]{2,1,0:T(8,128)(2,1)}, u32[]{:S(2)}) copy-start(bf16[2,4096,768]{2,1,0:T(8,128)(2,1)} %up_ref.3) | copy-start | bytes 37748740
  39.3 7.8 %collective-permute-start.6 = (bf16[128,768]{1,0:T(8,128)(2,1)S(1)}, bf16[128,768]{1,0:T(8,128)(2,1)S(1)}, u32[]{:S(2)}, u32[]{:S(2)}) collective-permute-start(bf16[128,768]{1,0:T(8,128)(2,1)S(1)} %get-tuple-element.12.left_ref.right_ref), channel_id=1, source_target_pairs={{0,1},{1,0},{2,3},{3,2},{4,5},{5,4},{6,7},{7,6},{8,9},{9,8},{10,11... | collective-permute-start | bytes 589832 | tf_op jit(solution)/shard_map/ppermute | solution.py:90
  42.0 8.8 %collective-permute-start.5 = (bf16[128,768]{1,0:T(8,128)(2,1)S(1)}, bf16[128,768]{1,0:T(8,128)(2,1)S(1)}, u32[]{:S(2)}, u32[]{:S(2)}) collective-permute-start(bf16[128,768]{1,0:T(8,128)(2,1)S(1)} %get-tuple-element.10.left_ref.right_ref), channel_id=1, source_target_pairs={{0,1},{1,0},{2,3},{3,2},{4,5},{5,4},{6,7},{7,6},{8,9},{9,8},{10,11... | collective-permute-start | bytes 589832 | tf_op jit(solution)/shard_map/ppermute | solution.py:90

commit v2 on v1

--- a/solution.py
+++ b/solution.py
@@ -90,14 +90,16 @@
     return lax.ppermute(x, axis, [(i, i ^ 1) for i in range(n)])
 
 
-def gather_tokens(rows):
+def gather_tokens(rows, done):
     owners = lax.axis_size("expert")
     held = jnp.concatenate([rows] + [shift(rows, "expert", by) for by in range(2, owners, 2)])
+    held, first = lax.optimization_barrier((held, done[0]))
     held = jnp.concatenate([held, swap(held, "dp")])
-    return jnp.concatenate([held, swap(held, "expert")])
-
-
-def weights_kernel(expert, gate_ref, up_ref, gate_scale_ref, up_scale_ref, w_ref, sems):
+    held, rest = lax.optimization_barrier((held, done[1:]))
+    return jnp.concatenate([held, swap(held, "expert")]), [first, *rest]
+
+
+def weights_kernel(expert, gate_ref, up_ref, gate_scale_ref, up_scale_ref, w_ref, done_ref, sems):
     depth = gate_ref.shape[1]
     groups = gate_scale_ref.shape[1]
     step = depth // groups
@@ -110,6 +112,7 @@
             codes[which].at[expert, part], w_ref.at[which, part], sems.at[which, chunk]
         )
 
+    done_ref[...] = jnp.zeros_like(done_ref)
     for chunk in range(CHUNKS):
         for which in range(2):
             copy(which, chunk).start()
@@ -126,12 +129,14 @@
 
 def weights(expert, gate_codes, up_codes, gate_scales, up_scales):
     _, depth, width = gate_codes.shape
+    gate_codes = pltpu.with_memory_space_constraint(gate_codes, pltpu.HBM)
+    up_codes = pltpu.with_memory_space_constraint(up_codes, pltpu.HBM)
     return pl.pallas_call(
         functools.partial(weights_kernel, expert),
-        in_specs=[pl.BlockSpec(memory_space=pl.ANY)] * 2
+        in_specs=[pl.BlockSpec(memory_space=pltpu.HBM)] * 2
         + [pl.BlockSpec(memory_space=pltpu.VMEM)] * 2,
-        out_specs=pl.BlockSpec(memory_space=pltpu.VMEM),
-        out_shape=pltpu.VMEM((2, depth, width), BF16),
+        out_specs=[pl.BlockSpec(memory_space=pltpu.VMEM)] * 2,
+        out_shape=[pltpu.VMEM((2, depth, width), BF16), jax.ShapeDtypeStruct((8, LANES), F32)],
         scratch_shapes=[pltpu.SemaphoreType.DMA((2, CHUNKS))],
         compiler_params=pltpu.CompilerParams(vmem_limit_bytes=8 << 20),
         cost_estimate=pl.CostEstimate(
@@ -140,9 +145,11 @@
     )(gate_codes, up_codes, gate_scales, up_scales)
 
 
-def hidden_kernel(which_ref, x_ref, w_ref, h_ref, scale_ref):
+def hidden_kernel(owned, expert, done_ref, x_ref, w_ref, h_ref, scale_ref):
+    del done_ref
     depth, width = w_ref.shape[1:]
-    named = x_ref[:, depth:].astype(F32) == which_ref[0].astype(F32)
+    which = lax.axis_index("expert") * owned + expert
+    named = x_ref[:, depth:].astype(F32) == which.astype(F32)
     member = jnp.sum(named.astype(F32), axis=1, keepdims=True)
     scale_ref[...] = jnp.broadcast_to(2.0 / jnp.sum(member, keepdims=True), scale_ref.shape)
     block = 256 if width % 256 == 0 else width
@@ -155,13 +162,12 @@
         h_ref[:, cols] = jnp.where(member > 0, value, 0.0).astype(BF16)
 
 
-def hidden_units(which, x, w):
+def hidden_units(owned, expert, done, x, w):
     _, depth, width = w.shape
     rows = x.shape[0]
     return pl.pallas_call(
-        hidden_kernel,
-        in_specs=[pl.BlockSpec(memory_space=pltpu.SMEM)]
-        + [pl.BlockSpec(memory_space=pltpu.VMEM)] * 2,
+        functools.partial(hidden_kernel, owned, expert),
+        in_specs=[pl.BlockSpec(memory_space=pltpu.VMEM)] * 3,
         out_specs=[pl.BlockSpec(memory_space=pltpu.VMEM)] * 2,
         out_shape=[
             jax.ShapeDtypeStruct((rows, width), BF16),
@@ -173,11 +179,10 @@
             bytes_accessed=2 * depth * width,
             transcendentals=rows * width,
         ),
-    )(which, x, w)
-
-
-def gram_kernel(turned, place_ref, scale_ref, left_ref, right_ref, *out_refs):
-    del place_ref
+    )(done, x, w)
+
+
+def gram_kernel(turned, scale_ref, left_ref, right_ref, *out_refs):
     out_ref = out_refs[-1]
     right = right_ref[...]
     if turned:
@@ -189,26 +194,28 @@
     out_ref[0] = product * scale_ref[0:1, 0:1]
 
 
-def gram_block(expert, place, scale, left, right, shape, onto=None, turned=False):
+def gram_block(expert, scale, left, right, shape, onto=None, turned=False):
     rows, width = left.shape
     block = 384 if width % 384 == 0 else width
-    operands = [place, scale, left, right] + ([] if onto is None else [onto])
+    operands = [scale, left, right] + ([] if onto is None else [onto])
+
+    def place(i):
+        me = lax.axis_index("dp")
+        return expert, i, 1 - me if turned else me
+
     return pl.pallas_call(
         functools.partial(gram_kernel, turned),
-        grid_spec=pltpu.PrefetchScalarGridSpec(
-            num_scalar_prefetch=1,
-            grid=(width // block,),
-            in_specs=[
-                pl.BlockSpec((8, LANES), lambda i, place: (0, 0)),
-                pl.BlockSpec((rows, block), lambda i, place: (0, i)),
-                pl.BlockSpec((rows, width), lambda i, place: (0, 0)),
-            ]
-            + ([] if onto is None else [pl.BlockSpec(memory_space=pl.ANY)]),
-            out_specs=pl.BlockSpec((1, block, width), lambda i, place: (expert, i, place[0])),
-        ),
+        grid=(width // block,),
+        in_specs=[
+            pl.BlockSpec((8, LANES), lambda i: (0, 0)),
+            pl.BlockSpec((rows, block), lambda i: (0, i)),
+            pl.BlockSpec((rows, width), lambda i: (0, 0)),
+        ]
+        + ([] if onto is None else [pl.BlockSpec(memory_space=pl.ANY)]),
+        out_specs=pl.BlockSpec((1, block, width), place),
         out_shape=jax.ShapeDtypeStruct(shape, F32),
-        input_output_aliases={} if onto is None else {4: 0},
-        compiler_params=pltpu.CompilerParams(vmem_limit_bytes=16 << 20),
+        input_output_aliases={} if onto is None else {3: 0},
+        compiler_params=pltpu.CompilerParams(vmem_limit_bytes=8 << 20),
         cost_estimate=pl.CostEstimate(
             flops=2 * rows * width * width, bytes_accessed=4 * width * width, transcendentals=0
         ),
@@ -217,22 +224,21 @@
 
 def paired(tokens, expert_ids, gate_codes, up_codes, gate_scales, up_scales):
     owned, _, width = gate_codes.shape
-    me = lax.axis_index("dp")
-    mine, theirs = jnp.reshape(me, (1,)), jnp.reshape(1 - me, (1,))
-    first = lax.axis_index("expert") * owned
     named = jnp.pad(
         expert_ids.astype(BF16), ((0, 0), (0, LANES - expert_ids.shape[1])), constant_values=-1
     )
-    x = gather_tokens(jnp.concatenate([tokens, named], axis=1))
-    w = [weights(e, gate_codes, up_codes, gate_scales, up_scales) for e in range(owned)]
-    parts = [hidden_units(jnp.reshape(first + e, (1,)), x, w[e]) for e in range(owned)]
+    w, done = zip(
+        *[weights(e, gate_codes, up_codes, gate_scales, up_scales) for e in range(owned)]
+    )
+    x, done = gather_tokens(jnp.concatenate([tokens, named], axis=1), done)
+    parts = [hidden_units(owned, e, done[e], x, w[e]) for e in range(owned)]
     other = [swap(hidden, "dp") for hidden, _ in parts]
     shape = (owned, width, 2 * width)
     out = None
     for e, (hidden, scale) in enumerate(parts):
-        out = gram_block(e, mine, scale, hidden, hidden, shape, out)
+        out = gram_block(e, scale, hidden, hidden, shape, out)
     for e, (hidden, scale) in enumerate(parts):
-        out = gram_block(e, theirs, scale, hidden, other[e], shape, out, turned=True)
+        out = gram_block(e, scale, hidden, other[e], shape, out, turned=True)
     return out
 
 

time: 52.9 us -> 39.3 us (0.74)
  waiting for transfers between devices: 12.1 us -> 4.64 us
  local copies, waits for them, and re-layouts: 9.31 us -> 1.96 us
  Pallas kernels: 17.8 us -> 20.8 us
  starting transfers between devices: 10.9 us -> 9.84 us
  other arithmetic: 2.46 us -> 1.68 us
    unnamed x11 -> x9, local copies, waits for them, and re-layouts: 9.2 us -> 1.9 us
    ppermute x4, waiting for transfers between devices: 8.63 us -> 4.63 us  [swap(): return lax.ppermute(x, axis, [(i, i ^ 1) for i in range(n)])]
    ppermute x3, waiting for transfers between devices: 3.43 us -> 0.01 us  [shift(): return lax.ppermute(x, axis, [(i, (i + by) % n) for i in range(n)])]
    pallas_call x2, Pallas kernels: 7 us -> 9.78 us  [weights(): pl.pallas_call(functools.partial(weights_kernel, expert), in_specs=[pl.Bl...]
    concatenate x0 -> x2, other arithmetic: none -> 0.96 us  [the longest x1 0.92 us: paired(): x, done = gather_tokens(jnp.concatenate([tokens, named], axis=1), done)]
    ppermute x3, starting transfers between devices: 7.01 us -> 6.06 us  [shift(): return lax.ppermute(x, axis, [(i, (i + by) % n) for i in range(n)])]
    unnamed x1 -> x0, other arithmetic: 0.91 us -> none
    concatenate x1, other arithmetic: 0.86 us -> 0.03 us  [gather_tokens(): jnp.concatenate([rows] + [shift(rows, 'expert', by) for by in range(2, ow...]
  transfers between devices with their start and end apart: 7 -> 7, of which waited for: 6 -> 4; matrix products, arithmetic and copies ran while one was open for 0% -> 0% of each run, Pallas kernels for 27% -> 44%
where the time goes in v2:
time: 39.3 us; the launch traced here: 39 us
  Pallas kernels  20.8 us (53%)
  starting transfers between devices  9.84 us (25%)
  waiting for transfers between devices  4.64 us (12%)
  local copies, waits for them, and re-layouts  1.96 us (5%)
  other arithmetic  1.68 us (4%)
    pallas_call x2, Pallas kernels, weights(): pl.pallas_call(functools.partial(weights_kernel, expert), in_specs=[pl.Bl...  9.78 us
    pallas_call x4, Pallas kernels, gram_block(): pl.pallas_call(functools.partial(gram_kernel, turned), grid=(width // blo...  7.17 us
    ppermute x3, starting transfers between devices, shift(): return lax.ppermute(x, axis, [(i, (i + by) % n) for i in range(n)])  6.06 us
    ppermute x4, waiting for transfers between devices, swap(): return lax.ppermute(x, axis, [(i, i ^ 1) for i in range(n)])  4.63 us
    pallas_call x2, Pallas kernels, hidden_units(): pl.pallas_call(functools.partial(hidden_kernel, owned, expert), in_specs=...  3.87 us
    ppermute x4, starting transfers between devices, swap(): return lax.ppermute(x, axis, [(i, i ^ 1) for i in range(n)])  3.78 us
    unnamed x9, local copies, waits for them, and re-layouts  1.9 us
    concatenate x1, other arithmetic, paired(): x, done = gather_tokens(jnp.concatenate([tokens, named], axis=1), done)  0.92 us
  transfers between devices with their start and end apart: 7, of which 4 were waited for; matrix products, arithmetic and copies ran while one was open for 0% of the time, Pallas kernels for 44%

profile of v2, /device:TPU:0, one launch (start us, length us, event | category | flops | bytes accessed | tf_op | source)
XLA Modules:
  0.0 39.0 jit_solution(13464575664996053189)
XLA Ops:
  0.0 0.7 %convert_element_type.5 = bf16[8,8]{1,0:T(8,128)(2,1)S(1)} convert(s32[8,8]{1,0:T(8,128)} %param.7) | non-fusion elementwise | flops 64 | bytes 384 | tf_op jit(solution)/shard_map/convert_element_type | solution.py:228
  0.7 0.0 copy-start.3
  0.7 0.9 %pad_maximum_fusion.2 = bf16[8,4224]{1,0:T(8,128)(2,1)S(1)} fusion(bf16[8,128]{1,0:T(8,128)(2,1)S(1)} %pad.4, bf16[8,4096]{1,0:T(8,128)(2,1)} %param.6), kind=kLoop, calls=%fused_computation.2 | loop fusion | flops 135168 | bytes 135168 | tf_op jit(solution)/shard_map/concatenate | solution.py:233
  1.6 5.0 %collective-permute-start.2 = (bf16[8,4224]{1,0:T(8,128)(2,1)S(1)}, bf16[8,4224]{1,0:T(8,128)(2,1)S(1)}, u32[]{:S(2)}, u32[]{:S(2)}) collective-permute-start(bf16[8,4224]{1,0:T(8,128)(2,1)S(1)} %pad_maximum_fusion.2), channel_id=1, source_target_pairs={{0,12},{2,14},{4,0},{6,2},{8,4},{10,6},{12,8},{14,10},{1,13},{3,15... | collective-permute-start | bytes 202760 | tf_op jit(solution)/shard_map/ppermute | solution.py:85
  6.7 0.0 collective-permute-start.1
  6.7 1.0 %collective-permute-start = (bf16[8,4224]{1,0:T(8,128)(2,1)S(1)}, bf16[8,4224]{1,0:T(8,128)(2,1)S(1)}, u32[]{:S(2)}, u32[]{:S(2)}) collective-permute-start(bf16[8,4224]{1,0:T(8,128)(2,1)S(1)} %pad_maximum_fusion.2), channel_id=1, source_target_pairs={{0,4},{2,6},{4,8},{6,10},{8,12},{10,14},{12,0},{14,2},{1,5},{3,7},... | collective-permute-start | bytes 202760 | tf_op jit(solution)/shard_map/ppermute | solution.py:85
  7.7 0.0 copy-start
  7.7 0.9 %copy-done = f32[2,32,768]{2,1,0:T(8,128)S(1)} copy-done((f32[2,32,768]{2,1,0:T(8,128)S(1)}, f32[2,32,768]{2,1,0:T(8,128)}, u32[]{:S(2)}) %copy-start) | copy-done | bytes 196632
  8.6 0.0 copy-start.2
  8.6 0.9 %copy-done.2 = f32[2,32,768]{2,1,0:T(8,128)S(1)} copy-done((f32[2,32,768]{2,1,0:T(8,128)S(1)}, f32[2,32,768]{2,1,0:T(8,128)}, u32[]{:S(2)}) %copy-start.2) | copy-done | bytes 196632
  9.5 0.0 copy-start.1
  9.5 4.9 %shard_map.64 = (bf16[2,4096,768]{2,1,0:T(8,128)(2,1)S(1)}, f32[8,128]{1,0:T(8,128)S(1)}) custom-call(bf16[2,4096,768]{2,1,0:T(8,128)(2,1)} %gate_ref.3, bf16[2,4096,768]{2,1,0:T(8,128)(2,1)} %up_ref.3, f32[2,32,768]{2,1,0:T(8,128)S(1)} %copy-done, f32[2,32,768]{2,1,0:T(8,128)S(1)} %copy-done.2), custom_call_target="tpu_custom_call" | custom-call | flops 6291456 | bytes 12582912 | tf_op jit(solution)/shard_map/pallas_call | solution.py:134
  14.5 0.0 collective-permute-done.2
  14.5 0.0 collective-permute-done.1
  14.5 0.0 collective-permute-done
  14.5 0.0 copy-done.3
  14.5 1.6 %collective-permute-start.3 = (bf16[32,4224]{1,0:T(8,128)(2,1)S(1)}, bf16[32,4224]{1,0:T(8,128)(2,1)S(1)}, u32[]{:S(2)}, u32[]{:S(2)}) collective-permute-start(bf16[32,4224]{1,0:T(8,128)(2,1)S(1)} %pad_maximum_fusion.1), channel_id=1, source_target_pairs={{0,1},{1,0},{2,3},{3,2},{4,5},{5,4},{6,7},{7,6},{8,9},{9,8},{10,11... | collective-permute-start | bytes 811016 | tf_op jit(solution)/shard_map/ppermute | solution.py:90
  16.1 0.0 copy-done.1
  16.1 4.9 %shard_map.65 = (bf16[2,4096,768]{2,1,0:T(8,128)(2,1)S(1)}, f32[8,128]{1,0:T(8,128)S(1)}) custom-call(bf16[2,4096,768]{2,1,0:T(8,128)(2,1)} %gate_ref.3, bf16[2,4096,768]{2,1,0:T(8,128)(2,1)} %up_ref.3, f32[2,32,768]{2,1,0:T(8,128)S(1)} %copy-done.1, f32[2,32,768]{2,1,0:T(8,128)S(1)} %copy-done.2), custom_call_target="tpu_custom_call" | custom-call | flops 6291456 | bytes 12582912 | tf_op jit(solution)/shard_map/pallas_call | solution.py:134
  21.0 1.0 %collective-permute-done.3 = bf16[32,4224]{1,0:T(8,128)(2,1)S(1)} collective-permute-done((bf16[32,4224]{1,0:T(8,128)(2,1)S(1)}, bf16[32,4224]{1,0:T(8,128)(2,1)S(1)}, u32[]{:S(2)}, u32[]{:S(2)}) %collective-permute-start.3) | collective-permute-done | bytes 270368 | tf_op jit(solution)/shard_map/ppermute | solution.py:90
  22.0 0.1 collective-permute-start.4
  22.1 1.9 %collective-permute-done.4 = bf16[64,4224]{1,0:T(8,128)(2,1)S(1)} collective-permute-done((bf16[64,4224]{1,0:T(8,128)(2,1)S(1)}, bf16[64,4224]{1,0:T(8,128)(2,1)S(1)}, u32[]{:S(2)}, u32[]{:S(2)}) %collective-permute-start.4) | collective-permute-done | bytes 540704 | tf_op jit(solution)/shard_map/ppermute | solution.py:90
  24.1 1.9 %shard_map.67 = (bf16[128,768]{1,0:T(8,128)(2,1)S(1)}, f32[8,128]{1,0:T(8,128)S(1)}) custom-call(f32[8,128]{1,0:T(8,128)S(1)} %get-tuple-element.25.done_ref, bf16[128,4224]{1,0:T(8,128)(2,1)S(1)} %constant_dynamic-update-slice_fusion.x_ref, bf16[2,4096,768]{2,1,0:T(8,128)(2,1)S(1)} %get-tuple-element.26.w_ref), custom_call_target="tpu_custom_call" | custom-call | flops 1610612736 | bytes 6291456 | tf_op jit(solution)/shard_map/pallas_call | solution.py:168
  26.0 1.6 %collective-permute-start.6 = (bf16[128,768]{1,0:T(8,128)(2,1)S(1)}, bf16[128,768]{1,0:T(8,128)(2,1)S(1)}, u32[]{:S(2)}, u32[]{:S(2)}) collective-permute-start(bf16[128,768]{1,0:T(8,128)(2,1)S(1)} %get-tuple-element.28.left_ref.right_ref), channel_id=1, source_target_pairs={{0,1},{1,0},{2,3},{3,2},{4,5},{5,4},{6,7},{7,6},{8,9},{9,8},{10,11... | collective-permute-start | bytes 589832 | tf_op jit(solution)/shard_map/ppermute | solution.py:90
  27.6 1.9 %shard_map.66 = (bf16[128,768]{1,0:T(8,128)(2,1)S(1)}, f32[8,128]{1,0:T(8,128)S(1)}) custom-call(f32[8,128]{1,0:T(8,128)S(1)} %get-tuple-element.20.done_ref, bf16[128,4224]{1,0:T(8,128)(2,1)S(1)} %constant_dynamic-update-slice_fusion.x_ref, bf16[2,4096,768]{2,1,0:T(8,128)(2,1)S(1)} %get-tuple-element.22.w_ref), custom_call_target="tpu_custom_call" | custom-call | flops 1610612736 | bytes 6291456 | tf_op jit(solution)/shard_map/pallas_call | solution.py:168
  29.5 0.6 %collective-permute-start.5 = (bf16[128,768]{1,0:T(8,128)(2,1)S(1)}, bf16[128,768]{1,0:T(8,128)(2,1)S(1)}, u32[]{:S(2)}, u32[]{:S(2)}) collective-permute-start(bf16[128,768]{1,0:T(8,128)(2,1)S(1)} %get-tuple-element.24.left_ref.right_ref), channel_id=1, source_target_pairs={{0,1},{1,0},{2,3},{3,2},{4,5},{5,4},{6,7},{7,6},{8,9},{9,8},{10,11... | collective-permute-start | bytes 589832 | tf_op jit(solution)/shard_map/ppermute | solution.py:90
  30.1 1.8 %shard_map.68.out_refs_0_ = f32[2,768,1536]{2,1,0:T(8,128)} custom-call(f32[8,128]{1,0:T(8,128)S(1)} %get-tuple-element.27.scale_ref, bf16[128,768]{1,0:T(8,128)(2,1)S(1)} %get-tuple-element.28.left_ref.right_ref, bf16[128,768]{1,0:T(8,128)(2,1)S(1)} %get-tuple-element.28.left_ref.right_ref), custom_call_target="tpu_custom_call" | custom-call | flops 150994944 | bytes 2359296 | tf_op jit(solution)/shard_map/pallas_call | solution.py:206
  31.9 1.8 %shard_map.69.out_refs_0_ = f32[2,768,1536]{2,1,0:T(8,128)} custom-call(f32[8,128]{1,0:T(8,128)S(1)} %get-tuple-element.23.scale_ref, bf16[128,768]{1,0:T(8,128)(2,1)S(1)} %get-tuple-element.24.left_ref.right_ref, bf16[128,768]{1,0:T(8,128)(2,1)S(1)} %get-tuple-element.24.left_ref.right_ref, ...), custom_call_target="tpu_custom_call", output_to_operand_aliasing={{}: (3, {})} | custom-call | flops 150994944 | bytes 2359296 | tf_op jit(solution)/shard_map/pallas_call | solution.py:206
  33.7 0.1 collective-permute-done.6.right_ref
  33.8 1.8 %shard_map.70.out_refs_0_ = f32[2,768,1536]{2,1,0:T(8,128)} custom-call(f32[8,128]{1,0:T(8,128)S(1)} %get-tuple-element.27.scale_ref, bf16[128,768]{1,0:T(8,128)(2,1)S(1)} %get-tuple-element.28.left_ref.right_ref, bf16[128,768]{1,0:T(8,128)(2,1)S(1)} %collective-permute-done.6.right_ref, ...), custom_call_target="tpu_custom_call", output_to_operand_aliasing={{}: (3, {})} | custom-call | flops 150994944 | bytes 2359296 | tf_op jit(solution)/shard_map/pallas_call | solution.py:206
  35.6 1.6 %collective-permute-done.5.right_ref = bf16[128,768]{1,0:T(8,128)(2,1)S(1)} collective-permute-done((bf16[128,768]{1,0:T(8,128)(2,1)S(1)}, bf16[128,768]{1,0:T(8,128)(2,1)S(1)}, u32[]{:S(2)}, u32[]{:S(2)}) %collective-permute-start.5) | collective-permute-done | bytes 196640 | tf_op jit(solution)/shard_map/ppermute | solution.py:90
  37.2 1.8 %shard_map.71 = f32[2,768,1536]{2,1,0:T(8,128)} custom-call(f32[8,128]{1,0:T(8,128)S(1)} %get-tuple-element.23.scale_ref, bf16[128,768]{1,0:T(8,128)(2,1)S(1)} %get-tuple-element.24.left_ref.right_ref, bf16[128,768]{1,0:T(8,128)(2,1)S(1)} %collective-permute-done.5.right_ref, f32[2,768,1536]{2,1,0:T(8,128)} %shard_map.70.out_refs_0_), custom_call_target="tpu_custom_call", output_to_operand_aliasing={{}: (3, {})} | custom-call | flops 150994944 | bytes 2359296 | tf_op jit(solution)/shard_map/pallas_call | solution.py:206
  (5 shorter events, 0.2 us)
Async XLA Ops:
  0.7 13.8 %copy-start.3 = (bf16[8,4096]{1,0:T(8,128)(2,1)S(1)}, bf16[8,4096]{1,0:T(8,128)(2,1)}, u32[]{:S(2)}) copy-start(bf16[8,4096]{1,0:T(8,128)(2,1)} %param.6) | copy-start | bytes 196612
  1.6 12.8 %collective-permute-start.2 = (bf16[8,4224]{1,0:T(8,128)(2,1)S(1)}, bf16[8,4224]{1,0:T(8,128)(2,1)S(1)}, u32[]{:S(2)}, u32[]{:S(2)}) collective-permute-start(bf16[8,4224]{1,0:T(8,128)(2,1)S(1)} %pad_maximum_fusion.2), channel_id=1, source_target_pairs={{0,12},{2,14},{4,0},{6,2},{8,4},{10,6},{12,8},{14,10},{1,13},{3,15... | collective-permute-start | bytes 202760 | tf_op jit(solution)/shard_map/ppermute | solution.py:85
  6.7 7.8 %collective-permute-start.1 = (bf16[8,4224]{1,0:T(8,128)(2,1)S(1)}, bf16[8,4224]{1,0:T(8,128)(2,1)S(1)}, u32[]{:S(2)}, u32[]{:S(2)}) collective-permute-start(bf16[8,4224]{1,0:T(8,128)(2,1)S(1)} %pad_maximum_fusion.2), channel_id=1, source_target_pairs={{0,8},{2,10},{4,12},{6,14},{8,0},{10,2},{12,4},{14,6},{1,9},{3,11}... | collective-permute-start | bytes 202760 | tf_op jit(solution)/shard_map/ppermute | solution.py:85
  6.7 7.8 %collective-permute-start = (bf16[8,4224]{1,0:T(8,128)(2,1)S(1)}, bf16[8,4224]{1,0:T(8,128)(2,1)S(1)}, u32[]{:S(2)}, u32[]{:S(2)}) collective-permute-start(bf16[8,4224]{1,0:T(8,128)(2,1)S(1)} %pad_maximum_fusion.2), channel_id=1, source_target_pairs={{0,4},{2,6},{4,8},{6,10},{8,12},{10,14},{12,0},{14,2},{1,5},{3,7},... | collective-permute-start | bytes 202760 | tf_op jit(solution)/shard_map/ppermute | solution.py:85
  7.7 0.9 %copy-start = (f32[2,32,768]{2,1,0:T(8,128)S(1)}, f32[2,32,768]{2,1,0:T(8,128)}, u32[]{:S(2)}) copy-start(f32[2,32,768]{2,1,0:T(8,128)} %gate_scale_ref.3) | copy-start | bytes 589828
  8.6 0.9 %copy-start.2 = (f32[2,32,768]{2,1,0:T(8,128)S(1)}, f32[2,32,768]{2,1,0:T(8,128)}, u32[]{:S(2)}) copy-start(f32[2,32,768]{2,1,0:T(8,128)} %up_scale_ref.3) | copy-start | bytes 589828
  9.5 6.5 %copy-start.1 = (f32[2,32,768]{2,1,0:T(8,128)S(1)}, f32[2,32,768]{2,1,0:T(8,128)}, u32[]{:S(2)}) copy-start(f32[2,32,768]{2,1,0:T(8,128)} %gate_scale_ref.3) | copy-start | bytes 589828
  14.5 7.4 %collective-permute-start.3 = (bf16[32,4224]{1,0:T(8,128)(2,1)S(1)}, bf16[32,4224]{1,0:T(8,128)(2,1)S(1)}, u32[]{:S(2)}, u32[]{:S(2)}) collective-permute-start(bf16[32,4224]{1,0:T(8,128)(2,1)S(1)} %pad_maximum_fusion.1), channel_id=1, source_target_pairs={{0,1},{1,0},{2,3},{3,2},{4,5},{5,4},{6,7},{7,6},{8,9},{9,8},{10,11... | collective-permute-start | bytes 811016 | tf_op jit(solution)/shard_map/ppermute | solution.py:90
  22.0 2.0 %collective-permute-start.4 = (bf16[64,4224]{1,0:T(8,128)(2,1)S(1)}, bf16[64,4224]{1,0:T(8,128)(2,1)S(1)}, u32[]{:S(2)}, u32[]{:S(2)}) collective-permute-start(bf16[64,4224]{1,0:T(8,128)(2,1)S(1)} %pad_maximum_fusion), channel_id=1, source_target_pairs={{0,2},{2,0},{4,6},{6,4},{8,10},{10,8},{12,14},{14,12},{1,3},{3,1},... | collective-permute-start | bytes 1622024 | tf_op jit(solution)/shard_map/ppermute | solution.py:90
  26.0 7.8 %collective-permute-start.6 = (bf16[128,768]{1,0:T(8,128)(2,1)S(1)}, bf16[128,768]{1,0:T(8,128)(2,1)S(1)}, u32[]{:S(2)}, u32[]{:S(2)}) collective-permute-start(bf16[128,768]{1,0:T(8,128)(2,1)S(1)} %get-tuple-element.28.left_ref.right_ref), channel_id=1, source_target_pairs={{0,1},{1,0},{2,3},{3,2},{4,5},{5,4},{6,7},{7,6},{8,9},{9,8},{10,11... | collective-permute-start | bytes 589832 | tf_op jit(solution)/shard_map/ppermute | solution.py:90
  29.5 7.7 %collective-permute-start.5 = (bf16[128,768]{1,0:T(8,128)(2,1)S(1)}, bf16[128,768]{1,0:T(8,128)(2,1)S(1)}, u32[]{:S(2)}, u32[]{:S(2)}) collective-permute-start(bf16[128,768]{1,0:T(8,128)(2,1)S(1)} %get-tuple-element.24.left_ref.right_ref), channel_id=1, source_target_pairs={{0,1},{1,0},{2,3},{3,2},{4,5},{5,4},{6,7},{7,6},{8,9},{9,8},{10,11... | collective-permute-start | bytes 589832 | tf_op jit(solution)/shard_map/ppermute | solution.py:90

commit v3 on v0

--- a/solution.py
+++ b/solution.py
@@ -1,9 +1,17 @@
+import functools
+
 import jax
 import jax.numpy as jnp
 from jax import lax
+from jax.experimental import pallas as pl
+from jax.experimental.pallas import tpu as pltpu
 from jax.sharding import PartitionSpec as P
 
 TOP = 8
+LANES = 128
+HIDDEN_BLOCK = 128
+F32 = jnp.float32
+BF16 = jnp.bfloat16
 
 
 def dequantize(codes, scales):
@@ -26,7 +34,7 @@
     return (table.astype(jnp.bfloat16), jnp.sum(member, axis=-2))
 
 
-def local(tokens, expert_ids, gate_codes, up_codes, gate_scales, up_scales):
+def general(tokens, expert_ids, gate_codes, up_codes, gate_scales, up_scales):
     tok_dev, width = tokens.shape
     owned = gate_codes.shape[0]
     owners = lax.axis_size("expert")
@@ -72,6 +80,230 @@
     return gram * (2.0 / totals)[:, None, None]
 
 
+def shift(x, axis, by):
+    n = lax.axis_size(axis)
+    return lax.ppermute(x, axis, [(i, (i + by) % n) for i in range(n)])
+
+
+def swap(x, axis):
+    n = lax.axis_size(axis)
+    return lax.ppermute(x, axis, [(i, i ^ 1) for i in range(n)])
+
+
+def label_kernel(rows_ref, ids_ref, out_ref):
+    depth = rows_ref.shape[1]
+    ids = ids_ref[...].astype(F32).astype(BF16)
+    blank = jnp.full((ids.shape[0], LANES - ids.shape[1]), -1, BF16)
+    out_ref[:, :depth] = rows_ref[...]
+    out_ref[:, depth:] = jnp.concatenate([ids, blank], axis=1)
+
+
+def label(rows, ids, cost):
+    rows = pltpu.with_memory_space_constraint(rows, pltpu.HBM)
+    ids = pltpu.with_memory_space_constraint(ids, pltpu.HBM)
+    return pl.pallas_call(
+        label_kernel,
+        out_shape=jax.ShapeDtypeStruct((rows.shape[0], rows.shape[1] + LANES), BF16),
+        compiler_params=pltpu.CompilerParams(vmem_limit_bytes=1 << 20),
+        cost_estimate=pl.CostEstimate(flops=cost, bytes_accessed=1 << 20, transcendentals=0),
+    )(rows, ids)
+
+
+def join_kernel(done_ref, *refs):
+    del done_ref
+    parts = [ref[...].astype(F32) for ref in refs[:-1]]
+    refs[-1][...] = jnp.concatenate(parts).astype(BF16)
+
+
+def join(done, parts):
+    rows = sum(part.shape[0] for part in parts)
+    return pl.pallas_call(
+        join_kernel,
+        in_specs=[pl.BlockSpec(memory_space=pltpu.VMEM)] * (1 + len(parts)),
+        out_specs=pl.BlockSpec(memory_space=pltpu.VMEM),
+        out_shape=jax.ShapeDtypeStruct((rows, parts[0].shape[1]), BF16),
+        compiler_params=pltpu.CompilerParams(vmem_limit_bytes=1 << 20),
+        cost_estimate=pl.CostEstimate(
+            flops=0, bytes_accessed=4 * rows * parts[0].shape[1], transcendentals=0
+        ),
+    )(done, *parts)
+
+
+def weights_kernel(codes_ref, scale_ref, *refs):
+    w_refs, done_ref = refs[:-1], refs[-1]
+    owned, depth, _ = codes_ref.shape
+    groups = scale_ref.shape[1]
+    step = depth // groups
+    done_ref[...] = jnp.zeros_like(done_ref)
+    for expert in range(owned):
+
+        @pl.loop(0, groups)
+        def _(i):
+            part = pl.ds(pl.multiple_of(i * step, step), step)
+            scale = scale_ref[expert, pl.ds(i, 1), :]
+            w_refs[expert][part, :] = (codes_ref[expert, part, :].astype(F32) * scale).astype(BF16)
+
+
+def weights(codes, scales):
+    owned = codes.shape[0]
+    return pl.pallas_call(
+        weights_kernel,
+        in_specs=[pl.BlockSpec(memory_space=pltpu.VMEM)] * 2,
+        out_specs=[pl.BlockSpec(memory_space=pltpu.VMEM)] * (owned + 1),
+        out_shape=[pltpu.VMEM(codes.shape[1:], BF16)] * owned
+        + [jax.ShapeDtypeStruct((8, LANES), F32)],
+        compiler_params=pltpu.CompilerParams(vmem_limit_bytes=1 << 20),
+        cost_estimate=pl.CostEstimate(
+            flops=1 << 33, bytes_accessed=4 * codes.size, transcendentals=0
+        ),
+    )(codes, scales)
+
+
+def hidden_kernel(owned, experts, done_ref, mine_ref, theirs_ref, *refs):
+    del done_ref
+    w_refs, h_ref, count_ref = refs[:-2], refs[-2], refs[-1]
+    depth, width = w_refs[0].shape
+    block = HIDDEN_BLOCK if width % HIDDEN_BLOCK == 0 else width
+    labelled = jnp.concatenate([mine_ref[...], theirs_ref[...]])
+    named = labelled[:, depth:].astype(F32)
+    x = labelled[:, :depth]
+    for at, expert in enumerate(experts):
+        which = lax.axis_index("expert") * owned + expert
+        member = jnp.sum((named == which.astype(F32)).astype(F32), axis=1, keepdims=True)
+        count_ref[at] = jnp.broadcast_to(jnp.sum(member, keepdims=True), count_ref.shape[1:])
+        for col in range(0, width, block):
+            cols = pl.ds(col, block)
+            gate = jnp.dot(x, w_refs[2 * at][:, cols], preferred_element_type=F32)
+            up = jnp.dot(x, w_refs[2 * at + 1][:, cols], preferred_element_type=F32)
+            value = gate / (1.0 + jnp.exp(-gate)) * up
+            h_ref[at, :, cols] = jnp.where(member > 0, value, 0.0).astype(BF16)
+
+
+def hidden_units(owned, experts, done, x, w):
+    depth, width = w[0][0].shape
+    flat = [w[e][i] for e in experts for i in range(2)]
+    rows = sum(part.shape[0] for part in x)
+    return pl.pallas_call(
+        functools.partial(hidden_kernel, owned, experts),
+        in_specs=[pl.BlockSpec(memory_space=pltpu.VMEM)] * (3 + len(flat)),
+        out_specs=[pl.BlockSpec(memory_space=pltpu.VMEM)] * 2,
+        out_shape=[
+            jax.ShapeDtypeStruct((len(experts), rows, width), BF16),
+            jax.ShapeDtypeStruct((len(experts), 8, LANES), F32),
+        ],
+        compiler_params=pltpu.CompilerParams(vmem_limit_bytes=4 << 20),
+        cost_estimate=pl.CostEstimate(
+            flops=4 * len(experts) * rows * depth * width,
+            bytes_accessed=4 * len(experts) * depth * width,
+            transcendentals=len(experts) * rows * width,
+        ),
+    )(done, *x, *flat)
+
+
+def gram_kernel(jobs, *refs):
+    n = len(jobs)
+    blocks = [refs[6 * i : 6 * i + 6] for i in range(n)]
+    out_ref, buffer, sems = refs[-3:]
+    me = lax.axis_index("dp")
+    width = buffer.shape[2]
+    half = width // 2
+    copies = []
+    for i, (expert, first, second, theirs) in enumerate(jobs):
+        place = pl.ds(pl.multiple_of((1 - me if theirs else me) * width, LANES), width)
+        left_a, left_b, right_a, right_b, count_a, count_b = blocks[i]
+        left = jnp.concatenate([left_a[first], left_b[second]])
+        if theirs:
+            right = jnp.concatenate([right_b[second], right_a[first]])
+        else:
+            right = jnp.concatenate([right_a[first], right_b[second]])
+        scale = 2.0 / (count_a[first, 0:1, 0:1] + count_b[second, 0:1, 0:1])
+        for part in range(2):
+            rows = pl.ds(part * half, half)
+            product = lax.dot_general(
+                left[:, part * half : (part + 1) * half],
+                right,
+                (((0,), (0,)), ((), ())),
+                preferred_element_type=F32,
+            )
+            buffer[i, rows, :] = product * scale
+            copy = pltpu.make_async_copy(
+                buffer.at[i, rows], out_ref.at[expert, rows, place], sems.at[i, part]
+            )
+            copy.start()
+            copies.append(copy)
+    for copy in copies:
+        copy.wait()
+
+
+def gram_blocks(jobs, operands, shape, onto=None):
+    width = shape[1]
+    n = len(jobs)
+    flat = [x for group in operands for x in group]
+    return pl.pallas_call(
+        functools.partial(gram_kernel, jobs),
+        in_specs=[pl.BlockSpec(memory_space=pltpu.VMEM)] * len(flat)
+        + ([] if onto is None else [pl.BlockSpec(memory_space=pl.ANY)]),
+        out_specs=pl.BlockSpec(memory_space=pl.ANY),
+        out_shape=jax.ShapeDtypeStruct(shape, F32),
+        input_output_aliases={} if onto is None else {len(flat): 0},
+        scratch_shapes=[
+            pltpu.VMEM((n, width, width), F32),
+            pltpu.SemaphoreType.DMA((n, 2)),
+        ],
+        compiler_params=pltpu.CompilerParams(vmem_limit_bytes=12 << 20),
+        cost_estimate=pl.CostEstimate(
+            flops=2 * n * 128 * width * width,
+            bytes_accessed=4 * n * width * width,
+            transcendentals=0,
+        ),
+    )(*flat, *([] if onto is None else [onto]))
+
+
+def paired(tokens, expert_ids, gate_codes, up_codes, gate_scales, up_scales):
+    owned, _, width = gate_codes.shape
+    owners = lax.axis_size("expert")
+    every = tuple(range(owned))
+    rows = label(tokens, expert_ids, 1 << 34)
+    *w_gate, gate_done = weights(gate_codes, gate_scales)
+    near = join(gate_done, [rows] + [shift(rows, "expert", by) for by in range(2, owners, 2)])
+    far = swap(near, "dp")
+    *w_up, up_done = weights(up_codes, up_scales)
+    w = list(zip(w_gate, w_up))
+    near = (near, swap(near, "expert"))
+    near_hidden, near_count = hidden_units(owned, every, up_done, near, w)
+    far, near_count = lax.optimization_barrier((far, near_count))
+    far = (far, swap(far, "expert"))
+    near_other = swap(near_hidden, "dp")
+    far_parts = [hidden_units(owned, (e,), up_done, far, w) for e in every]
+    far_other = [swap(hidden, "dp") for hidden, _ in far_parts]
+    shape = (owned, width, 2 * width)
+    own, other = [], []
+    for e in every:
+        hidden, count = far_parts[e]
+        own.append((near_hidden, hidden, near_hidden, hidden, near_count, count))
+        other.append((near_hidden, hidden, near_other, far_other[e], near_count, count))
+    last = owned - 1
+    jobs = [(e, e, 0, False) for e in every] + [(e, e, 0, True) for e in range(last)]
+    out = gram_blocks(jobs, own + other[:last], shape)
+    return gram_blocks([(last, last, 0, True)], other[last:], shape, out)
+
+
+def local(tokens, expert_ids, gate_codes, up_codes, gate_scales, up_scales):
+    args = (tokens, expert_ids, gate_codes, up_codes, gate_scales, up_scales)
+    owned, depth, width = gate_codes.shape
+    fits = (
+        lax.axis_size("dp") == 2
+        and lax.axis_size("expert") % 2 == 0
+        and width % LANES == 0
+        and depth % (16 * gate_scales.shape[1]) == 0
+        and tokens.shape[0] * (lax.axis_size("expert") // 2) % 16 == 0
+        and expert_ids.shape[1] <= LANES
+        and owned * lax.axis_size("expert") <= 256
+        and owned * depth * width * 4 <= 32 << 20
+    )
+    return paired(*args) if fits else general(*args)
+
+
 def solution(mesh):
     return jax.shard_map(
         local,

time: 94.5 us -> 35.3 us (0.37)
  the two profiles are of different devices: /device:TPU:13 before, /device:TPU:0 now
where the time goes in v3:
time: 35.3 us; the launch traced here: 35.1 us
  Pallas kernels  19.1 us (54%)
  starting transfers between devices  12.5 us (35%)
  waiting for transfers between devices  3.42 us (10%)
    pallas_call x3, Pallas kernels, hidden_units(): pl.pallas_call(functools.partial(hidden_kernel, owned, experts), in_specs...  7.96 us
    ppermute x3, starting transfers between devices, shift(): return lax.ppermute(x, axis, [(i, (i + by) % n) for i in range(n)])  7.03 us
    ppermute x6, starting transfers between devices, swap(): return lax.ppermute(x, axis, [(i, i ^ 1) for i in range(n)])  5.47 us
    pallas_call x2, Pallas kernels, gram_blocks(): pl.pallas_call(functools.partial(gram_kernel, jobs), in_specs=[pl.BlockSp...  5.2 us
    pallas_call x2, Pallas kernels, weights(): pl.pallas_call(weights_kernel, in_specs=[pl.BlockSpec(memory_space=pltpu....  4.92 us
    ppermute x6, waiting for transfers between devices, swap(): return lax.ppermute(x, axis, [(i, i ^ 1) for i in range(n)])  2.46 us
    pallas_call x1, Pallas kernels, label(): pl.pallas_call(label_kernel, out_shape=jax.ShapeDtypeStruct((rows.shape[0...  1 us
    ppermute x3, waiting for transfers between devices, shift(): return lax.ppermute(x, axis, [(i, (i + by) % n) for i in range(n)])  0.96 us
  transfers between devices with their start and end apart: 9, of which 4 were waited for; matrix products, arithmetic and copies ran while one was open for 0% of the time, Pallas kernels for 46%

profile of v3, /device:TPU:0, one launch (start us, length us, event | category | flops | bytes accessed | tf_op | source)
XLA Modules:
  0.0 35.1 jit_solution(2358073747337959178)
XLA Ops:
  0.0 1.0 %shard_map.66.refs_0_ = bf16[8,4224]{1,0:T(8,128)(2,1)S(1)} custom-call(bf16[8,4096]{1,0:T(8,128)(2,1)} %rows_ref.1, s32[8,8]{1,0:T(8,128)} %ids_ref.1), custom_call_target="tpu_custom_call" | custom-call | flops 17179869184 | bytes 1048576 | tf_op jit(solution)/shard_map/pallas_call | solution.py:104
  1.0 0.0 copy-start.2
  1.0 3.1 %collective-permute-start = (bf16[8,4224]{1,0:T(8,128)(2,1)S(1)}, bf16[8,4224]{1,0:T(8,128)(2,1)S(1)}, u32[]{:S(2)}, u32[]{:S(2)}) collective-permute-start(bf16[8,4224]{1,0:T(8,128)(2,1)S(1)} %shard_map.66.refs_0_), channel_id=1, source_target_pairs={{0,4},{2,6},{4,8},{6,10},{8,12},{10,14},{12,0},{14,2},{1,5},{3,7},... | collective-permute-start | bytes 202760 | tf_op jit(solution)/shard_map/ppermute | solution.py:85
  4.1 2.6 %collective-permute-start.1 = (bf16[8,4224]{1,0:T(8,128)(2,1)S(1)}, bf16[8,4224]{1,0:T(8,128)(2,1)S(1)}, u32[]{:S(2)}, u32[]{:S(2)}) collective-permute-start(bf16[8,4224]{1,0:T(8,128)(2,1)S(1)} %shard_map.66.refs_0_), channel_id=1, source_target_pairs={{0,8},{2,10},{4,12},{6,14},{8,0},{10,2},{12,4},{14,6},{1,9},{3,11}... | collective-permute-start | bytes 202760 | tf_op jit(solution)/shard_map/ppermute | solution.py:85
  6.7 1.3 %collective-permute-start.2 = (bf16[8,4224]{1,0:T(8,128)(2,1)S(1)}, bf16[8,4224]{1,0:T(8,128)(2,1)S(1)}, u32[]{:S(2)}, u32[]{:S(2)}) collective-permute-start(bf16[8,4224]{1,0:T(8,128)(2,1)S(1)} %shard_map.66.refs_0_), channel_id=1, source_target_pairs={{0,12},{2,14},{4,0},{6,2},{8,4},{10,6},{12,8},{14,10},{1,13},{3,15... | collective-permute-start | bytes 202760 | tf_op jit(solution)/shard_map/ppermute | solution.py:85
  8.1 0.0 copy-done
  8.1 0.0 copy-done.1
  8.1 2.5 %shard_map.65 = (bf16[4096,768]{1,0:T(8,128)(2,1)S(1)}, bf16[4096,768]{1,0:T(8,128)(2,1)S(1)}, f32[8,128]{1,0:T(8,128)S(1)}) custom-call(bf16[2,4096,768]{2,1,0:T(8,128)(2,1)S(1)} %copy-done, f32[2,32,768]{2,1,0:T(8,128)S(1)} %copy-done.1), custom_call_target="tpu_custom_call" | custom-call | flops 8589934592 | bytes 25165824 | tf_op jit(solution)/shard_map/pallas_call | solution.py:149
  10.5 0.0 collective-permute-done.refs_1_
  10.5 0.8 %collective-permute-done.1.refs_2_ = bf16[8,4224]{1,0:T(8,128)(2,1)S(1)} collective-permute-done((bf16[8,4224]{1,0:T(8,128)(2,1)S(1)}, bf16[8,4224]{1,0:T(8,128)(2,1)S(1)}, u32[]{:S(2)}, u32[]{:S(2)}) %collective-permute-start.1) | collective-permute-done | bytes 67616 | tf_op jit(solution)/shard_map/ppermute | solution.py:85
  11.3 0.2 collective-permute-done.2.refs_3_
  11.5 0.1 collective-permute-start.3
  11.6 1.6 %collective-permute-start.4 = (bf16[32,4224]{1,0:T(8,128)(2,1)S(1)}, bf16[32,4224]{1,0:T(8,128)(2,1)S(1)}, u32[]{:S(2)}, u32[]{:S(2)}) collective-permute-start(bf16[32,4224]{1,0:T(8,128)(2,1)S(1)} %shard_map.67.mine_ref), channel_id=1, source_target_pairs={{0,1},{1,0},{2,3},{3,2},{4,5},{5,4},{6,7},{7,6},{8,9},{9,8},{10,11... | collective-permute-start | bytes 811016 | tf_op jit(solution)/shard_map/ppermute | solution.py:90
  13.2 0.0 slice-done
  13.2 0.0 slice-done.1
  13.2 0.0 copy-done.2
  13.3 2.5 %shard_map.64 = (bf16[4096,768]{1,0:T(8,128)(2,1)S(1)}, bf16[4096,768]{1,0:T(8,128)(2,1)S(1)}, f32[8,128]{1,0:T(8,128)S(1)}) custom-call(bf16[2,4096,768]{2,1,0:T(8,128)(2,1)S(1)} %bitcast.1, f32[2,32,768]{2,1,0:T(8,128)S(1)} %copy-done.2), custom_call_target="tpu_custom_call" | custom-call | flops 8589934592 | bytes 25165824 | tf_op jit(solution)/shard_map/pallas_call | solution.py:149
  15.7 0.0 collective-permute-done.3.theirs_ref
  15.7 3.8 %shard_map.68 = (bf16[2,64,768]{2,1,0:T(8,128)(2,1)S(1)}, f32[2,8,128]{2,1,0:T(8,128)S(1)}) custom-call(f32[8,128]{1,0:T(8,128)S(1)} %get-tuple-element.19.done_ref, bf16[32,4224]{1,0:T(8,128)(2,1)S(1)} %shard_map.67.mine_ref, bf16[32,4224]{1,0:T(8,128)(2,1)S(1)} %collective-permute-done.3.theirs_ref, bf16[4096,768]{1,0:T(8,128)(2,1)S(1)} %get-tuple-element.21.refs_0_, ...), custom_call_target="tpu_custom_call" | custom-call | flops 1610612736 | bytes 25165824 | tf_op jit(solution)/shard_map/pallas_call | solution.py:186
  19.5 0.9 %collective-permute-done.4.mine_ref = bf16[32,4224]{1,0:T(8,128)(2,1)S(1)} collective-permute-done((bf16[32,4224]{1,0:T(8,128)(2,1)S(1)}, bf16[32,4224]{1,0:T(8,128)(2,1)S(1)}, u32[]{:S(2)}, u32[]{:S(2)}) %collective-permute-start.4) | collective-permute-done | bytes 270368 | tf_op jit(solution)/shard_map/ppermute | solution.py:90
  20.5 0.0 collective-permute-start.5
  20.5 1.6 %collective-permute-start.6 = (bf16[2,64,768]{2,1,0:T(8,128)(2,1)S(1)}, bf16[2,64,768]{2,1,0:T(8,128)(2,1)S(1)}, u32[]{:S(2)}, u32[]{:S(2)}) collective-permute-start(bf16[2,64,768]{2,1,0:T(8,128)(2,1)S(1)} %get-tuple-element.25.refs_0_.refs_2_.refs_6_.refs_8_.refs_12_), channel_id=1, source_target_pairs={{0,1},{1,0},{2,3},{3,2},{4,5},{5,4},{6,7},{7,6},{8,9},{9,8},{10,11... | collective-permute-start | bytes 589832 | tf_op jit(solution)/shard_map/ppermute | solution.py:90
  22.1 0.0 collective-permute-done.5.theirs_ref
  22.1 2.1 %shard_map.70 = (bf16[1,64,768]{2,1,0:T(8,128)(2,1)S(1)}, f32[1,8,128]{2,1,0:T(8,128)S(1)}) custom-call(f32[8,128]{1,0:T(8,128)S(1)} %get-tuple-element.19.done_ref, bf16[32,4224]{1,0:T(8,128)(2,1)S(1)} %collective-permute-done.4.mine_ref, bf16[32,4224]{1,0:T(8,128)(2,1)S(1)} %collective-permute-done.5.theirs_ref, ...), custom_call_target="tpu_custom_call" | custom-call | flops 805306368 | bytes 12582912 | tf_op jit(solution)/shard_map/pallas_call | solution.py:186
  24.2 1.6 %collective-permute-start.8 = (bf16[1,64,768]{2,1,0:T(8,128)(2,1)S(1)}, bf16[1,64,768]{2,1,0:T(8,128)(2,1)S(1)}, u32[]{:S(2)}, u32[]{:S(2)}) collective-permute-start(bf16[1,64,768]{2,1,0:T(8,128)(2,1)S(1)} %get-tuple-element.31.refs_1_.refs_3_.refs_13_), channel_id=1, source_target_pairs={{0,1},{1,0},{2,3},{3,2},{4,5},{5,4},{6,7},{7,6},{8,9},{9,8},{10,11... | collective-permute-start | bytes 294920 | tf_op jit(solution)/shard_map/ppermute | solution.py:90
  25.8 2.1 %shard_map.69 = (bf16[1,64,768]{2,1,0:T(8,128)(2,1)S(1)}, f32[1,8,128]{2,1,0:T(8,128)S(1)}) custom-call(f32[8,128]{1,0:T(8,128)S(1)} %get-tuple-element.19.done_ref, bf16[32,4224]{1,0:T(8,128)(2,1)S(1)} %collective-permute-done.4.mine_ref, bf16[32,4224]{1,0:T(8,128)(2,1)S(1)} %collective-permute-done.5.theirs_ref, ...), custom_call_target="tpu_custom_call" | custom-call | flops 805306368 | bytes 12582912 | tf_op jit(solution)/shard_map/pallas_call | solution.py:186
  27.8 0.6 %collective-permute-start.7 = (bf16[1,64,768]{2,1,0:T(8,128)(2,1)S(1)}, bf16[1,64,768]{2,1,0:T(8,128)(2,1)S(1)}, u32[]{:S(2)}, u32[]{:S(2)}) collective-permute-start(bf16[1,64,768]{2,1,0:T(8,128)(2,1)S(1)} %get-tuple-element.28.refs_7_.refs_9_.refs_1_), channel_id=1, source_target_pairs={{0,1},{1,0},{2,3},{3,2},{4,5},{5,4},{6,7},{7,6},{8,9},{9,8},{10,11... | collective-permute-start | bytes 294920 | tf_op jit(solution)/shard_map/ppermute | solution.py:90
  28.4 0.0 collective-permute-done.6.refs_14_.refs_2_
  28.4 1.5 %collective-permute-done.8.refs_15_ = bf16[1,64,768]{2,1,0:T(8,128)(2,1)S(1)} collective-permute-done((bf16[1,64,768]{2,1,0:T(8,128)(2,1)S(1)}, bf16[1,64,768]{2,1,0:T(8,128)(2,1)S(1)}, u32[]{:S(2)}, u32[]{:S(2)}) %collective-permute-start.8) | collective-permute-done | bytes 98336 | tf_op jit(solution)/shard_map/ppermute | solution.py:90
  29.9 3.4 %shard_map.71.refs_6_ = f32[2,768,1536]{2,1,0:T(8,128)} custom-call(bf16[2,64,768]{2,1,0:T(8,128)(2,1)S(1)} %get-tuple-element.25.refs_0_.refs_2_.refs_6_.refs_8_.refs_12_, bf16[1,64,768]{2,1,0:T(8,128)(2,1)S(1)} %get-tuple-element.31.refs_1_.refs_3_.refs_13_, bf16[2,64,768]{2,1,0:T(8,128)(2,1)S(1)} %get-tuple-element.25.refs_0_.refs_2_.refs_6_.refs_8_.refs_12_, ...), custom_call_target="tpu_custom_call" | custom-call | flops 452984832 | bytes 7077888 | tf_op jit(solution)/shard_map/pallas_call | solution.py:242
  33.3 0.0 collective-permute-done.7.refs_3_
  33.3 1.8 %shard_map.72 = f32[2,768,1536]{2,1,0:T(8,128)} custom-call(bf16[2,64,768]{2,1,0:T(8,128)(2,1)S(1)} %get-tuple-element.25.refs_0_.refs_2_.refs_6_.refs_8_.refs_12_, bf16[1,64,768]{2,1,0:T(8,128)(2,1)S(1)} %get-tuple-element.28.refs_7_.refs_9_.refs_1_, ...), custom_call_target="tpu_custom_call", output_to_operand_aliasing={{}: (6, {})} | custom-call | flops 150994944 | bytes 2359296 | tf_op jit(solution)/shard_map/pallas_call | solution.py:242
  (8 shorter events, 0.0 us)
Async XLA Ops:
  0.0 8.1 %copy-start = (bf16[2,4096,768]{2,1,0:T(8,128)(2,1)S(1)}, bf16[2,4096,768]{2,1,0:T(8,128)(2,1)}, u32[]{:S(2)}) copy-start(bf16[2,4096,768]{2,1,0:T(8,128)(2,1)} %codes_ref.3) | copy-start | bytes 37748740
  0.0 8.1 %copy-start.1 = (f32[2,32,768]{2,1,0:T(8,128)S(1)}, f32[2,32,768]{2,1,0:T(8,128)}, u32[]{:S(2)}) copy-start(f32[2,32,768]{2,1,0:T(8,128)} %scale_ref.3) | copy-start | bytes 589828
  0.0 13.2 %slice-start = ((s8[12582912]{0:T(1024)(128)(4,1)}), s8[4194304]{0:T(1024)(128)(4,1)S(1)}, s32[]{:S(2)}) async-start(s8[12582912]{0:T(1024)(128)(4,1)} %bitcast), calls=%async_computation | async-start | bytes 8388608
  0.0 13.2 %slice-start.1 = ((s8[12582912]{0:T(1024)(128)(4,1)}), s8[4194304]{0:T(1024)(128)(4,1)S(1)}, s32[]{:S(2)}) async-start(s8[12582912]{0:T(1024)(128)(4,1)} %bitcast), calls=%async_computation.1 | async-start | bytes 8388608
  1.0 12.2 %slice-start.2 = ((s8[12582912]{0:T(1024)(128)(4,1)}), s8[4194304]{0:T(1024)(128)(4,1)S(1)}, s32[]{:S(2)}) async-start(s8[12582912]{0:T(1024)(128)(4,1)} %bitcast), calls=%async_computation.2 | async-start | bytes 8388608
  1.0 12.2 %copy-start.2 = (f32[2,32,768]{2,1,0:T(8,128)S(1)}, f32[2,32,768]{2,1,0:T(8,128)}, u32[]{:S(2)}) copy-start(f32[2,32,768]{2,1,0:T(8,128)} %scale_ref.2) | copy-start | bytes 589828
  1.0 9.5 %collective-permute-start = (bf16[8,4224]{1,0:T(8,128)(2,1)S(1)}, bf16[8,4224]{1,0:T(8,128)(2,1)S(1)}, u32[]{:S(2)}, u32[]{:S(2)}) collective-permute-start(bf16[8,4224]{1,0:T(8,128)(2,1)S(1)} %shard_map.66.refs_0_), channel_id=1, source_target_pairs={{0,4},{2,6},{4,8},{6,10},{8,12},{10,14},{12,0},{14,2},{1,5},{3,7},... | collective-permute-start | bytes 202760 | tf_op jit(solution)/shard_map/ppermute | solution.py:85
  4.1 7.2 %collective-permute-start.1 = (bf16[8,4224]{1,0:T(8,128)(2,1)S(1)}, bf16[8,4224]{1,0:T(8,128)(2,1)S(1)}, u32[]{:S(2)}, u32[]{:S(2)}) collective-permute-start(bf16[8,4224]{1,0:T(8,128)(2,1)S(1)} %shard_map.66.refs_0_), channel_id=1, source_target_pairs={{0,8},{2,10},{4,12},{6,14},{8,0},{10,2},{12,4},{14,6},{1,9},{3,11}... | collective-permute-start | bytes 202760 | tf_op jit(solution)/shard_map/ppermute | solution.py:85
  6.7 4.8 %collective-permute-start.2 = (bf16[8,4224]{1,0:T(8,128)(2,1)S(1)}, bf16[8,4224]{1,0:T(8,128)(2,1)S(1)}, u32[]{:S(2)}, u32[]{:S(2)}) collective-permute-start(bf16[8,4224]{1,0:T(8,128)(2,1)S(1)} %shard_map.66.refs_0_), channel_id=1, source_target_pairs={{0,12},{2,14},{4,0},{6,2},{8,4},{10,6},{12,8},{14,10},{1,13},{3,15... | collective-permute-start | bytes 202760 | tf_op jit(solution)/shard_map/ppermute | solution.py:85
  11.5 4.2 %collective-permute-start.3 = (bf16[32,4224]{1,0:T(8,128)(2,1)S(1)}, bf16[32,4224]{1,0:T(8,128)(2,1)S(1)}, u32[]{:S(2)}, u32[]{:S(2)}) collective-permute-start(bf16[32,4224]{1,0:T(8,128)(2,1)S(1)} %shard_map.67.mine_ref), channel_id=1, source_target_pairs={{0,2},{2,0},{4,6},{6,4},{8,10},{10,8},{12,14},{14,12},{1,3},{3,1},... | collective-permute-start | bytes 811016 | tf_op jit(solution)/shard_map/ppermute | solution.py:90
  11.6 8.9 %collective-permute-start.4 = (bf16[32,4224]{1,0:T(8,128)(2,1)S(1)}, bf16[32,4224]{1,0:T(8,128)(2,1)S(1)}, u32[]{:S(2)}, u32[]{:S(2)}) collective-permute-start(bf16[32,4224]{1,0:T(8,128)(2,1)S(1)} %shard_map.67.mine_ref), channel_id=1, source_target_pairs={{0,1},{1,0},{2,3},{3,2},{4,5},{5,4},{6,7},{7,6},{8,9},{9,8},{10,11... | collective-permute-start | bytes 811016 | tf_op jit(solution)/shard_map/ppermute | solution.py:90
  20.5 1.6 %collective-permute-start.5 = (bf16[32,4224]{1,0:T(8,128)(2,1)S(1)}, bf16[32,4224]{1,0:T(8,128)(2,1)S(1)}, u32[]{:S(2)}, u32[]{:S(2)}) collective-permute-start(bf16[32,4224]{1,0:T(8,128)(2,1)S(1)} %collective-permute-done.4.mine_ref), channel_id=1, source_target_pairs={{0,2},{2,0},{4,6},{6,4},{8,10},{10,8},{12,14},{14,12},{1,3},{3,1},... | collective-permute-start | bytes 811016 | tf_op jit(solution)/shard_map/ppermute | solution.py:90
  20.5 7.9 %collective-permute-start.6 = (bf16[2,64,768]{2,1,0:T(8,128)(2,1)S(1)}, bf16[2,64,768]{2,1,0:T(8,128)(2,1)S(1)}, u32[]{:S(2)}, u32[]{:S(2)}) collective-permute-start(bf16[2,64,768]{2,1,0:T(8,128)(2,1)S(1)} %get-tuple-element.25.refs_0_.refs_2_.refs_6_.refs_8_.refs_12_), channel_id=1, source_target_pairs={{0,1},{1,0},{2,3},{3,2},{4,5},{5,4},{6,7},{7,6},{8,9},{9,8},{10,11... | collective-permute-start | bytes 589832 | tf_op jit(solution)/shard_map/ppermute | solution.py:90
  24.2 5.7 %collective-permute-start.8 = (bf16[1,64,768]{2,1,0:T(8,128)(2,1)S(1)}, bf16[1,64,768]{2,1,0:T(8,128)(2,1)S(1)}, u32[]{:S(2)}, u32[]{:S(2)}) collective-permute-start(bf16[1,64,768]{2,1,0:T(8,128)(2,1)S(1)} %get-tuple-element.31.refs_1_.refs_3_.refs_13_), channel_id=1, source_target_pairs={{0,1},{1,0},{2,3},{3,2},{4,5},{5,4},{6,7},{7,6},{8,9},{9,8},{10,11... | collective-permute-start | bytes 294920 | tf_op jit(solution)/shard_map/ppermute | solution.py:90
  27.8 5.5 %collective-permute-start.7 = (bf16[1,64,768]{2,1,0:T(8,128)(2,1)S(1)}, bf16[1,64,768]{2,1,0:T(8,128)(2,1)S(1)}, u32[]{:S(2)}, u32[]{:S(2)}) collective-permute-start(bf16[1,64,768]{2,1,0:T(8,128)(2,1)S(1)} %get-tuple-element.28.refs_7_.refs_9_.refs_1_), channel_id=1, source_target_pairs={{0,1},{1,0},{2,3},{3,2},{4,5},{5,4},{6,7},{7,6},{8,9},{9,8},{10,11... | collective-permute-start | bytes 294920 | tf_op jit(solution)/shard_map/ppermute | solution.py:90

commit v4 on v3

--- a/solution.py
+++ b/solution.py
@@ -9,7 +9,8 @@
 
 TOP = 8
 LANES = 128
-HIDDEN_BLOCK = 128
+NEAR_BLOCK = 768
+FAR_BLOCK = 128
 F32 = jnp.float32
 BF16 = jnp.bfloat16
 
@@ -109,24 +110,23 @@
     )(rows, ids)
 
 
-def join_kernel(done_ref, *refs):
-    del done_ref
-    parts = [ref[...].astype(F32) for ref in refs[:-1]]
+def join_kernel(count, *refs):
+    parts = [ref[...].astype(F32) for ref in refs[:count]]
     refs[-1][...] = jnp.concatenate(parts).astype(BF16)
 
 
-def join(done, parts):
+def join(parts, after):
     rows = sum(part.shape[0] for part in parts)
     return pl.pallas_call(
-        join_kernel,
-        in_specs=[pl.BlockSpec(memory_space=pltpu.VMEM)] * (1 + len(parts)),
+        functools.partial(join_kernel, len(parts)),
+        in_specs=[pl.BlockSpec(memory_space=pltpu.VMEM)] * (len(parts) + len(after)),
         out_specs=pl.BlockSpec(memory_space=pltpu.VMEM),
         out_shape=jax.ShapeDtypeStruct((rows, parts[0].shape[1]), BF16),
         compiler_params=pltpu.CompilerParams(vmem_limit_bytes=1 << 20),
         cost_estimate=pl.CostEstimate(
             flops=0, bytes_accessed=4 * rows * parts[0].shape[1], transcendentals=0
         ),
-    )(done, *parts)
+    )(*parts, *after)
 
 
 def weights_kernel(codes_ref, scale_ref, *refs):
@@ -151,7 +151,7 @@
         in_specs=[pl.BlockSpec(memory_space=pltpu.VMEM)] * 2,
         out_specs=[pl.BlockSpec(memory_space=pltpu.VMEM)] * (owned + 1),
         out_shape=[pltpu.VMEM(codes.shape[1:], BF16)] * owned
-        + [jax.ShapeDtypeStruct((8, LANES), F32)],
+        + [jax.ShapeDtypeStruct((32, LANES), F32)],
         compiler_params=pltpu.CompilerParams(vmem_limit_bytes=1 << 20),
         cost_estimate=pl.CostEstimate(
             flops=1 << 33, bytes_accessed=4 * codes.size, transcendentals=0
@@ -159,45 +159,98 @@
     )(codes, scales)
 
 
-def hidden_kernel(owned, experts, done_ref, mine_ref, theirs_ref, *refs):
-    del done_ref
-    w_refs, h_ref, count_ref = refs[:-2], refs[-2], refs[-1]
-    depth, width = w_refs[0].shape
-    block = HIDDEN_BLOCK if width % HIDDEN_BLOCK == 0 else width
+def finish(owned, expert, named, gate, up, h_ref, at, cols):
+    which = lax.axis_index("expert") * owned + expert
+    member = jnp.sum((named == which.astype(F32)).astype(F32), axis=1, keepdims=True)
+    value = gate / (1.0 + jnp.exp(-gate)) * up
+    h_ref[at, :, cols] = jnp.where(member > 0, value, 0.0).astype(BF16)
+    return jnp.sum(member, keepdims=True)
+
+
+def near_kernel(owned, mine_ref, theirs_ref, codes_ref, scale_ref, *refs):
+    gate_refs, h_ref, count_ref = refs[:owned], refs[owned], refs[owned + 1]
+    up_refs, x_ref = refs[-owned - 1 : -1], refs[-1]
+    _, depth, width = codes_ref.shape
+    groups = scale_ref.shape[1]
+    step = depth // groups
+    several = 2 if groups % 2 == 0 else 1
     labelled = jnp.concatenate([mine_ref[...], theirs_ref[...]])
     named = labelled[:, depth:].astype(F32)
-    x = labelled[:, :depth]
-    for at, expert in enumerate(experts):
-        which = lax.axis_index("expert") * owned + expert
-        member = jnp.sum((named == which.astype(F32)).astype(F32), axis=1, keepdims=True)
-        count_ref[at] = jnp.broadcast_to(jnp.sum(member, keepdims=True), count_ref.shape[1:])
+    x_ref[...] = labelled[:, :depth]
+    block = NEAR_BLOCK if width % NEAR_BLOCK == 0 else width
+    for expert in range(owned):
         for col in range(0, width, block):
             cols = pl.ds(col, block)
-            gate = jnp.dot(x, w_refs[2 * at][:, cols], preferred_element_type=F32)
-            up = jnp.dot(x, w_refs[2 * at + 1][:, cols], preferred_element_type=F32)
-            value = gate / (1.0 + jnp.exp(-gate)) * up
-            h_ref[at, :, cols] = jnp.where(member > 0, value, 0.0).astype(BF16)
-
-
-def hidden_units(owned, experts, done, x, w):
-    depth, width = w[0][0].shape
-    flat = [w[e][i] for e in experts for i in range(2)]
+            gate = jnp.dot(x_ref[...], gate_refs[expert][:, cols], preferred_element_type=F32)
+            up = jnp.zeros(gate.shape, F32)
+            for group in range(0, groups, several):
+                part = pl.ds(group * step, several * step)
+                codes = codes_ref[expert, part, cols].astype(F32).reshape(several, step, block)
+                scale = scale_ref[expert, pl.ds(group, several), cols]
+                w = (codes * scale[:, None, :]).astype(BF16).reshape(several * step, block)
+                up_refs[expert][part, cols] = w
+                up = up + jnp.dot(
+                    x_ref[:, pl.ds(group * step, several * step)], w, preferred_element_type=F32
+                )
+            count = finish(owned, expert, named, gate, up, h_ref, expert, cols)
+        count_ref[expert] = jnp.broadcast_to(count, count_ref.shape[1:])
+
+
+def near_units(x, w_gate, up_codes, up_scales):
+    owned, depth, width = up_codes.shape
     rows = sum(part.shape[0] for part in x)
     return pl.pallas_call(
-        functools.partial(hidden_kernel, owned, experts),
-        in_specs=[pl.BlockSpec(memory_space=pltpu.VMEM)] * (3 + len(flat)),
+        functools.partial(near_kernel, owned),
+        in_specs=[pl.BlockSpec(memory_space=pltpu.VMEM)] * (4 + owned),
+        out_specs=[pl.BlockSpec(memory_space=pltpu.VMEM)] * (2 + owned),
+        out_shape=[
+            jax.ShapeDtypeStruct((owned, rows, width), BF16),
+            jax.ShapeDtypeStruct((owned, 32, LANES), F32),
+        ]
+        + [pltpu.VMEM((depth, width), BF16)] * owned,
+        scratch_shapes=[pltpu.VMEM((rows, depth), BF16)],
+        compiler_params=pltpu.CompilerParams(vmem_limit_bytes=2 << 20),
+        cost_estimate=pl.CostEstimate(
+            flops=1 << 33, bytes_accessed=4 * owned * depth * width, transcendentals=0
+        ),
+    )(*x, up_codes, up_scales, *w_gate)
+
+
+def far_kernel(
+    owned, expert, mine_ref, theirs_ref, gate_ref, up_ref, h_ref, count_ref, x_ref
+):
+    depth, width = gate_ref.shape
+    labelled = jnp.concatenate([mine_ref[...], theirs_ref[...]])
+    named = labelled[:, depth:].astype(F32)
+    x_ref[...] = labelled[:, :depth]
+    block = FAR_BLOCK if width % FAR_BLOCK == 0 else width
+    for col in range(0, width, block):
+        cols = pl.ds(col, block)
+        gate = jnp.dot(x_ref[...], gate_ref[:, cols], preferred_element_type=F32)
+        up = jnp.dot(x_ref[...], up_ref[:, cols], preferred_element_type=F32)
+        count = finish(owned, expert, named, gate, up, h_ref, 0, cols)
+    count_ref[0] = jnp.broadcast_to(count, count_ref.shape[1:])
+
+
+def far_units(owned, expert, x, gate, up):
+    depth, width = gate.shape
+    rows = sum(part.shape[0] for part in x)
+    return pl.pallas_call(
+        functools.partial(far_kernel, owned, expert),
+        in_specs=[pl.BlockSpec(memory_space=pltpu.VMEM)] * 4,
         out_specs=[pl.BlockSpec(memory_space=pltpu.VMEM)] * 2,
         out_shape=[
-            jax.ShapeDtypeStruct((len(experts), rows, width), BF16),
-            jax.ShapeDtypeStruct((len(experts), 8, LANES), F32),
+            jax.ShapeDtypeStruct((1, rows, width), BF16),
+            jax.ShapeDtypeStruct((1, 32, LANES), F32),
         ],
-        compiler_params=pltpu.CompilerParams(vmem_limit_bytes=4 << 20),
-        cost_estimate=pl.CostEstimate(
-            flops=4 * len(experts) * rows * depth * width,
-            bytes_accessed=4 * len(experts) * depth * width,
-            transcendentals=len(experts) * rows * width,
-        ),
-    )(done, *x, *flat)
+        scratch_shapes=[pltpu.VMEM((rows, depth), BF16)],
+        compiler_params=pltpu.CompilerParams(vmem_limit_bytes=2 << 20),
+        cost_estimate=pl.CostEstimate(
+            flops=4 * rows * depth * width,
+            bytes_accessed=4 * depth * width,
+            transcendentals=rows * width,
+        ),
+    )(*x, gate, up)
 
 
 def gram_kernel(jobs, *refs):
@@ -265,16 +318,16 @@
     every = tuple(range(owned))
     rows = label(tokens, expert_ids, 1 << 34)
     *w_gate, gate_done = weights(gate_codes, gate_scales)
-    near = join(gate_done, [rows] + [shift(rows, "expert", by) for by in range(2, owners, 2)])
-    far = swap(near, "dp")
-    *w_up, up_done = weights(up_codes, up_scales)
-    w = list(zip(w_gate, w_up))
+    far_own = swap(rows, "dp")
+    ring = [shift(rows, "expert", by) for by in range(2, owners, 2)]
+    near = join([rows] + ring, [far_own, gate_done])
+    far_ring = swap(join(ring, [gate_done]), "dp")
     near = (near, swap(near, "expert"))
-    near_hidden, near_count = hidden_units(owned, every, up_done, near, w)
-    far, near_count = lax.optimization_barrier((far, near_count))
+    near_hidden, near_count, *w_up = near_units(near, w_gate, up_codes, up_scales)
+    far = join([far_own, far_ring], [near_count])
     far = (far, swap(far, "expert"))
     near_other = swap(near_hidden, "dp")
-    far_parts = [hidden_units(owned, (e,), up_done, far, w) for e in every]
+    far_parts = [far_units(owned, e, far, w_gate[e], w_up[e]) for e in every]
     far_other = [swap(hidden, "dp") for hidden, _ in far_parts]
     shape = (owned, width, 2 * width)
     own, other = [], []
@@ -282,10 +335,10 @@
         hidden, count = far_parts[e]
         own.append((near_hidden, hidden, near_hidden, hidden, near_count, count))
         other.append((near_hidden, hidden, near_other, far_other[e], near_count, count))
-    last = owned - 1
-    jobs = [(e, e, 0, False) for e in every] + [(e, e, 0, True) for e in range(last)]
-    out = gram_blocks(jobs, own + other[:last], shape)
-    return gram_blocks([(last, last, 0, True)], other[last:], shape, out)
+    out = gram_blocks([(e, e, 0, False) for e in every], own, shape)
+    for e in every:
+        out = gram_blocks([(e, e, 0, True)], other[e : e + 1], shape, out)
+    return out
 
 
 def local(tokens, expert_ids, gate_codes, up_codes, gate_scales, up_scales):

time: 35.3 us -> 34 us (0.963)
  Pallas kernels: 19.1 us -> 17.4 us
  starting transfers between devices: 12.5 us -> 13.9 us
  waiting for transfers between devices: 3.42 us -> 2.34 us
    pallas_call x2 -> x1, Pallas kernels: 4.92 us -> 2.46 us  [weights(): pl.pallas_call(weights_kernel, in_specs=[pl.BlockSpec(memory_space=pltpu....]
    ppermute x6 -> x7, starting transfers between devices: 5.47 us -> 6.9 us  [swap(): return lax.ppermute(x, axis, [(i, i ^ 1) for i in range(n)])]
    pallas_call x2 -> x3, Pallas kernels: 5.2 us -> 6.26 us  [gram_blocks(): pl.pallas_call(functools.partial(gram_kernel, jobs), in_specs=[pl.BlockSp...]
    ppermute x3, waiting for transfers between devices: 0.96 us -> 0.01 us  [shift(): return lax.ppermute(x, axis, [(i, (i + by) % n) for i in range(n)])]
    pallas_call x4 -> x6, Pallas kernels: 7.98 us -> 7.66 us  [the longest x1 3.87 us: near_units(): pl.pallas_call(functools.partial(near_kernel, owned), in_specs=[pl.BlockS...]
    ppermute x6 -> x7, waiting for transfers between devices: 2.46 us -> 2.33 us  [swap(): return lax.ppermute(x, axis, [(i, i ^ 1) for i in range(n)])]
  transfers between devices with their start and end apart: 9 -> 10, of which waited for: 4 -> 2; matrix products, arithmetic and copies ran while one was open for 0% -> 0% of each run, Pallas kernels for 46% -> 43%
where the time goes in v4:
time: 34 us; the launch traced here: 33.8 us
  Pallas kernels  17.4 us (51%)
  starting transfers between devices  13.9 us (41%)
  waiting for transfers between devices  2.34 us (7%)
    ppermute x3, starting transfers between devices, shift(): return lax.ppermute(x, axis, [(i, (i + by) % n) for i in range(n)])  7.03 us
    ppermute x7, starting transfers between devices, swap(): return lax.ppermute(x, axis, [(i, i ^ 1) for i in range(n)])  6.9 us
    pallas_call x3, Pallas kernels, gram_blocks(): pl.pallas_call(functools.partial(gram_kernel, jobs), in_specs=[pl.BlockSp...  6.26 us
    pallas_call x1, Pallas kernels, near_units(): pl.pallas_call(functools.partial(near_kernel, owned), in_specs=[pl.BlockS...  3.87 us
    pallas_call x2, Pallas kernels, far_units(): pl.pallas_call(functools.partial(far_kernel, owned, expert), in_specs=[pl...  3.74 us
    pallas_call x1, Pallas kernels, weights(): pl.pallas_call(weights_kernel, in_specs=[pl.BlockSpec(memory_space=pltpu....  2.46 us
    ppermute x7, waiting for transfers between devices, swap(): return lax.ppermute(x, axis, [(i, i ^ 1) for i in range(n)])  2.33 us
    pallas_call x1, Pallas kernels, label(): pl.pallas_call(label_kernel, out_shape=jax.ShapeDtypeStruct((rows.shape[0...  1 us
  transfers between devices with their start and end apart: 10, of which 2 were waited for; matrix products, arithmetic and copies ran while one was open for 0% of the time, Pallas kernels for 43%

profile of v4, /device:TPU:0, one launch (start us, length us, event | category | flops | bytes accessed | tf_op | source)
XLA Modules:
  0.0 33.8 jit_solution(4272218617075838292)
XLA Ops:
  0.0 1.0 %shard_map.64.refs_0_ = bf16[8,4224]{1,0:T(8,128)(2,1)S(1)} custom-call(bf16[8,4096]{1,0:T(8,128)(2,1)} %rows_ref.1, s32[8,8]{1,0:T(8,128)} %ids_ref.1), custom_call_target="tpu_custom_call" | custom-call | flops 17179869184 | bytes 1048576 | tf_op jit(solution)/shard_map/pallas_call | solution.py:105
  1.0 0.0 copy-start.2
  1.0 3.1 %collective-permute-start = (bf16[8,4224]{1,0:T(8,128)(2,1)S(1)}, bf16[8,4224]{1,0:T(8,128)(2,1)S(1)}, u32[]{:S(2)}, u32[]{:S(2)}) collective-permute-start(bf16[8,4224]{1,0:T(8,128)(2,1)S(1)} %shard_map.64.refs_0_), channel_id=1, source_target_pairs={{0,4},{2,6},{4,8},{6,10},{8,12},{10,14},{12,0},{14,2},{1,5},{3,7},... | collective-permute-start | bytes 202760 | tf_op jit(solution)/shard_map/ppermute | solution.py:86
  4.1 2.6 %collective-permute-start.1 = (bf16[8,4224]{1,0:T(8,128)(2,1)S(1)}, bf16[8,4224]{1,0:T(8,128)(2,1)S(1)}, u32[]{:S(2)}, u32[]{:S(2)}) collective-permute-start(bf16[8,4224]{1,0:T(8,128)(2,1)S(1)} %shard_map.64.refs_0_), channel_id=1, source_target_pairs={{0,8},{2,10},{4,12},{6,14},{8,0},{10,2},{12,4},{14,6},{1,9},{3,11}... | collective-permute-start | bytes 202760 | tf_op jit(solution)/shard_map/ppermute | solution.py:86
  6.7 1.3 %collective-permute-start.2 = (bf16[8,4224]{1,0:T(8,128)(2,1)S(1)}, bf16[8,4224]{1,0:T(8,128)(2,1)S(1)}, u32[]{:S(2)}, u32[]{:S(2)}) collective-permute-start(bf16[8,4224]{1,0:T(8,128)(2,1)S(1)} %shard_map.64.refs_0_), channel_id=1, source_target_pairs={{0,12},{2,14},{4,0},{6,2},{8,4},{10,6},{12,8},{14,10},{1,13},{3,15... | collective-permute-start | bytes 202760 | tf_op jit(solution)/shard_map/ppermute | solution.py:86
  8.1 1.5 %collective-permute-start.3 = (bf16[8,4224]{1,0:T(8,128)(2,1)S(1)}, bf16[8,4224]{1,0:T(8,128)(2,1)S(1)}, u32[]{:S(2)}, u32[]{:S(2)}) collective-permute-start(bf16[8,4224]{1,0:T(8,128)(2,1)S(1)} %shard_map.64.refs_0_), channel_id=1, source_target_pairs={{0,1},{1,0},{2,3},{3,2},{4,5},{5,4},{6,7},{7,6},{8,9},{9,8},{10,11... | collective-permute-start | bytes 202760 | tf_op jit(solution)/shard_map/ppermute | solution.py:91
  9.5 0.0 copy-done.1
  9.6 0.0 copy-done
  9.6 2.5 %shard_map.65 = (bf16[4096,768]{1,0:T(8,128)(2,1)S(1)}, bf16[4096,768]{1,0:T(8,128)(2,1)S(1)}, f32[32,128]{1,0:T(8,128)S(1)}) custom-call(bf16[2,4096,768]{2,1,0:T(8,128)(2,1)S(1)} %copy-done, f32[2,32,768]{2,1,0:T(8,128)S(1)} %copy-done.1), custom_call_target="tpu_custom_call" | custom-call | flops 8589934592 | bytes 25165824 | tf_op jit(solution)/shard_map/pallas_call | solution.py:149
  12.0 0.0 collective-permute-done.refs_1_.refs_0_
  12.0 0.0 collective-permute-done.1.refs_2_.refs_1_
  12.0 0.0 collective-permute-done.2.refs_3_.refs_2_
  12.0 0.3 collective-permute-done.3.refs_4_.refs_0_
  12.4 0.1 collective-permute-start.4
  12.5 1.6 %collective-permute-start.5 = (bf16[24,4224]{1,0:T(8,128)(2,1)S(1)}, bf16[24,4224]{1,0:T(8,128)(2,1)S(1)}, u32[]{:S(2)}, u32[]{:S(2)}) collective-permute-start(bf16[24,4224]{1,0:T(8,128)(2,1)S(1)} %shard_map.68), channel_id=1, source_target_pairs={{0,1},{1,0},{2,3},{3,2},{4,5},{5,4},{6,7},{7,6},{8,9},{9,8},{10,11... | collective-permute-start | bytes 608264 | tf_op jit(solution)/shard_map/ppermute | solution.py:91
  14.0 0.0 collective-permute-done.4.theirs_ref
  14.0 0.0 slice-done
  14.1 3.9 %shard_map.67 = (bf16[2,64,768]{2,1,0:T(8,128)(2,1)S(1)}, f32[2,32,128]{2,1,0:T(8,128)S(1)}, bf16[4096,768]{1,0:T(8,128)(2,1)S(1)}, bf16[4096,768]{1,0:T(8,128)(2,1)S(1)}) custom-call(bf16[32,4224]{1,0:T(8,128)(2,1)S(1)} %shard_map.66.mine_ref, bf16[32,4224]{1,0:T(8,128)(2,1)S(1)} %collective-permute-done.4.theirs_ref, bf16[2,4096,768]{2,1,0:T(8,128)(2,1)S(1)} %bitcast.1, ...), custom_call_target="tpu_custom_call" | custom-call | flops 8589934592 | bytes 25165824 | tf_op jit(solution)/shard_map/pallas_call | solution.py:202
  17.9 2.0 %collective-permute-done.5.refs_1_ = bf16[24,4224]{1,0:T(8,128)(2,1)S(1)} collective-permute-done((bf16[24,4224]{1,0:T(8,128)(2,1)S(1)}, bf16[24,4224]{1,0:T(8,128)(2,1)S(1)}, u32[]{:S(2)}, u32[]{:S(2)}) %collective-permute-start.5) | collective-permute-done | bytes 202784 | tf_op jit(solution)/shard_map/ppermute | solution.py:91
  20.0 0.1 collective-permute-start.6
  20.1 1.6 %collective-permute-start.7 = (bf16[2,64,768]{2,1,0:T(8,128)(2,1)S(1)}, bf16[2,64,768]{2,1,0:T(8,128)(2,1)S(1)}, u32[]{:S(2)}, u32[]{:S(2)}) collective-permute-start(bf16[2,64,768]{2,1,0:T(8,128)(2,1)S(1)} %get-tuple-element.19.refs_0_.refs_2_.refs_6_.refs_8_), channel_id=1, source_target_pairs={{0,1},{1,0},{2,3},{3,2},{4,5},{5,4},{6,7},{7,6},{8,9},{9,8},{10,11... | collective-permute-start | bytes 589832 | tf_op jit(solution)/shard_map/ppermute | solution.py:91
  21.6 0.0 collective-permute-done.6.theirs_ref
  21.6 1.9 %shard_map.71 = (bf16[1,64,768]{2,1,0:T(8,128)(2,1)S(1)}, f32[1,32,128]{2,1,0:T(8,128)S(1)}) custom-call(bf16[32,4224]{1,0:T(8,128)(2,1)S(1)} %shard_map.69.mine_ref, bf16[32,4224]{1,0:T(8,128)(2,1)S(1)} %collective-permute-done.6.theirs_ref, bf16[4096,768]{1,0:T(8,128)(2,1)S(1)} %get-tuple-element.17.refs_0_.gate_ref, ...), custom_call_target="tpu_custom_call" | custom-call | flops 805306368 | bytes 12582912 | tf_op jit(solution)/shard_map/pallas_call | solution.py:238
  23.5 1.5 %collective-permute-start.9 = (bf16[1,64,768]{2,1,0:T(8,128)(2,1)S(1)}, bf16[1,64,768]{2,1,0:T(8,128)(2,1)S(1)}, u32[]{:S(2)}, u32[]{:S(2)}) collective-permute-start(bf16[1,64,768]{2,1,0:T(8,128)(2,1)S(1)} %get-tuple-element.25.refs_1_.refs_3_), channel_id=1, source_target_pairs={{0,1},{1,0},{2,3},{3,2},{4,5},{5,4},{6,7},{7,6},{8,9},{9,8},{10,11... | collective-permute-start | bytes 294920 | tf_op jit(solution)/shard_map/ppermute | solution.py:91
  25.0 1.9 %shard_map.70 = (bf16[1,64,768]{2,1,0:T(8,128)(2,1)S(1)}, f32[1,32,128]{2,1,0:T(8,128)S(1)}) custom-call(bf16[32,4224]{1,0:T(8,128)(2,1)S(1)} %shard_map.69.mine_ref, bf16[32,4224]{1,0:T(8,128)(2,1)S(1)} %collective-permute-done.6.theirs_ref, bf16[4096,768]{1,0:T(8,128)(2,1)S(1)} %get-tuple-element.18.refs_1_.gate_ref, ...), custom_call_target="tpu_custom_call" | custom-call | flops 805306368 | bytes 12582912 | tf_op jit(solution)/shard_map/pallas_call | solution.py:238
  26.9 0.6 %collective-permute-start.8 = (bf16[1,64,768]{2,1,0:T(8,128)(2,1)S(1)}, bf16[1,64,768]{2,1,0:T(8,128)(2,1)S(1)}, u32[]{:S(2)}, u32[]{:S(2)}) collective-permute-start(bf16[1,64,768]{2,1,0:T(8,128)(2,1)S(1)} %get-tuple-element.22.refs_7_.refs_9_.refs_1_), channel_id=1, source_target_pairs={{0,1},{1,0},{2,3},{3,2},{4,5},{5,4},{6,7},{7,6},{8,9},{9,8},{10,11... | collective-permute-start | bytes 294920 | tf_op jit(solution)/shard_map/ppermute | solution.py:91
  27.5 2.6 %shard_map.72.refs_6_ = f32[2,768,1536]{2,1,0:T(8,128)} custom-call(bf16[2,64,768]{2,1,0:T(8,128)(2,1)S(1)} %get-tuple-element.19.refs_0_.refs_2_.refs_6_.refs_8_, bf16[1,64,768]{2,1,0:T(8,128)(2,1)S(1)} %get-tuple-element.25.refs_1_.refs_3_, bf16[2,64,768]{2,1,0:T(8,128)(2,1)S(1)} %get-tuple-element.19.refs_0_.refs_2_.refs_6_.refs_8_, ...), custom_call_target="tpu_custom_call" | custom-call | flops 301989888 | bytes 4718592 | tf_op jit(solution)/shard_map/pallas_call | solution.py:295
  30.1 0.0 collective-permute-done.7.refs_2_
  30.2 0.0 collective-permute-done.9.refs_3_
  30.2 1.8 %shard_map.73.refs_6_ = f32[2,768,1536]{2,1,0:T(8,128)} custom-call(bf16[2,64,768]{2,1,0:T(8,128)(2,1)S(1)} %get-tuple-element.19.refs_0_.refs_2_.refs_6_.refs_8_, bf16[1,64,768]{2,1,0:T(8,128)(2,1)S(1)} %get-tuple-element.25.refs_1_.refs_3_, bf16[2,64,768]{2,1,0:T(8,128)(2,1)S(1)} %collective-permute-done.7.refs_2_, ...), custom_call_target="tpu_custom_call", output_to_operand_aliasing={{}: (6, {})} | custom-call | flops 150994944 | bytes 2359296 | tf_op jit(solution)/shard_map/pallas_call | solution.py:295
  32.0 0.0 collective-permute-done.8.refs_3_
  32.0 1.8 %shard_map.74 = f32[2,768,1536]{2,1,0:T(8,128)} custom-call(bf16[2,64,768]{2,1,0:T(8,128)(2,1)S(1)} %get-tuple-element.19.refs_0_.refs_2_.refs_6_.refs_8_, bf16[1,64,768]{2,1,0:T(8,128)(2,1)S(1)} %get-tuple-element.22.refs_7_.refs_9_.refs_1_, bf16[2,64,768]{2,1,0:T(8,128)(2,1)S(1)} %collective-permute-done.7.refs_2_, ...), custom_call_target="tpu_custom_call", output_to_operand_aliasing={{}: (6, {})} | custom-call | flops 150994944 | bytes 2359296 | tf_op jit(solution)/shard_map/pallas_call | solution.py:295
  (12 shorter events, 0.1 us)
Async XLA Ops:
  0.0 9.6 %copy-start.1 = (f32[2,32,768]{2,1,0:T(8,128)S(1)}, f32[2,32,768]{2,1,0:T(8,128)}, u32[]{:S(2)}) copy-start(f32[2,32,768]{2,1,0:T(8,128)} %scale_ref.2) | copy-start | bytes 589828
  0.0 9.6 %copy-start = (bf16[2,4096,768]{2,1,0:T(8,128)(2,1)S(1)}, bf16[2,4096,768]{2,1,0:T(8,128)(2,1)}, u32[]{:S(2)}) copy-start(bf16[2,4096,768]{2,1,0:T(8,128)(2,1)} %codes_ref.2) | copy-start | bytes 37748740
  0.0 14.0 %slice-start = ((s8[12582912]{0:T(1024)(128)(4,1)}), s8[4194304]{0:T(1024)(128)(4,1)S(1)}, s32[]{:S(2)}) async-start(s8[12582912]{0:T(1024)(128)(4,1)} %bitcast), calls=%async_computation | async-start | bytes 8388608
  0.0 14.0 %slice-start.1 = ((s8[12582912]{0:T(1024)(128)(4,1)}), s8[4194304]{0:T(1024)(128)(4,1)S(1)}, s32[]{:S(2)}) async-start(s8[12582912]{0:T(1024)(128)(4,1)} %bitcast), calls=%async_computation.1 | async-start | bytes 8388608
  1.0 13.0 %slice-start.2 = ((s8[12582912]{0:T(1024)(128)(4,1)}), s8[4194304]{0:T(1024)(128)(4,1)S(1)}, s32[]{:S(2)}) async-start(s8[12582912]{0:T(1024)(128)(4,1)} %bitcast), calls=%async_computation.2 | async-start | bytes 8388608
  1.0 13.0 %copy-start.2 = (f32[2,32,768]{2,1,0:T(8,128)S(1)}, f32[2,32,768]{2,1,0:T(8,128)}, u32[]{:S(2)}) copy-start(f32[2,32,768]{2,1,0:T(8,128)} %scale_ref.3) | copy-start | bytes 589828
  1.0 11.0 %collective-permute-start = (bf16[8,4224]{1,0:T(8,128)(2,1)S(1)}, bf16[8,4224]{1,0:T(8,128)(2,1)S(1)}, u32[]{:S(2)}, u32[]{:S(2)}) collective-permute-start(bf16[8,4224]{1,0:T(8,128)(2,1)S(1)} %shard_map.64.refs_0_), channel_id=1, source_target_pairs={{0,4},{2,6},{4,8},{6,10},{8,12},{10,14},{12,0},{14,2},{1,5},{3,7},... | collective-permute-start | bytes 202760 | tf_op jit(solution)/shard_map/ppermute | solution.py:86
  4.1 7.9 %collective-permute-start.1 = (bf16[8,4224]{1,0:T(8,128)(2,1)S(1)}, bf16[8,4224]{1,0:T(8,128)(2,1)S(1)}, u32[]{:S(2)}, u32[]{:S(2)}) collective-permute-start(bf16[8,4224]{1,0:T(8,128)(2,1)S(1)} %shard_map.64.refs_0_), channel_id=1, source_target_pairs={{0,8},{2,10},{4,12},{6,14},{8,0},{10,2},{12,4},{14,6},{1,9},{3,11}... | collective-permute-start | bytes 202760 | tf_op jit(solution)/shard_map/ppermute | solution.py:86
  6.7 5.3 %collective-permute-start.2 = (bf16[8,4224]{1,0:T(8,128)(2,1)S(1)}, bf16[8,4224]{1,0:T(8,128)(2,1)S(1)}, u32[]{:S(2)}, u32[]{:S(2)}) collective-permute-start(bf16[8,4224]{1,0:T(8,128)(2,1)S(1)} %shard_map.64.refs_0_), channel_id=1, source_target_pairs={{0,12},{2,14},{4,0},{6,2},{8,4},{10,6},{12,8},{14,10},{1,13},{3,15... | collective-permute-start | bytes 202760 | tf_op jit(solution)/shard_map/ppermute | solution.py:86
  8.1 4.3 %collective-permute-start.3 = (bf16[8,4224]{1,0:T(8,128)(2,1)S(1)}, bf16[8,4224]{1,0:T(8,128)(2,1)S(1)}, u32[]{:S(2)}, u32[]{:S(2)}) collective-permute-start(bf16[8,4224]{1,0:T(8,128)(2,1)S(1)} %shard_map.64.refs_0_), channel_id=1, source_target_pairs={{0,1},{1,0},{2,3},{3,2},{4,5},{5,4},{6,7},{7,6},{8,9},{9,8},{10,11... | collective-permute-start | bytes 202760 | tf_op jit(solution)/shard_map/ppermute | solution.py:91
  12.4 1.7 %collective-permute-start.4 = (bf16[32,4224]{1,0:T(8,128)(2,1)S(1)}, bf16[32,4224]{1,0:T(8,128)(2,1)S(1)}, u32[]{:S(2)}, u32[]{:S(2)}) collective-permute-start(bf16[32,4224]{1,0:T(8,128)(2,1)S(1)} %shard_map.66.mine_ref), channel_id=1, source_target_pairs={{0,2},{2,0},{4,6},{6,4},{8,10},{10,8},{12,14},{14,12},{1,3},{3,1},... | collective-permute-start | bytes 811016 | tf_op jit(solution)/shard_map/ppermute | solution.py:91
  12.5 7.5 %collective-permute-start.5 = (bf16[24,4224]{1,0:T(8,128)(2,1)S(1)}, bf16[24,4224]{1,0:T(8,128)(2,1)S(1)}, u32[]{:S(2)}, u32[]{:S(2)}) collective-permute-start(bf16[24,4224]{1,0:T(8,128)(2,1)S(1)} %shard_map.68), channel_id=1, source_target_pairs={{0,1},{1,0},{2,3},{3,2},{4,5},{5,4},{6,7},{7,6},{8,9},{9,8},{10,11... | collective-permute-start | bytes 608264 | tf_op jit(solution)/shard_map/ppermute | solution.py:91
  20.0 1.6 %collective-permute-start.6 = (bf16[32,4224]{1,0:T(8,128)(2,1)S(1)}, bf16[32,4224]{1,0:T(8,128)(2,1)S(1)}, u32[]{:S(2)}, u32[]{:S(2)}) collective-permute-start(bf16[32,4224]{1,0:T(8,128)(2,1)S(1)} %shard_map.69.mine_ref), channel_id=1, source_target_pairs={{0,2},{2,0},{4,6},{6,4},{8,10},{10,8},{12,14},{14,12},{1,3},{3,1},... | collective-permute-start | bytes 811016 | tf_op jit(solution)/shard_map/ppermute | solution.py:91
  20.1 10.1 %collective-permute-start.7 = (bf16[2,64,768]{2,1,0:T(8,128)(2,1)S(1)}, bf16[2,64,768]{2,1,0:T(8,128)(2,1)S(1)}, u32[]{:S(2)}, u32[]{:S(2)}) collective-permute-start(bf16[2,64,768]{2,1,0:T(8,128)(2,1)S(1)} %get-tuple-element.19.refs_0_.refs_2_.refs_6_.refs_8_), channel_id=1, source_target_pairs={{0,1},{1,0},{2,3},{3,2},{4,5},{5,4},{6,7},{7,6},{8,9},{9,8},{10,11... | collective-permute-start | bytes 589832 | tf_op jit(solution)/shard_map/ppermute | solution.py:91
  23.5 6.7 %collective-permute-start.9 = (bf16[1,64,768]{2,1,0:T(8,128)(2,1)S(1)}, bf16[1,64,768]{2,1,0:T(8,128)(2,1)S(1)}, u32[]{:S(2)}, u32[]{:S(2)}) collective-permute-start(bf16[1,64,768]{2,1,0:T(8,128)(2,1)S(1)} %get-tuple-element.25.refs_1_.refs_3_), channel_id=1, source_target_pairs={{0,1},{1,0},{2,3},{3,2},{4,5},{5,4},{6,7},{7,6},{8,9},{9,8},{10,11... | collective-permute-start | bytes 294920 | tf_op jit(solution)/shard_map/ppermute | solution.py:91
  26.9 5.1 %collective-permute-start.8 = (bf16[1,64,768]{2,1,0:T(8,128)(2,1)S(1)}, bf16[1,64,768]{2,1,0:T(8,128)(2,1)S(1)}, u32[]{:S(2)}, u32[]{:S(2)}) collective-permute-start(bf16[1,64,768]{2,1,0:T(8,128)(2,1)S(1)} %get-tuple-element.22.refs_7_.refs_9_.refs_1_), channel_id=1, source_target_pairs={{0,1},{1,0},{2,3},{3,2},{4,5},{5,4},{6,7},{7,6},{8,9},{9,8},{10,11... | collective-permute-start | bytes 294920 | tf_op jit(solution)/shard_map/ppermute | solution.py:91

commit v5 on v4

--- a/solution.py
+++ b/solution.py
@@ -105,28 +105,36 @@
     return pl.pallas_call(
         label_kernel,
         out_shape=jax.ShapeDtypeStruct((rows.shape[0], rows.shape[1] + LANES), BF16),
-        compiler_params=pltpu.CompilerParams(vmem_limit_bytes=1 << 20),
+        compiler_params=pltpu.CompilerParams(vmem_limit_bytes=2 << 20),
         cost_estimate=pl.CostEstimate(flops=cost, bytes_accessed=1 << 20, transcendentals=0),
     )(rows, ids)
 
 
-def join_kernel(count, *refs):
-    parts = [ref[...].astype(F32) for ref in refs[:count]]
-    refs[-1][...] = jnp.concatenate(parts).astype(BF16)
-
-
-def join(parts, after):
+def join_kernel(order, kept, *refs):
+    outs = refs[len(refs) - 1 - kept :]
+    parts = [refs[at][...].astype(F32) for at in order]
+    outs[0][...] = jnp.concatenate(parts).astype(BF16)
+    if kept:
+        outs[1][...] = refs[len(order)][...]
+
+
+def join(parts, after, order=None, keep=False):
+    order = tuple(range(len(parts))) if order is None else order
     rows = sum(part.shape[0] for part in parts)
-    return pl.pallas_call(
-        functools.partial(join_kernel, len(parts)),
+    shapes = [jax.ShapeDtypeStruct((rows, parts[0].shape[1]), BF16)]
+    if keep:
+        shapes.append(jax.ShapeDtypeStruct(after[0].shape, BF16))
+    made = pl.pallas_call(
+        functools.partial(join_kernel, order, int(keep)),
         in_specs=[pl.BlockSpec(memory_space=pltpu.VMEM)] * (len(parts) + len(after)),
-        out_specs=pl.BlockSpec(memory_space=pltpu.VMEM),
-        out_shape=jax.ShapeDtypeStruct((rows, parts[0].shape[1]), BF16),
-        compiler_params=pltpu.CompilerParams(vmem_limit_bytes=1 << 20),
+        out_specs=[pl.BlockSpec(memory_space=pltpu.VMEM)] * len(shapes),
+        out_shape=shapes,
+        compiler_params=pltpu.CompilerParams(vmem_limit_bytes=2 << 20),
         cost_estimate=pl.CostEstimate(
             flops=0, bytes_accessed=4 * rows * parts[0].shape[1], transcendentals=0
         ),
     )(*parts, *after)
+    return made if keep else made[0]
 
 
 def weights_kernel(codes_ref, scale_ref, *refs):
@@ -152,7 +160,7 @@
         out_specs=[pl.BlockSpec(memory_space=pltpu.VMEM)] * (owned + 1),
         out_shape=[pltpu.VMEM(codes.shape[1:], BF16)] * owned
         + [jax.ShapeDtypeStruct((32, LANES), F32)],
-        compiler_params=pltpu.CompilerParams(vmem_limit_bytes=1 << 20),
+        compiler_params=pltpu.CompilerParams(vmem_limit_bytes=2 << 20),
         cost_estimate=pl.CostEstimate(
             flops=1 << 33, bytes_accessed=4 * codes.size, transcendentals=0
         ),
@@ -303,7 +311,7 @@
             pltpu.VMEM((n, width, width), F32),
             pltpu.SemaphoreType.DMA((n, 2)),
         ],
-        compiler_params=pltpu.CompilerParams(vmem_limit_bytes=12 << 20),
+        compiler_params=pltpu.CompilerParams(vmem_limit_bytes=8 << 20),
         cost_estimate=pl.CostEstimate(
             flops=2 * n * 128 * width * width,
             bytes_accessed=4 * n * width * width,
@@ -320,11 +328,13 @@
     *w_gate, gate_done = weights(gate_codes, gate_scales)
     far_own = swap(rows, "dp")
     ring = [shift(rows, "expert", by) for by in range(2, owners, 2)]
-    near = join([rows] + ring, [far_own, gate_done])
-    far_ring = swap(join(ring, [gate_done]), "dp")
+    order = (0, *range(2, len(ring) + 1), 1)
+    near, far_own = join([rows] + ring, [far_own, gate_done], order, keep=True)
+    far_next = shift(far_own, "expert", 2)
+    far_ring = swap(join(ring[1:], [ring[0], gate_done]), "dp")
     near = (near, swap(near, "expert"))
     near_hidden, near_count, *w_up = near_units(near, w_gate, up_codes, up_scales)
-    far = join([far_own, far_ring], [near_count])
+    far = join([far_own, far_ring, far_next], [near_count])
     far = (far, swap(far, "expert"))
     near_other = swap(near_hidden, "dp")
     far_parts = [far_units(owned, e, far, w_gate[e], w_up[e]) for e in every]

time: 34 us -> 33.3 us (0.979)
  waiting for transfers between devices: 2.34 us -> 0.37 us
  starting transfers between devices: 13.9 us -> 14.8 us
  Pallas kernels: 17.4 us -> 17.8 us
    ppermute x7, waiting for transfers between devices: 2.33 us -> 0.36 us  [swap(): return lax.ppermute(x, axis, [(i, i ^ 1) for i in range(n)])]
    ppermute x3 -> x4, starting transfers between devices: 7.03 us -> 7.93 us  [shift(): return lax.ppermute(x, axis, [(i, (i + by) % n) for i in range(n)])]
  transfers between devices with their start and end apart: 10 -> 11, of which waited for: 2 -> 1; matrix products, arithmetic and copies ran while one was open for 0% -> 0% of each run, Pallas kernels for 43% -> 45%
where the time goes in v5:
time: 33.3 us; the launch traced here: 33.1 us
  Pallas kernels  17.8 us (53%)
  starting transfers between devices  14.8 us (44%)
  waiting for transfers between devices  0.37 us (1%)
    ppermute x4, starting transfers between devices, shift(): return lax.ppermute(x, axis, [(i, (i + by) % n) for i in range(n)])  7.93 us
    ppermute x7, starting transfers between devices, swap(): return lax.ppermute(x, axis, [(i, i ^ 1) for i in range(n)])  6.9 us
    pallas_call x3, Pallas kernels, gram_blocks(): pl.pallas_call(functools.partial(gram_kernel, jobs), in_specs=[pl.BlockSp...  6.25 us
    pallas_call x1, Pallas kernels, near_units(): pl.pallas_call(functools.partial(near_kernel, owned), in_specs=[pl.BlockS...  4.06 us
    pallas_call x2, Pallas kernels, far_units(): pl.pallas_call(functools.partial(far_kernel, owned, expert), in_specs=[pl...  3.95 us
    pallas_call x1, Pallas kernels, weights(): pl.pallas_call(weights_kernel, in_specs=[pl.BlockSpec(memory_space=pltpu....  2.46 us
    pallas_call x1, Pallas kernels, label(): pl.pallas_call(label_kernel, out_shape=jax.ShapeDtypeStruct((rows.shape[0...  1 us
  transfers between devices with their start and end apart: 11, of which 1 were waited for; matrix products, arithmetic and copies ran while one was open for 0% of the time, Pallas kernels for 45%

profile of v5, /device:TPU:0, one launch (start us, length us, event | category | flops | bytes accessed | tf_op | source)
XLA Modules:
  0.0 33.1 jit_solution(5402973324551803047)
XLA Ops:
  0.0 1.0 %shard_map.64.refs_0_ = bf16[8,4224]{1,0:T(8,128)(2,1)S(1)} custom-call(bf16[8,4096]{1,0:T(8,128)(2,1)} %rows_ref.1, s32[8,8]{1,0:T(8,128)} %ids_ref.1), custom_call_target="tpu_custom_call" | custom-call | flops 17179869184 | bytes 1048576 | tf_op jit(solution)/shard_map/pallas_call | solution.py:105
  1.0 0.0 copy-start.2
  1.0 3.1 %collective-permute-start = (bf16[8,4224]{1,0:T(8,128)(2,1)S(1)}, bf16[8,4224]{1,0:T(8,128)(2,1)S(1)}, u32[]{:S(2)}, u32[]{:S(2)}) collective-permute-start(bf16[8,4224]{1,0:T(8,128)(2,1)S(1)} %shard_map.64.refs_0_), channel_id=1, source_target_pairs={{0,4},{2,6},{4,8},{6,10},{8,12},{10,14},{12,0},{14,2},{1,5},{3,7},... | collective-permute-start | bytes 202760 | tf_op jit(solution)/shard_map/ppermute | solution.py:86
  4.1 2.6 %collective-permute-start.1 = (bf16[8,4224]{1,0:T(8,128)(2,1)S(1)}, bf16[8,4224]{1,0:T(8,128)(2,1)S(1)}, u32[]{:S(2)}, u32[]{:S(2)}) collective-permute-start(bf16[8,4224]{1,0:T(8,128)(2,1)S(1)} %shard_map.64.refs_0_), channel_id=1, source_target_pairs={{0,8},{2,10},{4,12},{6,14},{8,0},{10,2},{12,4},{14,6},{1,9},{3,11}... | collective-permute-start | bytes 202760 | tf_op jit(solution)/shard_map/ppermute | solution.py:86
  6.7 1.3 %collective-permute-start.2 = (bf16[8,4224]{1,0:T(8,128)(2,1)S(1)}, bf16[8,4224]{1,0:T(8,128)(2,1)S(1)}, u32[]{:S(2)}, u32[]{:S(2)}) collective-permute-start(bf16[8,4224]{1,0:T(8,128)(2,1)S(1)} %shard_map.64.refs_0_), channel_id=1, source_target_pairs={{0,12},{2,14},{4,0},{6,2},{8,4},{10,6},{12,8},{14,10},{1,13},{3,15... | collective-permute-start | bytes 202760 | tf_op jit(solution)/shard_map/ppermute | solution.py:86
  8.1 1.5 %collective-permute-start.3 = (bf16[8,4224]{1,0:T(8,128)(2,1)S(1)}, bf16[8,4224]{1,0:T(8,128)(2,1)S(1)}, u32[]{:S(2)}, u32[]{:S(2)}) collective-permute-start(bf16[8,4224]{1,0:T(8,128)(2,1)S(1)} %shard_map.64.refs_0_), channel_id=1, source_target_pairs={{0,1},{1,0},{2,3},{3,2},{4,5},{5,4},{6,7},{7,6},{8,9},{9,8},{10,11... | collective-permute-start | bytes 202760 | tf_op jit(solution)/shard_map/ppermute | solution.py:91
  9.6 2.5 %shard_map.65 = (bf16[4096,768]{1,0:T(8,128)(2,1)S(1)}, bf16[4096,768]{1,0:T(8,128)(2,1)S(1)}, f32[32,128]{1,0:T(8,128)S(1)}) custom-call(bf16[2,4096,768]{2,1,0:T(8,128)(2,1)S(1)} %copy-done, f32[2,32,768]{2,1,0:T(8,128)S(1)} %copy-done.1), custom_call_target="tpu_custom_call" | custom-call | flops 8589934592 | bytes 25165824 | tf_op jit(solution)/shard_map/pallas_call | solution.py:157
  12.0 0.0 collective-permute-done.refs_1_.refs_2_
  12.0 0.0 collective-permute-done.1.refs_2_.refs_0_
  12.0 0.0 collective-permute-done.2.refs_3_.refs_1_
  12.0 0.3 collective-permute-done.3.refs_4_
  12.4 0.1 collective-permute-start.4
  12.5 0.9 %collective-permute-start.6 = (bf16[8,4224]{1,0:T(8,128)(2,1)S(1)}, bf16[8,4224]{1,0:T(8,128)(2,1)S(1)}, u32[]{:S(2)}, u32[]{:S(2)}) collective-permute-start(bf16[8,4224]{1,0:T(8,128)(2,1)S(1)} %get-tuple-element.23.refs_0_), channel_id=1, source_target_pairs={{0,4},{2,6},{4,8},{6,10},{8,12},{10,14},{12,0},{14,2},{1,5},{3,7},... | collective-permute-start | bytes 202760 | tf_op jit(solution)/shard_map/ppermute | solution.py:86
  13.4 1.6 %collective-permute-start.5 = (bf16[16,4224]{1,0:T(8,128)(2,1)S(1)}, bf16[16,4224]{1,0:T(8,128)(2,1)S(1)}, u32[]{:S(2)}, u32[]{:S(2)}) collective-permute-start(bf16[16,4224]{1,0:T(8,128)(2,1)S(1)} %shard_map.68), channel_id=1, source_target_pairs={{0,1},{1,0},{2,3},{3,2},{4,5},{5,4},{6,7},{7,6},{8,9},{9,8},{10,11... | collective-permute-start | bytes 405512 | tf_op jit(solution)/shard_map/ppermute | solution.py:91
  14.9 0.0 collective-permute-done.4.theirs_ref
  14.9 0.0 slice-done
  15.0 4.1 %shard_map.67 = (bf16[2,64,768]{2,1,0:T(8,128)(2,1)S(1)}, f32[2,32,128]{2,1,0:T(8,128)S(1)}, bf16[4096,768]{1,0:T(8,128)(2,1)S(1)}, bf16[4096,768]{1,0:T(8,128)(2,1)S(1)}) custom-call(bf16[32,4224]{1,0:T(8,128)(2,1)S(1)} %get-tuple-element.19.mine_ref, bf16[32,4224]{1,0:T(8,128)(2,1)S(1)} %collective-permute-done.4.theirs_ref, ...), custom_call_target="tpu_custom_call" | custom-call | flops 8589934592 | bytes 25165824 | tf_op jit(solution)/shard_map/pallas_call | solution.py:210
  19.0 0.0 collective-permute-done.6.refs_2_
  19.0 0.0 collective-permute-done.5.refs_1_
  19.1 0.1 collective-permute-start.7
  19.2 1.6 %collective-permute-start.8 = (bf16[2,64,768]{2,1,0:T(8,128)(2,1)S(1)}, bf16[2,64,768]{2,1,0:T(8,128)(2,1)S(1)}, u32[]{:S(2)}, u32[]{:S(2)}) collective-permute-start(bf16[2,64,768]{2,1,0:T(8,128)(2,1)S(1)} %get-tuple-element.22.refs_0_.refs_2_.refs_6_.refs_8_), channel_id=1, source_target_pairs={{0,1},{1,0},{2,3},{3,2},{4,5},{5,4},{6,7},{7,6},{8,9},{9,8},{10,11... | collective-permute-start | bytes 589832 | tf_op jit(solution)/shard_map/ppermute | solution.py:91
  20.7 0.0 collective-permute-done.7.theirs_ref
  20.7 2.0 %shard_map.71 = (bf16[1,64,768]{2,1,0:T(8,128)(2,1)S(1)}, f32[1,32,128]{2,1,0:T(8,128)S(1)}) custom-call(bf16[32,4224]{1,0:T(8,128)(2,1)S(1)} %shard_map.69.mine_ref, bf16[32,4224]{1,0:T(8,128)(2,1)S(1)} %collective-permute-done.7.theirs_ref, bf16[4096,768]{1,0:T(8,128)(2,1)S(1)} %get-tuple-element.20.refs_0_.gate_ref, ...), custom_call_target="tpu_custom_call" | custom-call | flops 805306368 | bytes 12582912 | tf_op jit(solution)/shard_map/pallas_call | solution.py:246
  22.7 1.5 %collective-permute-start.10 = (bf16[1,64,768]{2,1,0:T(8,128)(2,1)S(1)}, bf16[1,64,768]{2,1,0:T(8,128)(2,1)S(1)}, u32[]{:S(2)}, u32[]{:S(2)}) collective-permute-start(bf16[1,64,768]{2,1,0:T(8,128)(2,1)S(1)} %get-tuple-element.29.refs_1_.refs_3_), channel_id=1, source_target_pairs={{0,1},{1,0},{2,3},{3,2},{4,5},{5,4},{6,7},{7,6},{8,9},{9,8},{10,11... | collective-permute-start | bytes 294920 | tf_op jit(solution)/shard_map/ppermute | solution.py:91
  24.3 2.0 %shard_map.70 = (bf16[1,64,768]{2,1,0:T(8,128)(2,1)S(1)}, f32[1,32,128]{2,1,0:T(8,128)S(1)}) custom-call(bf16[32,4224]{1,0:T(8,128)(2,1)S(1)} %shard_map.69.mine_ref, bf16[32,4224]{1,0:T(8,128)(2,1)S(1)} %collective-permute-done.7.theirs_ref, bf16[4096,768]{1,0:T(8,128)(2,1)S(1)} %get-tuple-element.21.refs_1_.gate_ref, ...), custom_call_target="tpu_custom_call" | custom-call | flops 805306368 | bytes 12582912 | tf_op jit(solution)/shard_map/pallas_call | solution.py:246
  26.2 0.6 %collective-permute-start.9 = (bf16[1,64,768]{2,1,0:T(8,128)(2,1)S(1)}, bf16[1,64,768]{2,1,0:T(8,128)(2,1)S(1)}, u32[]{:S(2)}, u32[]{:S(2)}) collective-permute-start(bf16[1,64,768]{2,1,0:T(8,128)(2,1)S(1)} %get-tuple-element.26.refs_7_.refs_9_.refs_1_), channel_id=1, source_target_pairs={{0,1},{1,0},{2,3},{3,2},{4,5},{5,4},{6,7},{7,6},{8,9},{9,8},{10,11... | collective-permute-start | bytes 294920 | tf_op jit(solution)/shard_map/ppermute | solution.py:91
  26.9 2.6 %shard_map.72.refs_6_ = f32[2,768,1536]{2,1,0:T(8,128)} custom-call(bf16[2,64,768]{2,1,0:T(8,128)(2,1)S(1)} %get-tuple-element.22.refs_0_.refs_2_.refs_6_.refs_8_, bf16[1,64,768]{2,1,0:T(8,128)(2,1)S(1)} %get-tuple-element.29.refs_1_.refs_3_, bf16[2,64,768]{2,1,0:T(8,128)(2,1)S(1)} %get-tuple-element.22.refs_0_.refs_2_.refs_6_.refs_8_, ...), custom_call_target="tpu_custom_call" | custom-call | flops 301989888 | bytes 4718592 | tf_op jit(solution)/shard_map/pallas_call | solution.py:303
  29.5 0.0 collective-permute-done.8.refs_2_
  29.5 0.0 collective-permute-done.10.refs_3_
  29.5 1.8 %shard_map.73.refs_6_ = f32[2,768,1536]{2,1,0:T(8,128)} custom-call(bf16[2,64,768]{2,1,0:T(8,128)(2,1)S(1)} %get-tuple-element.22.refs_0_.refs_2_.refs_6_.refs_8_, bf16[1,64,768]{2,1,0:T(8,128)(2,1)S(1)} %get-tuple-element.29.refs_1_.refs_3_, bf16[2,64,768]{2,1,0:T(8,128)(2,1)S(1)} %collective-permute-done.8.refs_2_, ...), custom_call_target="tpu_custom_call", output_to_operand_aliasing={{}: (6, {})} | custom-call | flops 150994944 | bytes 2359296 | tf_op jit(solution)/shard_map/pallas_call | solution.py:303
  31.3 0.0 collective-permute-done.9.refs_3_
  31.3 1.8 %shard_map.74 = f32[2,768,1536]{2,1,0:T(8,128)} custom-call(bf16[2,64,768]{2,1,0:T(8,128)(2,1)S(1)} %get-tuple-element.22.refs_0_.refs_2_.refs_6_.refs_8_, bf16[1,64,768]{2,1,0:T(8,128)(2,1)S(1)} %get-tuple-element.26.refs_7_.refs_9_.refs_1_, bf16[2,64,768]{2,1,0:T(8,128)(2,1)S(1)} %collective-permute-done.8.refs_2_, ...), custom_call_target="tpu_custom_call", output_to_operand_aliasing={{}: (6, {})} | custom-call | flops 150994944 | bytes 2359296 | tf_op jit(solution)/shard_map/pallas_call | solution.py:303
  (14 shorter events, 0.1 us)
Async XLA Ops:
  0.0 9.6 %copy-start.1 = (f32[2,32,768]{2,1,0:T(8,128)S(1)}, f32[2,32,768]{2,1,0:T(8,128)}, u32[]{:S(2)}) copy-start(f32[2,32,768]{2,1,0:T(8,128)} %scale_ref.2) | copy-start | bytes 589828
  0.0 9.6 %copy-start = (bf16[2,4096,768]{2,1,0:T(8,128)(2,1)S(1)}, bf16[2,4096,768]{2,1,0:T(8,128)(2,1)}, u32[]{:S(2)}) copy-start(bf16[2,4096,768]{2,1,0:T(8,128)(2,1)} %codes_ref.2) | copy-start | bytes 37748740
  0.0 14.9 %slice-start = ((s8[12582912]{0:T(1024)(128)(4,1)}), s8[4194304]{0:T(1024)(128)(4,1)S(1)}, s32[]{:S(2)}) async-start(s8[12582912]{0:T(1024)(128)(4,1)} %bitcast), calls=%async_computation | async-start | bytes 8388608
  0.0 14.9 %slice-start.1 = ((s8[12582912]{0:T(1024)(128)(4,1)}), s8[4194304]{0:T(1024)(128)(4,1)S(1)}, s32[]{:S(2)}) async-start(s8[12582912]{0:T(1024)(128)(4,1)} %bitcast), calls=%async_computation.1 | async-start | bytes 8388608
  1.0 13.9 %slice-start.2 = ((s8[12582912]{0:T(1024)(128)(4,1)}), s8[4194304]{0:T(1024)(128)(4,1)S(1)}, s32[]{:S(2)}) async-start(s8[12582912]{0:T(1024)(128)(4,1)} %bitcast), calls=%async_computation.2 | async-start | bytes 8388608
  1.0 13.9 %copy-start.2 = (f32[2,32,768]{2,1,0:T(8,128)S(1)}, f32[2,32,768]{2,1,0:T(8,128)}, u32[]{:S(2)}) copy-start(f32[2,32,768]{2,1,0:T(8,128)} %scale_ref.3) | copy-start | bytes 589828
  1.0 11.0 %collective-permute-start = (bf16[8,4224]{1,0:T(8,128)(2,1)S(1)}, bf16[8,4224]{1,0:T(8,128)(2,1)S(1)}, u32[]{:S(2)}, u32[]{:S(2)}) collective-permute-start(bf16[8,4224]{1,0:T(8,128)(2,1)S(1)} %shard_map.64.refs_0_), channel_id=1, source_target_pairs={{0,4},{2,6},{4,8},{6,10},{8,12},{10,14},{12,0},{14,2},{1,5},{3,7},... | collective-permute-start | bytes 202760 | tf_op jit(solution)/shard_map/ppermute | solution.py:86
  4.1 7.9 %collective-permute-start.1 = (bf16[8,4224]{1,0:T(8,128)(2,1)S(1)}, bf16[8,4224]{1,0:T(8,128)(2,1)S(1)}, u32[]{:S(2)}, u32[]{:S(2)}) collective-permute-start(bf16[8,4224]{1,0:T(8,128)(2,1)S(1)} %shard_map.64.refs_0_), channel_id=1, source_target_pairs={{0,8},{2,10},{4,12},{6,14},{8,0},{10,2},{12,4},{14,6},{1,9},{3,11}... | collective-permute-start | bytes 202760 | tf_op jit(solution)/shard_map/ppermute | solution.py:86
  6.7 5.3 %collective-permute-start.2 = (bf16[8,4224]{1,0:T(8,128)(2,1)S(1)}, bf16[8,4224]{1,0:T(8,128)(2,1)S(1)}, u32[]{:S(2)}, u32[]{:S(2)}) collective-permute-start(bf16[8,4224]{1,0:T(8,128)(2,1)S(1)} %shard_map.64.refs_0_), channel_id=1, source_target_pairs={{0,12},{2,14},{4,0},{6,2},{8,4},{10,6},{12,8},{14,10},{1,13},{3,15... | collective-permute-start | bytes 202760 | tf_op jit(solution)/shard_map/ppermute | solution.py:86
  8.1 4.3 %collective-permute-start.3 = (bf16[8,4224]{1,0:T(8,128)(2,1)S(1)}, bf16[8,4224]{1,0:T(8,128)(2,1)S(1)}, u32[]{:S(2)}, u32[]{:S(2)}) collective-permute-start(bf16[8,4224]{1,0:T(8,128)(2,1)S(1)} %shard_map.64.refs_0_), channel_id=1, source_target_pairs={{0,1},{1,0},{2,3},{3,2},{4,5},{5,4},{6,7},{7,6},{8,9},{9,8},{10,11... | collective-permute-start | bytes 202760 | tf_op jit(solution)/shard_map/ppermute | solution.py:91
  12.4 2.6 %collective-permute-start.4 = (bf16[32,4224]{1,0:T(8,128)(2,1)S(1)}, bf16[32,4224]{1,0:T(8,128)(2,1)S(1)}, u32[]{:S(2)}, u32[]{:S(2)}) collective-permute-start(bf16[32,4224]{1,0:T(8,128)(2,1)S(1)} %get-tuple-element.19.mine_ref), channel_id=1, source_target_pairs={{0,2},{2,0},{4,6},{6,4},{8,10},{10,8},{12,14},{14,12},{1,3},{3,1},... | collective-permute-start | bytes 811016 | tf_op jit(solution)/shard_map/ppermute | solution.py:91
  12.5 6.6 %collective-permute-start.6 = (bf16[8,4224]{1,0:T(8,128)(2,1)S(1)}, bf16[8,4224]{1,0:T(8,128)(2,1)S(1)}, u32[]{:S(2)}, u32[]{:S(2)}) collective-permute-start(bf16[8,4224]{1,0:T(8,128)(2,1)S(1)} %get-tuple-element.23.refs_0_), channel_id=1, source_target_pairs={{0,4},{2,6},{4,8},{6,10},{8,12},{10,14},{12,0},{14,2},{1,5},{3,7},... | collective-permute-start | bytes 202760 | tf_op jit(solution)/shard_map/ppermute | solution.py:86
  13.4 5.7 %collective-permute-start.5 = (bf16[16,4224]{1,0:T(8,128)(2,1)S(1)}, bf16[16,4224]{1,0:T(8,128)(2,1)S(1)}, u32[]{:S(2)}, u32[]{:S(2)}) collective-permute-start(bf16[16,4224]{1,0:T(8,128)(2,1)S(1)} %shard_map.68), channel_id=1, source_target_pairs={{0,1},{1,0},{2,3},{3,2},{4,5},{5,4},{6,7},{7,6},{8,9},{9,8},{10,11... | collective-permute-start | bytes 405512 | tf_op jit(solution)/shard_map/ppermute | solution.py:91
  19.1 1.6 %collective-permute-start.7 = (bf16[32,4224]{1,0:T(8,128)(2,1)S(1)}, bf16[32,4224]{1,0:T(8,128)(2,1)S(1)}, u32[]{:S(2)}, u32[]{:S(2)}) collective-permute-start(bf16[32,4224]{1,0:T(8,128)(2,1)S(1)} %shard_map.69.mine_ref), channel_id=1, source_target_pairs={{0,2},{2,0},{4,6},{6,4},{8,10},{10,8},{12,14},{14,12},{1,3},{3,1},... | collective-permute-start | bytes 811016 | tf_op jit(solution)/shard_map/ppermute | solution.py:91
  19.2 10.3 %collective-permute-start.8 = (bf16[2,64,768]{2,1,0:T(8,128)(2,1)S(1)}, bf16[2,64,768]{2,1,0:T(8,128)(2,1)S(1)}, u32[]{:S(2)}, u32[]{:S(2)}) collective-permute-start(bf16[2,64,768]{2,1,0:T(8,128)(2,1)S(1)} %get-tuple-element.22.refs_0_.refs_2_.refs_6_.refs_8_), channel_id=1, source_target_pairs={{0,1},{1,0},{2,3},{3,2},{4,5},{5,4},{6,7},{7,6},{8,9},{9,8},{10,11... | collective-permute-start | bytes 589832 | tf_op jit(solution)/shard_map/ppermute | solution.py:91
  22.7 6.8 %collective-permute-start.10 = (bf16[1,64,768]{2,1,0:T(8,128)(2,1)S(1)}, bf16[1,64,768]{2,1,0:T(8,128)(2,1)S(1)}, u32[]{:S(2)}, u32[]{:S(2)}) collective-permute-start(bf16[1,64,768]{2,1,0:T(8,128)(2,1)S(1)} %get-tuple-element.29.refs_1_.refs_3_), channel_id=1, source_target_pairs={{0,1},{1,0},{2,3},{3,2},{4,5},{5,4},{6,7},{7,6},{8,9},{9,8},{10,11... | collective-permute-start | bytes 294920 | tf_op jit(solution)/shard_map/ppermute | solution.py:91
  26.2 5.1 %collective-permute-start.9 = (bf16[1,64,768]{2,1,0:T(8,128)(2,1)S(1)}, bf16[1,64,768]{2,1,0:T(8,128)(2,1)S(1)}, u32[]{:S(2)}, u32[]{:S(2)}) collective-permute-start(bf16[1,64,768]{2,1,0:T(8,128)(2,1)S(1)} %get-tuple-element.26.refs_7_.refs_9_.refs_1_), channel_id=1, source_target_pairs={{0,1},{1,0},{2,3},{3,2},{4,5},{5,4},{6,7},{7,6},{8,9},{9,8},{10,11... | collective-permute-start | bytes 294920 | tf_op jit(solution)/shard_map/ppermute | solution.py:91

commit v6 on v5

--- a/solution.py
+++ b/solution.py
@@ -11,6 +11,7 @@
 LANES = 128
 NEAR_BLOCK = 768
 FAR_BLOCK = 128
+PARTS = 3
 F32 = jnp.float32
 BF16 = jnp.bfloat16
 
@@ -159,7 +160,7 @@
         in_specs=[pl.BlockSpec(memory_space=pltpu.VMEM)] * 2,
         out_specs=[pl.BlockSpec(memory_space=pltpu.VMEM)] * (owned + 1),
         out_shape=[pltpu.VMEM(codes.shape[1:], BF16)] * owned
-        + [jax.ShapeDtypeStruct((32, LANES), F32)],
+        + [jax.ShapeDtypeStruct((16, LANES), F32)],
         compiler_params=pltpu.CompilerParams(vmem_limit_bytes=2 << 20),
         cost_estimate=pl.CostEstimate(
             flops=1 << 33, bytes_accessed=4 * codes.size, transcendentals=0
@@ -267,7 +268,7 @@
     out_ref, buffer, sems = refs[-3:]
     me = lax.axis_index("dp")
     width = buffer.shape[2]
-    half = width // 2
+    size = width // PARTS
     copies = []
     for i, (expert, first, second, theirs) in enumerate(jobs):
         place = pl.ds(pl.multiple_of((1 - me if theirs else me) * width, LANES), width)
@@ -278,10 +279,10 @@
         else:
             right = jnp.concatenate([right_a[first], right_b[second]])
         scale = 2.0 / (count_a[first, 0:1, 0:1] + count_b[second, 0:1, 0:1])
-        for part in range(2):
-            rows = pl.ds(part * half, half)
+        for part in range(PARTS):
+            rows = pl.ds(part * size, size)
             product = lax.dot_general(
-                left[:, part * half : (part + 1) * half],
+                left[:, part * size : (part + 1) * size],
                 right,
                 (((0,), (0,)), ((), ())),
                 preferred_element_type=F32,
@@ -309,7 +310,7 @@
         input_output_aliases={} if onto is None else {len(flat): 0},
         scratch_shapes=[
             pltpu.VMEM((n, width, width), F32),
-            pltpu.SemaphoreType.DMA((n, 2)),
+            pltpu.SemaphoreType.DMA((n, PARTS)),
         ],
         compiler_params=pltpu.CompilerParams(vmem_limit_bytes=8 << 20),
         cost_estimate=pl.CostEstimate(
@@ -357,7 +358,8 @@
     fits = (
         lax.axis_size("dp") == 2
         and lax.axis_size("expert") % 2 == 0
-        and width % LANES == 0
+        and lax.axis_size("expert") >= 6
+        and width % (PARTS * LANES) == 0
         and depth % (16 * gate_scales.shape[1]) == 0
         and tokens.shape[0] * (lax.axis_size("expert") // 2) % 16 == 0
         and expert_ids.shape[1] <= LANES

time: 33.3 us -> 33 us (level)
  Pallas kernels: 17.8 us -> 17.3 us
  transfers between devices with their start and end apart: 11 -> 11, of which waited for: 1 -> 2; matrix products, arithmetic and copies ran while one was open for 0% -> 0% of each run, Pallas kernels for 45% -> 44%
where the time goes in v6:
time: 33 us; the launch traced here: 32.9 us
  Pallas kernels  17.3 us (52%)
  starting transfers between devices  14.8 us (45%)
  waiting for transfers between devices  0.56 us (2%)
    ppermute x4, starting transfers between devices, shift(): return lax.ppermute(x, axis, [(i, (i + by) % n) for i in range(n)])  7.93 us
    ppermute x7, starting transfers between devices, swap(): return lax.ppermute(x, axis, [(i, i ^ 1) for i in range(n)])  6.9 us
    pallas_call x3, Pallas kernels, gram_blocks(): pl.pallas_call(functools.partial(gram_kernel, jobs), in_specs=[pl.BlockSp...  5.97 us
    pallas_call x2, Pallas kernels, far_units(): pl.pallas_call(functools.partial(far_kernel, owned, expert), in_specs=[pl...  3.95 us
    pallas_call x1, Pallas kernels, near_units(): pl.pallas_call(functools.partial(near_kernel, owned), in_specs=[pl.BlockS...  3.87 us
    pallas_call x1, Pallas kernels, weights(): pl.pallas_call(weights_kernel, in_specs=[pl.BlockSpec(memory_space=pltpu....  2.45 us
    pallas_call x1, Pallas kernels, label(): pl.pallas_call(label_kernel, out_shape=jax.ShapeDtypeStruct((rows.shape[0...  1 us
  transfers between devices with their start and end apart: 11, of which 2 were waited for; matrix products, arithmetic and copies ran while one was open for 0% of the time, Pallas kernels for 44%

profile of v6, /device:TPU:0, one launch (start us, length us, event | category | flops | bytes accessed | tf_op | source)
XLA Modules:
  0.0 32.9 jit_solution(3903332869547108572)
XLA Ops:
  0.0 1.0 %shard_map.64.refs_0_ = bf16[8,4224]{1,0:T(8,128)(2,1)S(1)} custom-call(bf16[8,4096]{1,0:T(8,128)(2,1)} %rows_ref.1, s32[8,8]{1,0:T(8,128)} %ids_ref.1), custom_call_target="tpu_custom_call" | custom-call | flops 17179869184 | bytes 1048576 | tf_op jit(solution)/shard_map/pallas_call | solution.py:106
  1.0 0.0 copy-start.2
  1.0 3.1 %collective-permute-start = (bf16[8,4224]{1,0:T(8,128)(2,1)S(1)}, bf16[8,4224]{1,0:T(8,128)(2,1)S(1)}, u32[]{:S(2)}, u32[]{:S(2)}) collective-permute-start(bf16[8,4224]{1,0:T(8,128)(2,1)S(1)} %shard_map.64.refs_0_), channel_id=1, source_target_pairs={{0,4},{2,6},{4,8},{6,10},{8,12},{10,14},{12,0},{14,2},{1,5},{3,7},... | collective-permute-start | bytes 202760 | tf_op jit(solution)/shard_map/ppermute | solution.py:87
  4.1 2.6 %collective-permute-start.1 = (bf16[8,4224]{1,0:T(8,128)(2,1)S(1)}, bf16[8,4224]{1,0:T(8,128)(2,1)S(1)}, u32[]{:S(2)}, u32[]{:S(2)}) collective-permute-start(bf16[8,4224]{1,0:T(8,128)(2,1)S(1)} %shard_map.64.refs_0_), channel_id=1, source_target_pairs={{0,8},{2,10},{4,12},{6,14},{8,0},{10,2},{12,4},{14,6},{1,9},{3,11}... | collective-permute-start | bytes 202760 | tf_op jit(solution)/shard_map/ppermute | solution.py:87
  6.7 1.3 %collective-permute-start.2 = (bf16[8,4224]{1,0:T(8,128)(2,1)S(1)}, bf16[8,4224]{1,0:T(8,128)(2,1)S(1)}, u32[]{:S(2)}, u32[]{:S(2)}) collective-permute-start(bf16[8,4224]{1,0:T(8,128)(2,1)S(1)} %shard_map.64.refs_0_), channel_id=1, source_target_pairs={{0,12},{2,14},{4,0},{6,2},{8,4},{10,6},{12,8},{14,10},{1,13},{3,15... | collective-permute-start | bytes 202760 | tf_op jit(solution)/shard_map/ppermute | solution.py:87
  8.1 1.5 %collective-permute-start.3 = (bf16[8,4224]{1,0:T(8,128)(2,1)S(1)}, bf16[8,4224]{1,0:T(8,128)(2,1)S(1)}, u32[]{:S(2)}, u32[]{:S(2)}) collective-permute-start(bf16[8,4224]{1,0:T(8,128)(2,1)S(1)} %shard_map.64.refs_0_), channel_id=1, source_target_pairs={{0,1},{1,0},{2,3},{3,2},{4,5},{5,4},{6,7},{7,6},{8,9},{9,8},{10,11... | collective-permute-start | bytes 202760 | tf_op jit(solution)/shard_map/ppermute | solution.py:92
  9.5 0.0 copy-done.1
  9.6 2.5 %shard_map.65 = (bf16[4096,768]{1,0:T(8,128)(2,1)S(1)}, bf16[4096,768]{1,0:T(8,128)(2,1)S(1)}, f32[16,128]{1,0:T(8,128)S(1)}) custom-call(bf16[2,4096,768]{2,1,0:T(8,128)(2,1)S(1)} %copy-done, f32[2,32,768]{2,1,0:T(8,128)S(1)} %copy-done.1), custom_call_target="tpu_custom_call" | custom-call | flops 8589934592 | bytes 25165824 | tf_op jit(solution)/shard_map/pallas_call | solution.py:158
  12.0 0.0 collective-permute-done.refs_1_.refs_2_
  12.0 0.0 collective-permute-done.1.refs_2_.refs_0_
  12.0 0.0 collective-permute-done.2.refs_3_.refs_1_
  12.0 0.3 collective-permute-done.3.refs_4_
  12.4 0.1 collective-permute-start.4
  12.5 0.9 %collective-permute-start.6 = (bf16[8,4224]{1,0:T(8,128)(2,1)S(1)}, bf16[8,4224]{1,0:T(8,128)(2,1)S(1)}, u32[]{:S(2)}, u32[]{:S(2)}) collective-permute-start(bf16[8,4224]{1,0:T(8,128)(2,1)S(1)} %get-tuple-element.23.refs_0_), channel_id=1, source_target_pairs={{0,4},{2,6},{4,8},{6,10},{8,12},{10,14},{12,0},{14,2},{1,5},{3,7},... | collective-permute-start | bytes 202760 | tf_op jit(solution)/shard_map/ppermute | solution.py:87
  13.4 1.6 %collective-permute-start.5 = (bf16[16,4224]{1,0:T(8,128)(2,1)S(1)}, bf16[16,4224]{1,0:T(8,128)(2,1)S(1)}, u32[]{:S(2)}, u32[]{:S(2)}) collective-permute-start(bf16[16,4224]{1,0:T(8,128)(2,1)S(1)} %shard_map.68), channel_id=1, source_target_pairs={{0,1},{1,0},{2,3},{3,2},{4,5},{5,4},{6,7},{7,6},{8,9},{9,8},{10,11... | collective-permute-start | bytes 405512 | tf_op jit(solution)/shard_map/ppermute | solution.py:92
  14.9 0.0 collective-permute-done.4.theirs_ref
  15.0 3.9 %shard_map.67 = (bf16[2,64,768]{2,1,0:T(8,128)(2,1)S(1)}, f32[2,32,128]{2,1,0:T(8,128)S(1)}, bf16[4096,768]{1,0:T(8,128)(2,1)S(1)}, bf16[4096,768]{1,0:T(8,128)(2,1)S(1)}) custom-call(bf16[32,4224]{1,0:T(8,128)(2,1)S(1)} %get-tuple-element.19.mine_ref, bf16[32,4224]{1,0:T(8,128)(2,1)S(1)} %collective-permute-done.4.theirs_ref, ...), custom_call_target="tpu_custom_call" | custom-call | flops 8589934592 | bytes 25165824 | tf_op jit(solution)/shard_map/pallas_call | solution.py:211
  18.8 0.0 collective-permute-done.6.refs_2_
  18.8 0.2 collective-permute-done.5.refs_1_
  19.1 0.1 collective-permute-start.7
  19.2 1.6 %collective-permute-start.8 = (bf16[2,64,768]{2,1,0:T(8,128)(2,1)S(1)}, bf16[2,64,768]{2,1,0:T(8,128)(2,1)S(1)}, u32[]{:S(2)}, u32[]{:S(2)}) collective-permute-start(bf16[2,64,768]{2,1,0:T(8,128)(2,1)S(1)} %get-tuple-element.22.refs_0_.refs_2_.refs_6_.refs_8_), channel_id=1, source_target_pairs={{0,1},{1,0},{2,3},{3,2},{4,5},{5,4},{6,7},{7,6},{8,9},{9,8},{10,11... | collective-permute-start | bytes 589832 | tf_op jit(solution)/shard_map/ppermute | solution.py:92
  20.7 0.0 collective-permute-done.7.theirs_ref
  20.7 2.0 %shard_map.71 = (bf16[1,64,768]{2,1,0:T(8,128)(2,1)S(1)}, f32[1,32,128]{2,1,0:T(8,128)S(1)}) custom-call(bf16[32,4224]{1,0:T(8,128)(2,1)S(1)} %shard_map.69.mine_ref, bf16[32,4224]{1,0:T(8,128)(2,1)S(1)} %collective-permute-done.7.theirs_ref, bf16[4096,768]{1,0:T(8,128)(2,1)S(1)} %get-tuple-element.20.refs_0_.gate_ref, ...), custom_call_target="tpu_custom_call" | custom-call | flops 805306368 | bytes 12582912 | tf_op jit(solution)/shard_map/pallas_call | solution.py:247
  22.7 1.5 %collective-permute-start.10 = (bf16[1,64,768]{2,1,0:T(8,128)(2,1)S(1)}, bf16[1,64,768]{2,1,0:T(8,128)(2,1)S(1)}, u32[]{:S(2)}, u32[]{:S(2)}) collective-permute-start(bf16[1,64,768]{2,1,0:T(8,128)(2,1)S(1)} %get-tuple-element.29.refs_1_.refs_3_), channel_id=1, source_target_pairs={{0,1},{1,0},{2,3},{3,2},{4,5},{5,4},{6,7},{7,6},{8,9},{9,8},{10,11... | collective-permute-start | bytes 294920 | tf_op jit(solution)/shard_map/ppermute | solution.py:92
  24.3 2.0 %shard_map.70 = (bf16[1,64,768]{2,1,0:T(8,128)(2,1)S(1)}, f32[1,32,128]{2,1,0:T(8,128)S(1)}) custom-call(bf16[32,4224]{1,0:T(8,128)(2,1)S(1)} %shard_map.69.mine_ref, bf16[32,4224]{1,0:T(8,128)(2,1)S(1)} %collective-permute-done.7.theirs_ref, bf16[4096,768]{1,0:T(8,128)(2,1)S(1)} %get-tuple-element.21.refs_1_.gate_ref, ...), custom_call_target="tpu_custom_call" | custom-call | flops 805306368 | bytes 12582912 | tf_op jit(solution)/shard_map/pallas_call | solution.py:247
  26.2 0.6 %collective-permute-start.9 = (bf16[1,64,768]{2,1,0:T(8,128)(2,1)S(1)}, bf16[1,64,768]{2,1,0:T(8,128)(2,1)S(1)}, u32[]{:S(2)}, u32[]{:S(2)}) collective-permute-start(bf16[1,64,768]{2,1,0:T(8,128)(2,1)S(1)} %get-tuple-element.26.refs_7_.refs_9_.refs_1_), channel_id=1, source_target_pairs={{0,1},{1,0},{2,3},{3,2},{4,5},{5,4},{6,7},{7,6},{8,9},{9,8},{10,11... | collective-permute-start | bytes 294920 | tf_op jit(solution)/shard_map/ppermute | solution.py:92
  26.9 2.5 %shard_map.72.refs_6_ = f32[2,768,1536]{2,1,0:T(8,128)} custom-call(bf16[2,64,768]{2,1,0:T(8,128)(2,1)S(1)} %get-tuple-element.22.refs_0_.refs_2_.refs_6_.refs_8_, bf16[1,64,768]{2,1,0:T(8,128)(2,1)S(1)} %get-tuple-element.29.refs_1_.refs_3_, bf16[2,64,768]{2,1,0:T(8,128)(2,1)S(1)} %get-tuple-element.22.refs_0_.refs_2_.refs_6_.refs_8_, ...), custom_call_target="tpu_custom_call" | custom-call | flops 301989888 | bytes 4718592 | tf_op jit(solution)/shard_map/pallas_call | solution.py:304
  29.4 0.0 collective-permute-done.8.refs_2_
  29.4 0.0 collective-permute-done.10.refs_3_
  29.4 1.7 %shard_map.73.refs_6_ = f32[2,768,1536]{2,1,0:T(8,128)} custom-call(bf16[2,64,768]{2,1,0:T(8,128)(2,1)S(1)} %get-tuple-element.22.refs_0_.refs_2_.refs_6_.refs_8_, bf16[1,64,768]{2,1,0:T(8,128)(2,1)S(1)} %get-tuple-element.29.refs_1_.refs_3_, bf16[2,64,768]{2,1,0:T(8,128)(2,1)S(1)} %collective-permute-done.8.refs_2_, ...), custom_call_target="tpu_custom_call", output_to_operand_aliasing={{}: (6, {})} | custom-call | flops 150994944 | bytes 2359296 | tf_op jit(solution)/shard_map/pallas_call | solution.py:304
  31.2 0.0 collective-permute-done.9.refs_3_
  31.2 1.7 %shard_map.74 = f32[2,768,1536]{2,1,0:T(8,128)} custom-call(bf16[2,64,768]{2,1,0:T(8,128)(2,1)S(1)} %get-tuple-element.22.refs_0_.refs_2_.refs_6_.refs_8_, bf16[1,64,768]{2,1,0:T(8,128)(2,1)S(1)} %get-tuple-element.26.refs_7_.refs_9_.refs_1_, bf16[2,64,768]{2,1,0:T(8,128)(2,1)S(1)} %collective-permute-done.8.refs_2_, ...), custom_call_target="tpu_custom_call", output_to_operand_aliasing={{}: (6, {})} | custom-call | flops 150994944 | bytes 2359296 | tf_op jit(solution)/shard_map/pallas_call | solution.py:304
  (14 shorter events, 0.1 us)
Async XLA Ops:
  0.0 9.6 %copy-start.1 = (f32[2,32,768]{2,1,0:T(8,128)S(1)}, f32[2,32,768]{2,1,0:T(8,128)}, u32[]{:S(2)}) copy-start(f32[2,32,768]{2,1,0:T(8,128)} %scale_ref.2) | copy-start | bytes 589828
  0.0 9.6 %copy-start = (bf16[2,4096,768]{2,1,0:T(8,128)(2,1)S(1)}, bf16[2,4096,768]{2,1,0:T(8,128)(2,1)}, u32[]{:S(2)}) copy-start(bf16[2,4096,768]{2,1,0:T(8,128)(2,1)} %codes_ref.2) | copy-start | bytes 37748740
  0.0 14.9 %slice-start = ((s8[12582912]{0:T(1024)(128)(4,1)}), s8[4194304]{0:T(1024)(128)(4,1)S(1)}, s32[]{:S(2)}) async-start(s8[12582912]{0:T(1024)(128)(4,1)} %bitcast), calls=%async_computation | async-start | bytes 8388608
  0.0 14.9 %slice-start.1 = ((s8[12582912]{0:T(1024)(128)(4,1)}), s8[4194304]{0:T(1024)(128)(4,1)S(1)}, s32[]{:S(2)}) async-start(s8[12582912]{0:T(1024)(128)(4,1)} %bitcast), calls=%async_computation.1 | async-start | bytes 8388608
  1.0 13.9 %slice-start.2 = ((s8[12582912]{0:T(1024)(128)(4,1)}), s8[4194304]{0:T(1024)(128)(4,1)S(1)}, s32[]{:S(2)}) async-start(s8[12582912]{0:T(1024)(128)(4,1)} %bitcast), calls=%async_computation.2 | async-start | bytes 8388608
  1.0 13.9 %copy-start.2 = (f32[2,32,768]{2,1,0:T(8,128)S(1)}, f32[2,32,768]{2,1,0:T(8,128)}, u32[]{:S(2)}) copy-start(f32[2,32,768]{2,1,0:T(8,128)} %scale_ref.3) | copy-start | bytes 589828
  1.0 11.0 %collective-permute-start = (bf16[8,4224]{1,0:T(8,128)(2,1)S(1)}, bf16[8,4224]{1,0:T(8,128)(2,1)S(1)}, u32[]{:S(2)}, u32[]{:S(2)}) collective-permute-start(bf16[8,4224]{1,0:T(8,128)(2,1)S(1)} %shard_map.64.refs_0_), channel_id=1, source_target_pairs={{0,4},{2,6},{4,8},{6,10},{8,12},{10,14},{12,0},{14,2},{1,5},{3,7},... | collective-permute-start | bytes 202760 | tf_op jit(solution)/shard_map/ppermute | solution.py:87
  4.1 7.9 %collective-permute-start.1 = (bf16[8,4224]{1,0:T(8,128)(2,1)S(1)}, bf16[8,4224]{1,0:T(8,128)(2,1)S(1)}, u32[]{:S(2)}, u32[]{:S(2)}) collective-permute-start(bf16[8,4224]{1,0:T(8,128)(2,1)S(1)} %shard_map.64.refs_0_), channel_id=1, source_target_pairs={{0,8},{2,10},{4,12},{6,14},{8,0},{10,2},{12,4},{14,6},{1,9},{3,11}... | collective-permute-start | bytes 202760 | tf_op jit(solution)/shard_map/ppermute | solution.py:87
  6.7 5.3 %collective-permute-start.2 = (bf16[8,4224]{1,0:T(8,128)(2,1)S(1)}, bf16[8,4224]{1,0:T(8,128)(2,1)S(1)}, u32[]{:S(2)}, u32[]{:S(2)}) collective-permute-start(bf16[8,4224]{1,0:T(8,128)(2,1)S(1)} %shard_map.64.refs_0_), channel_id=1, source_target_pairs={{0,12},{2,14},{4,0},{6,2},{8,4},{10,6},{12,8},{14,10},{1,13},{3,15... | collective-permute-start | bytes 202760 | tf_op jit(solution)/shard_map/ppermute | solution.py:87
  8.1 4.3 %collective-permute-start.3 = (bf16[8,4224]{1,0:T(8,128)(2,1)S(1)}, bf16[8,4224]{1,0:T(8,128)(2,1)S(1)}, u32[]{:S(2)}, u32[]{:S(2)}) collective-permute-start(bf16[8,4224]{1,0:T(8,128)(2,1)S(1)} %shard_map.64.refs_0_), channel_id=1, source_target_pairs={{0,1},{1,0},{2,3},{3,2},{4,5},{5,4},{6,7},{7,6},{8,9},{9,8},{10,11... | collective-permute-start | bytes 202760 | tf_op jit(solution)/shard_map/ppermute | solution.py:92
  12.4 2.6 %collective-permute-start.4 = (bf16[32,4224]{1,0:T(8,128)(2,1)S(1)}, bf16[32,4224]{1,0:T(8,128)(2,1)S(1)}, u32[]{:S(2)}, u32[]{:S(2)}) collective-permute-start(bf16[32,4224]{1,0:T(8,128)(2,1)S(1)} %get-tuple-element.19.mine_ref), channel_id=1, source_target_pairs={{0,2},{2,0},{4,6},{6,4},{8,10},{10,8},{12,14},{14,12},{1,3},{3,1},... | collective-permute-start | bytes 811016 | tf_op jit(solution)/shard_map/ppermute | solution.py:92
  12.5 6.4 %collective-permute-start.6 = (bf16[8,4224]{1,0:T(8,128)(2,1)S(1)}, bf16[8,4224]{1,0:T(8,128)(2,1)S(1)}, u32[]{:S(2)}, u32[]{:S(2)}) collective-permute-start(bf16[8,4224]{1,0:T(8,128)(2,1)S(1)} %get-tuple-element.23.refs_0_), channel_id=1, source_target_pairs={{0,4},{2,6},{4,8},{6,10},{8,12},{10,14},{12,0},{14,2},{1,5},{3,7},... | collective-permute-start | bytes 202760 | tf_op jit(solution)/shard_map/ppermute | solution.py:87
  13.4 5.7 %collective-permute-start.5 = (bf16[16,4224]{1,0:T(8,128)(2,1)S(1)}, bf16[16,4224]{1,0:T(8,128)(2,1)S(1)}, u32[]{:S(2)}, u32[]{:S(2)}) collective-permute-start(bf16[16,4224]{1,0:T(8,128)(2,1)S(1)} %shard_map.68), channel_id=1, source_target_pairs={{0,1},{1,0},{2,3},{3,2},{4,5},{5,4},{6,7},{7,6},{8,9},{9,8},{10,11... | collective-permute-start | bytes 405512 | tf_op jit(solution)/shard_map/ppermute | solution.py:92
  19.1 1.6 %collective-permute-start.7 = (bf16[32,4224]{1,0:T(8,128)(2,1)S(1)}, bf16[32,4224]{1,0:T(8,128)(2,1)S(1)}, u32[]{:S(2)}, u32[]{:S(2)}) collective-permute-start(bf16[32,4224]{1,0:T(8,128)(2,1)S(1)} %shard_map.69.mine_ref), channel_id=1, source_target_pairs={{0,2},{2,0},{4,6},{6,4},{8,10},{10,8},{12,14},{14,12},{1,3},{3,1},... | collective-permute-start | bytes 811016 | tf_op jit(solution)/shard_map/ppermute | solution.py:92
  19.2 10.2 %collective-permute-start.8 = (bf16[2,64,768]{2,1,0:T(8,128)(2,1)S(1)}, bf16[2,64,768]{2,1,0:T(8,128)(2,1)S(1)}, u32[]{:S(2)}, u32[]{:S(2)}) collective-permute-start(bf16[2,64,768]{2,1,0:T(8,128)(2,1)S(1)} %get-tuple-element.22.refs_0_.refs_2_.refs_6_.refs_8_), channel_id=1, source_target_pairs={{0,1},{1,0},{2,3},{3,2},{4,5},{5,4},{6,7},{7,6},{8,9},{9,8},{10,11... | collective-permute-start | bytes 589832 | tf_op jit(solution)/shard_map/ppermute | solution.py:92
  22.7 6.7 %collective-permute-start.10 = (bf16[1,64,768]{2,1,0:T(8,128)(2,1)S(1)}, bf16[1,64,768]{2,1,0:T(8,128)(2,1)S(1)}, u32[]{:S(2)}, u32[]{:S(2)}) collective-permute-start(bf16[1,64,768]{2,1,0:T(8,128)(2,1)S(1)} %get-tuple-element.29.refs_1_.refs_3_), channel_id=1, source_target_pairs={{0,1},{1,0},{2,3},{3,2},{4,5},{5,4},{6,7},{7,6},{8,9},{9,8},{10,11... | collective-permute-start | bytes 294920 | tf_op jit(solution)/shard_map/ppermute | solution.py:92
  26.2 4.9 %collective-permute-start.9 = (bf16[1,64,768]{2,1,0:T(8,128)(2,1)S(1)}, bf16[1,64,768]{2,1,0:T(8,128)(2,1)S(1)}, u32[]{:S(2)}, u32[]{:S(2)}) collective-permute-start(bf16[1,64,768]{2,1,0:T(8,128)(2,1)S(1)} %get-tuple-element.26.refs_7_.refs_9_.refs_1_), channel_id=1, source_target_pairs={{0,1},{1,0},{2,3},{3,2},{4,5},{5,4},{6,7},{7,6},{8,9},{9,8},{10,11... | collective-permute-start | bytes 294920 | tf_op jit(solution)/shard_map/ppermute | solution.py:92

commit v7 on v6

--- a/solution.py
+++ b/solution.py
@@ -87,9 +87,9 @@
     return lax.ppermute(x, axis, [(i, (i + by) % n) for i in range(n)])
 
 
-def swap(x, axis):
+def swap(x, axis, by=1):
     n = lax.axis_size(axis)
-    return lax.ppermute(x, axis, [(i, i ^ 1) for i in range(n)])
+    return lax.ppermute(x, axis, [(i, i ^ by) for i in range(n)])
 
 
 def label_kernel(rows_ref, ids_ref, out_ref):
@@ -112,21 +112,27 @@
 
 
 def join_kernel(order, kept, *refs):
-    outs = refs[len(refs) - 1 - kept :]
-    parts = [refs[at][...].astype(F32) for at in order]
+    outs = refs[-2:] if kept else refs[-1:]
+    even = lax.rem(lax.axis_index("expert") // 2, 2) == 0
+    parts = []
+    for at in order:
+        if isinstance(at, tuple):
+            parts.append(jnp.where(even, refs[at[0]][...].astype(F32), refs[at[1]][...].astype(F32)))
+        else:
+            parts.append(refs[at][...].astype(F32))
     outs[0][...] = jnp.concatenate(parts).astype(BF16)
     if kept:
-        outs[1][...] = refs[len(order)][...]
+        outs[1][...] = refs[kept][...]
 
 
 def join(parts, after, order=None, keep=False):
     order = tuple(range(len(parts))) if order is None else order
-    rows = sum(part.shape[0] for part in parts)
+    rows = sum(parts[at[0] if isinstance(at, tuple) else at].shape[0] for at in order)
     shapes = [jax.ShapeDtypeStruct((rows, parts[0].shape[1]), BF16)]
     if keep:
         shapes.append(jax.ShapeDtypeStruct(after[0].shape, BF16))
     made = pl.pallas_call(
-        functools.partial(join_kernel, order, int(keep)),
+        functools.partial(join_kernel, order, len(parts) if keep else 0),
         in_specs=[pl.BlockSpec(memory_space=pltpu.VMEM)] * (len(parts) + len(after)),
         out_specs=[pl.BlockSpec(memory_space=pltpu.VMEM)] * len(shapes),
         out_shape=shapes,
@@ -329,11 +335,13 @@
     *w_gate, gate_done = weights(gate_codes, gate_scales)
     far_own = swap(rows, "dp")
     ring = [shift(rows, "expert", by) for by in range(2, owners, 2)]
-    order = (0, *range(2, len(ring) + 1), 1)
+    order = (0, 2, (1, 3), (3, 1))
     near, far_own = join([rows] + ring, [far_own, gate_done], order, keep=True)
-    far_next = shift(far_own, "expert", 2)
-    far_ring = swap(join(ring[1:], [ring[0], gate_done]), "dp")
+    far_ring = swap(join(ring, [gate_done], (1, (0, 2))), "dp")
     near = (near, swap(near, "expert"))
+    far_own, held = lax.optimization_barrier((far_own, near[1]))
+    far_next = swap(far_own, "expert", 2)
+    near = (near[0], held)
     near_hidden, near_count, *w_up = near_units(near, w_gate, up_codes, up_scales)
     far = join([far_own, far_ring, far_next], [near_count])
     far = (far, swap(far, "expert"))
@@ -357,8 +365,7 @@
     owned, depth, width = gate_codes.shape
     fits = (
         lax.axis_size("dp") == 2
-        and lax.axis_size("expert") % 2 == 0
-        and lax.axis_size("expert") >= 6
+        and lax.axis_size("expert") == 8
         and width % (PARTS * LANES) == 0
         and depth % (16 * gate_scales.shape[1]) == 0
         and tokens.shape[0] * (lax.axis_size("expert") // 2) % 16 == 0

time: 33 us -> 32.8 us (level)
    ppermute x4 -> x3, starting transfers between devices: 7.93 us -> 7.03 us  [shift(): return lax.ppermute(x, axis, [(i, (i + by) % n) for i in range(n)])]
    ppermute x7 -> x8, starting transfers between devices: 6.9 us -> 7.68 us  [swap(): return lax.ppermute(x, axis, [(i, i ^ by) for i in range(n)])]
  transfers between devices with their start and end apart: 11 -> 11, of which waited for: 2 -> 1; matrix products, arithmetic and copies ran while one was open for 0% -> 0% of each run, Pallas kernels for 44% -> 45%
where the time goes in v7:
time: 32.8 us; the launch traced here: 32.6 us
  Pallas kernels  17.4 us (53%)
  starting transfers between devices  14.7 us (45%)
  waiting for transfers between devices  0.37 us (1%)
    ppermute x8, starting transfers between devices, swap(): return lax.ppermute(x, axis, [(i, i ^ by) for i in range(n)])  7.68 us
    ppermute x3, starting transfers between devices, shift(): return lax.ppermute(x, axis, [(i, (i + by) % n) for i in range(n)])  7.03 us
    pallas_call x3, Pallas kernels, gram_blocks(): pl.pallas_call(functools.partial(gram_kernel, jobs), in_specs=[pl.BlockSp...  5.97 us
    pallas_call x2, Pallas kernels, far_units(): pl.pallas_call(functools.partial(far_kernel, owned, expert), in_specs=[pl...  3.95 us
    pallas_call x1, Pallas kernels, near_units(): pl.pallas_call(functools.partial(near_kernel, owned), in_specs=[pl.BlockS...  3.87 us
    pallas_call x1, Pallas kernels, weights(): pl.pallas_call(weights_kernel, in_specs=[pl.BlockSpec(memory_space=pltpu....  2.45 us
    pallas_call x1, Pallas kernels, label(): pl.pallas_call(label_kernel, out_shape=jax.ShapeDtypeStruct((rows.shape[0...  1 us
  transfers between devices with their start and end apart: 11, of which 1 were waited for; matrix products, arithmetic and copies ran while one was open for 0% of the time, Pallas kernels for 45%

profile of v7, /device:TPU:0, one launch (start us, length us, event | category | flops | bytes accessed | tf_op | source)
XLA Modules:
  0.0 32.6 jit_solution(3865885556479010759)
XLA Ops:
  0.0 1.0 %shard_map.64.refs_0_ = bf16[8,4224]{1,0:T(8,128)(2,1)S(1)} custom-call(bf16[8,4096]{1,0:T(8,128)(2,1)} %rows_ref.1, s32[8,8]{1,0:T(8,128)} %ids_ref.1), custom_call_target="tpu_custom_call" | custom-call | flops 17179869184 | bytes 1048576 | tf_op jit(solution)/shard_map/pallas_call | solution.py:106
  1.0 0.0 copy-start.2
  1.0 3.1 %collective-permute-start = (bf16[8,4224]{1,0:T(8,128)(2,1)S(1)}, bf16[8,4224]{1,0:T(8,128)(2,1)S(1)}, u32[]{:S(2)}, u32[]{:S(2)}) collective-permute-start(bf16[8,4224]{1,0:T(8,128)(2,1)S(1)} %shard_map.64.refs_0_), channel_id=1, source_target_pairs={{0,4},{2,6},{4,8},{6,10},{8,12},{10,14},{12,0},{14,2},{1,5},{3,7},... | collective-permute-start | bytes 202760 | tf_op jit(solution)/shard_map/ppermute | solution.py:87
  4.1 2.6 %collective-permute-start.1 = (bf16[8,4224]{1,0:T(8,128)(2,1)S(1)}, bf16[8,4224]{1,0:T(8,128)(2,1)S(1)}, u32[]{:S(2)}, u32[]{:S(2)}) collective-permute-start(bf16[8,4224]{1,0:T(8,128)(2,1)S(1)} %shard_map.64.refs_0_), channel_id=1, source_target_pairs={{0,8},{2,10},{4,12},{6,14},{8,0},{10,2},{12,4},{14,6},{1,9},{3,11}... | collective-permute-start | bytes 202760 | tf_op jit(solution)/shard_map/ppermute | solution.py:87
  6.7 1.3 %collective-permute-start.2 = (bf16[8,4224]{1,0:T(8,128)(2,1)S(1)}, bf16[8,4224]{1,0:T(8,128)(2,1)S(1)}, u32[]{:S(2)}, u32[]{:S(2)}) collective-permute-start(bf16[8,4224]{1,0:T(8,128)(2,1)S(1)} %shard_map.64.refs_0_), channel_id=1, source_target_pairs={{0,12},{2,14},{4,0},{6,2},{8,4},{10,6},{12,8},{14,10},{1,13},{3,15... | collective-permute-start | bytes 202760 | tf_op jit(solution)/shard_map/ppermute | solution.py:87
  8.1 1.5 %collective-permute-start.3 = (bf16[8,4224]{1,0:T(8,128)(2,1)S(1)}, bf16[8,4224]{1,0:T(8,128)(2,1)S(1)}, u32[]{:S(2)}, u32[]{:S(2)}) collective-permute-start(bf16[8,4224]{1,0:T(8,128)(2,1)S(1)} %shard_map.64.refs_0_), channel_id=1, source_target_pairs={{0,1},{1,0},{2,3},{3,2},{4,5},{5,4},{6,7},{7,6},{8,9},{9,8},{10,11... | collective-permute-start | bytes 202760 | tf_op jit(solution)/shard_map/ppermute | solution.py:92
  9.6 2.5 %shard_map.65 = (bf16[4096,768]{1,0:T(8,128)(2,1)S(1)}, bf16[4096,768]{1,0:T(8,128)(2,1)S(1)}, f32[16,128]{1,0:T(8,128)S(1)}) custom-call(bf16[2,4096,768]{2,1,0:T(8,128)(2,1)S(1)} %copy-done, f32[2,32,768]{2,1,0:T(8,128)S(1)} %copy-done.1), custom_call_target="tpu_custom_call" | custom-call | flops 8589934592 | bytes 25165824 | tf_op jit(solution)/shard_map/pallas_call | solution.py:164
  12.0 0.0 collective-permute-done.refs_1_.refs_0_
  12.0 0.0 collective-permute-done.1.refs_2_.refs_1_
  12.0 0.0 collective-permute-done.2.refs_3_.refs_2_
  12.0 0.3 collective-permute-done.3.refs_4_
  12.3 0.1 shard_map.66
  12.4 0.1 collective-permute-start.4
  12.5 1.6 %collective-permute-start.5 = (bf16[16,4224]{1,0:T(8,128)(2,1)S(1)}, bf16[16,4224]{1,0:T(8,128)(2,1)S(1)}, u32[]{:S(2)}, u32[]{:S(2)}) collective-permute-start(bf16[16,4224]{1,0:T(8,128)(2,1)S(1)} %shard_map.68), channel_id=1, source_target_pairs={{0,1},{1,0},{2,3},{3,2},{4,5},{5,4},{6,7},{7,6},{8,9},{9,8},{10,11... | collective-permute-start | bytes 405512 | tf_op jit(solution)/shard_map/ppermute | solution.py:92
  14.1 0.0 collective-permute-done.4.theirs_ref
  14.1 0.8 %collective-permute-start.6 = (bf16[8,4224]{1,0:T(8,128)(2,1)S(1)}, bf16[8,4224]{1,0:T(8,128)(2,1)S(1)}, u32[]{:S(2)}, u32[]{:S(2)}) collective-permute-start(bf16[8,4224]{1,0:T(8,128)(2,1)S(1)} %get-tuple-element.27.refs_0_), channel_id=1, source_target_pairs={{0,4},{2,6},{4,0},{6,2},{8,12},{10,14},{12,8},{14,10},{1,5},{3,7},... | collective-permute-start | bytes 202760 | tf_op jit(solution)/shard_map/ppermute | solution.py:92
  15.0 3.9 %shard_map.67 = (bf16[2,64,768]{2,1,0:T(8,128)(2,1)S(1)}, f32[2,32,128]{2,1,0:T(8,128)S(1)}, bf16[4096,768]{1,0:T(8,128)(2,1)S(1)}, bf16[4096,768]{1,0:T(8,128)(2,1)S(1)}) custom-call(bf16[32,4224]{1,0:T(8,128)(2,1)S(1)} %get-tuple-element.21.mine_ref, bf16[32,4224]{1,0:T(8,128)(2,1)S(1)} %collective-permute-done.4.theirs_ref, ...), custom_call_target="tpu_custom_call" | custom-call | flops 8589934592 | bytes 25165824 | tf_op jit(solution)/shard_map/pallas_call | solution.py:217
  18.8 0.0 collective-permute-done.5.refs_1_
  18.8 0.0 collective-permute-done.6.refs_2_
  18.9 0.1 collective-permute-start.7
  19.0 1.5 %collective-permute-start.8 = (bf16[2,64,768]{2,1,0:T(8,128)(2,1)S(1)}, bf16[2,64,768]{2,1,0:T(8,128)(2,1)S(1)}, u32[]{:S(2)}, u32[]{:S(2)}) collective-permute-start(bf16[2,64,768]{2,1,0:T(8,128)(2,1)S(1)} %get-tuple-element.26.refs_0_.refs_2_.refs_6_.refs_8_), channel_id=1, source_target_pairs={{0,1},{1,0},{2,3},{3,2},{4,5},{5,4},{6,7},{7,6},{8,9},{9,8},{10,11... | collective-permute-start | bytes 589832 | tf_op jit(solution)/shard_map/ppermute | solution.py:92
  20.4 0.0 collective-permute-done.7.theirs_ref
  20.5 2.0 %shard_map.71 = (bf16[1,64,768]{2,1,0:T(8,128)(2,1)S(1)}, f32[1,32,128]{2,1,0:T(8,128)S(1)}) custom-call(bf16[32,4224]{1,0:T(8,128)(2,1)S(1)} %shard_map.69.mine_ref, bf16[32,4224]{1,0:T(8,128)(2,1)S(1)} %collective-permute-done.7.theirs_ref, bf16[4096,768]{1,0:T(8,128)(2,1)S(1)} %get-tuple-element.24.refs_0_.gate_ref, ...), custom_call_target="tpu_custom_call" | custom-call | flops 805306368 | bytes 12582912 | tf_op jit(solution)/shard_map/pallas_call | solution.py:253
  22.5 1.5 %collective-permute-start.10 = (bf16[1,64,768]{2,1,0:T(8,128)(2,1)S(1)}, bf16[1,64,768]{2,1,0:T(8,128)(2,1)S(1)}, u32[]{:S(2)}, u32[]{:S(2)}) collective-permute-start(bf16[1,64,768]{2,1,0:T(8,128)(2,1)S(1)} %get-tuple-element.33.refs_1_.refs_3_), channel_id=1, source_target_pairs={{0,1},{1,0},{2,3},{3,2},{4,5},{5,4},{6,7},{7,6},{8,9},{9,8},{10,11... | collective-permute-start | bytes 294920 | tf_op jit(solution)/shard_map/ppermute | solution.py:92
  24.0 2.0 %shard_map.70 = (bf16[1,64,768]{2,1,0:T(8,128)(2,1)S(1)}, f32[1,32,128]{2,1,0:T(8,128)S(1)}) custom-call(bf16[32,4224]{1,0:T(8,128)(2,1)S(1)} %shard_map.69.mine_ref, bf16[32,4224]{1,0:T(8,128)(2,1)S(1)} %collective-permute-done.7.theirs_ref, bf16[4096,768]{1,0:T(8,128)(2,1)S(1)} %get-tuple-element.25.refs_1_.gate_ref, ...), custom_call_target="tpu_custom_call" | custom-call | flops 805306368 | bytes 12582912 | tf_op jit(solution)/shard_map/pallas_call | solution.py:253
  25.9 0.7 %collective-permute-start.9 = (bf16[1,64,768]{2,1,0:T(8,128)(2,1)S(1)}, bf16[1,64,768]{2,1,0:T(8,128)(2,1)S(1)}, u32[]{:S(2)}, u32[]{:S(2)}) collective-permute-start(bf16[1,64,768]{2,1,0:T(8,128)(2,1)S(1)} %get-tuple-element.30.refs_7_.refs_9_.refs_1_), channel_id=1, source_target_pairs={{0,1},{1,0},{2,3},{3,2},{4,5},{5,4},{6,7},{7,6},{8,9},{9,8},{10,11... | collective-permute-start | bytes 294920 | tf_op jit(solution)/shard_map/ppermute | solution.py:92
  26.6 2.5 %shard_map.72.refs_6_ = f32[2,768,1536]{2,1,0:T(8,128)} custom-call(bf16[2,64,768]{2,1,0:T(8,128)(2,1)S(1)} %get-tuple-element.26.refs_0_.refs_2_.refs_6_.refs_8_, bf16[1,64,768]{2,1,0:T(8,128)(2,1)S(1)} %get-tuple-element.33.refs_1_.refs_3_, bf16[2,64,768]{2,1,0:T(8,128)(2,1)S(1)} %get-tuple-element.26.refs_0_.refs_2_.refs_6_.refs_8_, ...), custom_call_target="tpu_custom_call" | custom-call | flops 301989888 | bytes 4718592 | tf_op jit(solution)/shard_map/pallas_call | solution.py:310
  29.2 0.0 collective-permute-done.8.refs_2_
  29.2 0.0 collective-permute-done.10.refs_3_
  29.2 1.7 %shard_map.73.refs_6_ = f32[2,768,1536]{2,1,0:T(8,128)} custom-call(bf16[2,64,768]{2,1,0:T(8,128)(2,1)S(1)} %get-tuple-element.26.refs_0_.refs_2_.refs_6_.refs_8_, bf16[1,64,768]{2,1,0:T(8,128)(2,1)S(1)} %get-tuple-element.33.refs_1_.refs_3_, bf16[2,64,768]{2,1,0:T(8,128)(2,1)S(1)} %collective-permute-done.8.refs_2_, ...), custom_call_target="tpu_custom_call", output_to_operand_aliasing={{}: (6, {})} | custom-call | flops 150994944 | bytes 2359296 | tf_op jit(solution)/shard_map/pallas_call | solution.py:310
  30.9 0.0 collective-permute-done.9.refs_3_
  30.9 1.7 %shard_map.74 = f32[2,768,1536]{2,1,0:T(8,128)} custom-call(bf16[2,64,768]{2,1,0:T(8,128)(2,1)S(1)} %get-tuple-element.26.refs_0_.refs_2_.refs_6_.refs_8_, bf16[1,64,768]{2,1,0:T(8,128)(2,1)S(1)} %get-tuple-element.30.refs_7_.refs_9_.refs_1_, bf16[2,64,768]{2,1,0:T(8,128)(2,1)S(1)} %collective-permute-done.8.refs_2_, ...), custom_call_target="tpu_custom_call", output_to_operand_aliasing={{}: (6, {})} | custom-call | flops 150994944 | bytes 2359296 | tf_op jit(solution)/shard_map/pallas_call | solution.py:310
  (14 shorter events, 0.1 us)
Async XLA Ops:
  0.0 9.6 %copy-start.1 = (f32[2,32,768]{2,1,0:T(8,128)S(1)}, f32[2,32,768]{2,1,0:T(8,128)}, u32[]{:S(2)}) copy-start(f32[2,32,768]{2,1,0:T(8,128)} %scale_ref.2) | copy-start | bytes 589828
  0.0 9.6 %copy-start = (bf16[2,4096,768]{2,1,0:T(8,128)(2,1)S(1)}, bf16[2,4096,768]{2,1,0:T(8,128)(2,1)}, u32[]{:S(2)}) copy-start(bf16[2,4096,768]{2,1,0:T(8,128)(2,1)} %codes_ref.2) | copy-start | bytes 37748740
  0.0 14.9 %slice-start = ((s8[12582912]{0:T(1024)(128)(4,1)}), s8[4194304]{0:T(1024)(128)(4,1)S(1)}, s32[]{:S(2)}) async-start(s8[12582912]{0:T(1024)(128)(4,1)} %bitcast), calls=%async_computation | async-start | bytes 8388608
  0.0 14.9 %slice-start.1 = ((s8[12582912]{0:T(1024)(128)(4,1)}), s8[4194304]{0:T(1024)(128)(4,1)S(1)}, s32[]{:S(2)}) async-start(s8[12582912]{0:T(1024)(128)(4,1)} %bitcast), calls=%async_computation.1 | async-start | bytes 8388608
  1.0 13.9 %slice-start.2 = ((s8[12582912]{0:T(1024)(128)(4,1)}), s8[4194304]{0:T(1024)(128)(4,1)S(1)}, s32[]{:S(2)}) async-start(s8[12582912]{0:T(1024)(128)(4,1)} %bitcast), calls=%async_computation.2 | async-start | bytes 8388608
  1.0 13.9 %copy-start.2 = (f32[2,32,768]{2,1,0:T(8,128)S(1)}, f32[2,32,768]{2,1,0:T(8,128)}, u32[]{:S(2)}) copy-start(f32[2,32,768]{2,1,0:T(8,128)} %scale_ref.3) | copy-start | bytes 589828
  1.0 11.0 %collective-permute-start = (bf16[8,4224]{1,0:T(8,128)(2,1)S(1)}, bf16[8,4224]{1,0:T(8,128)(2,1)S(1)}, u32[]{:S(2)}, u32[]{:S(2)}) collective-permute-start(bf16[8,4224]{1,0:T(8,128)(2,1)S(1)} %shard_map.64.refs_0_), channel_id=1, source_target_pairs={{0,4},{2,6},{4,8},{6,10},{8,12},{10,14},{12,0},{14,2},{1,5},{3,7},... | collective-permute-start | bytes 202760 | tf_op jit(solution)/shard_map/ppermute | solution.py:87
  4.1 7.9 %collective-permute-start.1 = (bf16[8,4224]{1,0:T(8,128)(2,1)S(1)}, bf16[8,4224]{1,0:T(8,128)(2,1)S(1)}, u32[]{:S(2)}, u32[]{:S(2)}) collective-permute-start(bf16[8,4224]{1,0:T(8,128)(2,1)S(1)} %shard_map.64.refs_0_), channel_id=1, source_target_pairs={{0,8},{2,10},{4,12},{6,14},{8,0},{10,2},{12,4},{14,6},{1,9},{3,11}... | collective-permute-start | bytes 202760 | tf_op jit(solution)/shard_map/ppermute | solution.py:87
  6.7 5.3 %collective-permute-start.2 = (bf16[8,4224]{1,0:T(8,128)(2,1)S(1)}, bf16[8,4224]{1,0:T(8,128)(2,1)S(1)}, u32[]{:S(2)}, u32[]{:S(2)}) collective-permute-start(bf16[8,4224]{1,0:T(8,128)(2,1)S(1)} %shard_map.64.refs_0_), channel_id=1, source_target_pairs={{0,12},{2,14},{4,0},{6,2},{8,4},{10,6},{12,8},{14,10},{1,13},{3,15... | collective-permute-start | bytes 202760 | tf_op jit(solution)/shard_map/ppermute | solution.py:87
  8.1 4.3 %collective-permute-start.3 = (bf16[8,4224]{1,0:T(8,128)(2,1)S(1)}, bf16[8,4224]{1,0:T(8,128)(2,1)S(1)}, u32[]{:S(2)}, u32[]{:S(2)}) collective-permute-start(bf16[8,4224]{1,0:T(8,128)(2,1)S(1)} %shard_map.64.refs_0_), channel_id=1, source_target_pairs={{0,1},{1,0},{2,3},{3,2},{4,5},{5,4},{6,7},{7,6},{8,9},{9,8},{10,11... | collective-permute-start | bytes 202760 | tf_op jit(solution)/shard_map/ppermute | solution.py:92
  12.4 1.7 %collective-permute-start.4 = (bf16[32,4224]{1,0:T(8,128)(2,1)S(1)}, bf16[32,4224]{1,0:T(8,128)(2,1)S(1)}, u32[]{:S(2)}, u32[]{:S(2)}) collective-permute-start(bf16[32,4224]{1,0:T(8,128)(2,1)S(1)} %get-tuple-element.21.mine_ref), channel_id=1, source_target_pairs={{0,2},{2,0},{4,6},{6,4},{8,10},{10,8},{12,14},{14,12},{1,3},{3,1},... | collective-permute-start | bytes 811016 | tf_op jit(solution)/shard_map/ppermute | solution.py:92
  12.5 6.3 %collective-permute-start.5 = (bf16[16,4224]{1,0:T(8,128)(2,1)S(1)}, bf16[16,4224]{1,0:T(8,128)(2,1)S(1)}, u32[]{:S(2)}, u32[]{:S(2)}) collective-permute-start(bf16[16,4224]{1,0:T(8,128)(2,1)S(1)} %shard_map.68), channel_id=1, source_target_pairs={{0,1},{1,0},{2,3},{3,2},{4,5},{5,4},{6,7},{7,6},{8,9},{9,8},{10,11... | collective-permute-start | bytes 405512 | tf_op jit(solution)/shard_map/ppermute | solution.py:92
  14.1 4.8 %collective-permute-start.6 = (bf16[8,4224]{1,0:T(8,128)(2,1)S(1)}, bf16[8,4224]{1,0:T(8,128)(2,1)S(1)}, u32[]{:S(2)}, u32[]{:S(2)}) collective-permute-start(bf16[8,4224]{1,0:T(8,128)(2,1)S(1)} %get-tuple-element.27.refs_0_), channel_id=1, source_target_pairs={{0,4},{2,6},{4,0},{6,2},{8,12},{10,14},{12,8},{14,10},{1,5},{3,7},... | collective-permute-start | bytes 202760 | tf_op jit(solution)/shard_map/ppermute | solution.py:92
  18.9 1.6 %collective-permute-start.7 = (bf16[32,4224]{1,0:T(8,128)(2,1)S(1)}, bf16[32,4224]{1,0:T(8,128)(2,1)S(1)}, u32[]{:S(2)}, u32[]{:S(2)}) collective-permute-start(bf16[32,4224]{1,0:T(8,128)(2,1)S(1)} %shard_map.69.mine_ref), channel_id=1, source_target_pairs={{0,2},{2,0},{4,6},{6,4},{8,10},{10,8},{12,14},{14,12},{1,3},{3,1},... | collective-permute-start | bytes 811016 | tf_op jit(solution)/shard_map/ppermute | solution.py:92
  19.0 10.2 %collective-permute-start.8 = (bf16[2,64,768]{2,1,0:T(8,128)(2,1)S(1)}, bf16[2,64,768]{2,1,0:T(8,128)(2,1)S(1)}, u32[]{:S(2)}, u32[]{:S(2)}) collective-permute-start(bf16[2,64,768]{2,1,0:T(8,128)(2,1)S(1)} %get-tuple-element.26.refs_0_.refs_2_.refs_6_.refs_8_), channel_id=1, source_target_pairs={{0,1},{1,0},{2,3},{3,2},{4,5},{5,4},{6,7},{7,6},{8,9},{9,8},{10,11... | collective-permute-start | bytes 589832 | tf_op jit(solution)/shard_map/ppermute | solution.py:92
  22.5 6.7 %collective-permute-start.10 = (bf16[1,64,768]{2,1,0:T(8,128)(2,1)S(1)}, bf16[1,64,768]{2,1,0:T(8,128)(2,1)S(1)}, u32[]{:S(2)}, u32[]{:S(2)}) collective-permute-start(bf16[1,64,768]{2,1,0:T(8,128)(2,1)S(1)} %get-tuple-element.33.refs_1_.refs_3_), channel_id=1, source_target_pairs={{0,1},{1,0},{2,3},{3,2},{4,5},{5,4},{6,7},{7,6},{8,9},{9,8},{10,11... | collective-permute-start | bytes 294920 | tf_op jit(solution)/shard_map/ppermute | solution.py:92
  25.9 5.0 %collective-permute-start.9 = (bf16[1,64,768]{2,1,0:T(8,128)(2,1)S(1)}, bf16[1,64,768]{2,1,0:T(8,128)(2,1)S(1)}, u32[]{:S(2)}, u32[]{:S(2)}) collective-permute-start(bf16[1,64,768]{2,1,0:T(8,128)(2,1)S(1)} %get-tuple-element.30.refs_7_.refs_9_.refs_1_), channel_id=1, source_target_pairs={{0,1},{1,0},{2,3},{3,2},{4,5},{5,4},{6,7},{7,6},{8,9},{9,8},{10,11... | collective-permute-start | bytes 294920 | tf_op jit(solution)/shard_map/ppermute | solution.py:92

commit v8 on v7

--- a/solution.py
+++ b/solution.py
@@ -11,7 +11,7 @@
 LANES = 128
 NEAR_BLOCK = 768
 FAR_BLOCK = 128
-PARTS = 3
+PARTS = 6
 F32 = jnp.float32
 BF16 = jnp.bfloat16
 

time: 32.8 us -> 32.7 us (level)
  no operation moved by 1% of the time
where the time goes in v8:
time: 32.7 us; the launch traced here: 32.6 us
  Pallas kernels  17.3 us (53%)
  starting transfers between devices  14.7 us (45%)
  waiting for transfers between devices  0.37 us (1%)
    ppermute x8, starting transfers between devices, swap(): return lax.ppermute(x, axis, [(i, i ^ by) for i in range(n)])  7.68 us
    ppermute x3, starting transfers between devices, shift(): return lax.ppermute(x, axis, [(i, (i + by) % n) for i in range(n)])  7.03 us
    pallas_call x3, Pallas kernels, gram_blocks(): pl.pallas_call(functools.partial(gram_kernel, jobs), in_specs=[pl.BlockSp...  5.95 us
    pallas_call x2, Pallas kernels, far_units(): pl.pallas_call(functools.partial(far_kernel, owned, expert), in_specs=[pl...  3.95 us
    pallas_call x1, Pallas kernels, near_units(): pl.pallas_call(functools.partial(near_kernel, owned), in_specs=[pl.BlockS...  3.87 us
    pallas_call x1, Pallas kernels, weights(): pl.pallas_call(weights_kernel, in_specs=[pl.BlockSpec(memory_space=pltpu....  2.45 us
    pallas_call x1, Pallas kernels, label(): pl.pallas_call(label_kernel, out_shape=jax.ShapeDtypeStruct((rows.shape[0...  1 us
  transfers between devices with their start and end apart: 11, of which 1 were waited for; matrix products, arithmetic and copies ran while one was open for 0% of the time, Pallas kernels for 45%

profile of v8, /device:TPU:0, one launch (start us, length us, event | category | flops | bytes accessed | tf_op | source)
XLA Modules:
  0.0 32.6 jit_solution(12365009758011644455)
XLA Ops:
  0.0 1.0 %shard_map.64.refs_0_ = bf16[8,4224]{1,0:T(8,128)(2,1)S(1)} custom-call(bf16[8,4096]{1,0:T(8,128)(2,1)} %rows_ref.1, s32[8,8]{1,0:T(8,128)} %ids_ref.1), custom_call_target="tpu_custom_call" | custom-call | flops 17179869184 | bytes 1048576 | tf_op jit(solution)/shard_map/pallas_call | solution.py:106
  1.0 0.0 copy-start.2
  1.0 3.1 %collective-permute-start = (bf16[8,4224]{1,0:T(8,128)(2,1)S(1)}, bf16[8,4224]{1,0:T(8,128)(2,1)S(1)}, u32[]{:S(2)}, u32[]{:S(2)}) collective-permute-start(bf16[8,4224]{1,0:T(8,128)(2,1)S(1)} %shard_map.64.refs_0_), channel_id=1, source_target_pairs={{0,4},{2,6},{4,8},{6,10},{8,12},{10,14},{12,0},{14,2},{1,5},{3,7},... | collective-permute-start | bytes 202760 | tf_op jit(solution)/shard_map/ppermute | solution.py:87
  4.1 2.6 %collective-permute-start.1 = (bf16[8,4224]{1,0:T(8,128)(2,1)S(1)}, bf16[8,4224]{1,0:T(8,128)(2,1)S(1)}, u32[]{:S(2)}, u32[]{:S(2)}) collective-permute-start(bf16[8,4224]{1,0:T(8,128)(2,1)S(1)} %shard_map.64.refs_0_), channel_id=1, source_target_pairs={{0,8},{2,10},{4,12},{6,14},{8,0},{10,2},{12,4},{14,6},{1,9},{3,11}... | collective-permute-start | bytes 202760 | tf_op jit(solution)/shard_map/ppermute | solution.py:87
  6.7 1.3 %collective-permute-start.2 = (bf16[8,4224]{1,0:T(8,128)(2,1)S(1)}, bf16[8,4224]{1,0:T(8,128)(2,1)S(1)}, u32[]{:S(2)}, u32[]{:S(2)}) collective-permute-start(bf16[8,4224]{1,0:T(8,128)(2,1)S(1)} %shard_map.64.refs_0_), channel_id=1, source_target_pairs={{0,12},{2,14},{4,0},{6,2},{8,4},{10,6},{12,8},{14,10},{1,13},{3,15... | collective-permute-start | bytes 202760 | tf_op jit(solution)/shard_map/ppermute | solution.py:87
  8.1 1.5 %collective-permute-start.3 = (bf16[8,4224]{1,0:T(8,128)(2,1)S(1)}, bf16[8,4224]{1,0:T(8,128)(2,1)S(1)}, u32[]{:S(2)}, u32[]{:S(2)}) collective-permute-start(bf16[8,4224]{1,0:T(8,128)(2,1)S(1)} %shard_map.64.refs_0_), channel_id=1, source_target_pairs={{0,1},{1,0},{2,3},{3,2},{4,5},{5,4},{6,7},{7,6},{8,9},{9,8},{10,11... | collective-permute-start | bytes 202760 | tf_op jit(solution)/shard_map/ppermute | solution.py:92
  9.6 2.5 %shard_map.65 = (bf16[4096,768]{1,0:T(8,128)(2,1)S(1)}, bf16[4096,768]{1,0:T(8,128)(2,1)S(1)}, f32[16,128]{1,0:T(8,128)S(1)}) custom-call(bf16[2,4096,768]{2,1,0:T(8,128)(2,1)S(1)} %copy-done, f32[2,32,768]{2,1,0:T(8,128)S(1)} %copy-done.1), custom_call_target="tpu_custom_call" | custom-call | flops 8589934592 | bytes 25165824 | tf_op jit(solution)/shard_map/pallas_call | solution.py:164
  12.0 0.0 collective-permute-done.refs_1_.refs_0_
  12.0 0.0 collective-permute-done.1.refs_2_.refs_1_
  12.0 0.0 collective-permute-done.2.refs_3_.refs_2_
  12.0 0.3 collective-permute-done.3.refs_4_
  12.3 0.1 shard_map.66
  12.4 0.1 collective-permute-start.4
  12.5 1.6 %collective-permute-start.5 = (bf16[16,4224]{1,0:T(8,128)(2,1)S(1)}, bf16[16,4224]{1,0:T(8,128)(2,1)S(1)}, u32[]{:S(2)}, u32[]{:S(2)}) collective-permute-start(bf16[16,4224]{1,0:T(8,128)(2,1)S(1)} %shard_map.68), channel_id=1, source_target_pairs={{0,1},{1,0},{2,3},{3,2},{4,5},{5,4},{6,7},{7,6},{8,9},{9,8},{10,11... | collective-permute-start | bytes 405512 | tf_op jit(solution)/shard_map/ppermute | solution.py:92
  14.1 0.0 collective-permute-done.4.theirs_ref
  14.1 0.8 %collective-permute-start.6 = (bf16[8,4224]{1,0:T(8,128)(2,1)S(1)}, bf16[8,4224]{1,0:T(8,128)(2,1)S(1)}, u32[]{:S(2)}, u32[]{:S(2)}) collective-permute-start(bf16[8,4224]{1,0:T(8,128)(2,1)S(1)} %get-tuple-element.27.refs_0_), channel_id=1, source_target_pairs={{0,4},{2,6},{4,0},{6,2},{8,12},{10,14},{12,8},{14,10},{1,5},{3,7},... | collective-permute-start | bytes 202760 | tf_op jit(solution)/shard_map/ppermute | solution.py:92
  15.0 3.9 %shard_map.67 = (bf16[2,64,768]{2,1,0:T(8,128)(2,1)S(1)}, f32[2,32,128]{2,1,0:T(8,128)S(1)}, bf16[4096,768]{1,0:T(8,128)(2,1)S(1)}, bf16[4096,768]{1,0:T(8,128)(2,1)S(1)}) custom-call(bf16[32,4224]{1,0:T(8,128)(2,1)S(1)} %get-tuple-element.21.mine_ref, bf16[32,4224]{1,0:T(8,128)(2,1)S(1)} %collective-permute-done.4.theirs_ref, ...), custom_call_target="tpu_custom_call" | custom-call | flops 8589934592 | bytes 25165824 | tf_op jit(solution)/shard_map/pallas_call | solution.py:217
  18.8 0.0 collective-permute-done.5.refs_1_
  18.8 0.0 collective-permute-done.6.refs_2_
  18.9 0.1 collective-permute-start.7
  19.0 1.5 %collective-permute-start.8 = (bf16[2,64,768]{2,1,0:T(8,128)(2,1)S(1)}, bf16[2,64,768]{2,1,0:T(8,128)(2,1)S(1)}, u32[]{:S(2)}, u32[]{:S(2)}) collective-permute-start(bf16[2,64,768]{2,1,0:T(8,128)(2,1)S(1)} %get-tuple-element.26.refs_0_.refs_2_.refs_6_.refs_8_), channel_id=1, source_target_pairs={{0,1},{1,0},{2,3},{3,2},{4,5},{5,4},{6,7},{7,6},{8,9},{9,8},{10,11... | collective-permute-start | bytes 589832 | tf_op jit(solution)/shard_map/ppermute | solution.py:92
  20.4 0.0 collective-permute-done.7.theirs_ref
  20.5 2.0 %shard_map.71 = (bf16[1,64,768]{2,1,0:T(8,128)(2,1)S(1)}, f32[1,32,128]{2,1,0:T(8,128)S(1)}) custom-call(bf16[32,4224]{1,0:T(8,128)(2,1)S(1)} %shard_map.69.mine_ref, bf16[32,4224]{1,0:T(8,128)(2,1)S(1)} %collective-permute-done.7.theirs_ref, bf16[4096,768]{1,0:T(8,128)(2,1)S(1)} %get-tuple-element.24.refs_0_.gate_ref, ...), custom_call_target="tpu_custom_call" | custom-call | flops 805306368 | bytes 12582912 | tf_op jit(solution)/shard_map/pallas_call | solution.py:253
  22.5 1.5 %collective-permute-start.10 = (bf16[1,64,768]{2,1,0:T(8,128)(2,1)S(1)}, bf16[1,64,768]{2,1,0:T(8,128)(2,1)S(1)}, u32[]{:S(2)}, u32[]{:S(2)}) collective-permute-start(bf16[1,64,768]{2,1,0:T(8,128)(2,1)S(1)} %get-tuple-element.33.refs_1_.refs_3_), channel_id=1, source_target_pairs={{0,1},{1,0},{2,3},{3,2},{4,5},{5,4},{6,7},{7,6},{8,9},{9,8},{10,11... | collective-permute-start | bytes 294920 | tf_op jit(solution)/shard_map/ppermute | solution.py:92
  24.0 2.0 %shard_map.70 = (bf16[1,64,768]{2,1,0:T(8,128)(2,1)S(1)}, f32[1,32,128]{2,1,0:T(8,128)S(1)}) custom-call(bf16[32,4224]{1,0:T(8,128)(2,1)S(1)} %shard_map.69.mine_ref, bf16[32,4224]{1,0:T(8,128)(2,1)S(1)} %collective-permute-done.7.theirs_ref, bf16[4096,768]{1,0:T(8,128)(2,1)S(1)} %get-tuple-element.25.refs_1_.gate_ref, ...), custom_call_target="tpu_custom_call" | custom-call | flops 805306368 | bytes 12582912 | tf_op jit(solution)/shard_map/pallas_call | solution.py:253
  25.9 0.7 %collective-permute-start.9 = (bf16[1,64,768]{2,1,0:T(8,128)(2,1)S(1)}, bf16[1,64,768]{2,1,0:T(8,128)(2,1)S(1)}, u32[]{:S(2)}, u32[]{:S(2)}) collective-permute-start(bf16[1,64,768]{2,1,0:T(8,128)(2,1)S(1)} %get-tuple-element.30.refs_7_.refs_9_.refs_1_), channel_id=1, source_target_pairs={{0,1},{1,0},{2,3},{3,2},{4,5},{5,4},{6,7},{7,6},{8,9},{9,8},{10,11... | collective-permute-start | bytes 294920 | tf_op jit(solution)/shard_map/ppermute | solution.py:92
  26.6 2.5 %shard_map.72.refs_6_ = f32[2,768,1536]{2,1,0:T(8,128)} custom-call(bf16[2,64,768]{2,1,0:T(8,128)(2,1)S(1)} %get-tuple-element.26.refs_0_.refs_2_.refs_6_.refs_8_, bf16[1,64,768]{2,1,0:T(8,128)(2,1)S(1)} %get-tuple-element.33.refs_1_.refs_3_, bf16[2,64,768]{2,1,0:T(8,128)(2,1)S(1)} %get-tuple-element.26.refs_0_.refs_2_.refs_6_.refs_8_, ...), custom_call_target="tpu_custom_call" | custom-call | flops 301989888 | bytes 4718592 | tf_op jit(solution)/shard_map/pallas_call | solution.py:310
  29.1 0.0 collective-permute-done.8.refs_2_
  29.1 0.0 collective-permute-done.10.refs_3_
  29.2 1.7 %shard_map.73.refs_6_ = f32[2,768,1536]{2,1,0:T(8,128)} custom-call(bf16[2,64,768]{2,1,0:T(8,128)(2,1)S(1)} %get-tuple-element.26.refs_0_.refs_2_.refs_6_.refs_8_, bf16[1,64,768]{2,1,0:T(8,128)(2,1)S(1)} %get-tuple-element.33.refs_1_.refs_3_, bf16[2,64,768]{2,1,0:T(8,128)(2,1)S(1)} %collective-permute-done.8.refs_2_, ...), custom_call_target="tpu_custom_call", output_to_operand_aliasing={{}: (6, {})} | custom-call | flops 150994944 | bytes 2359296 | tf_op jit(solution)/shard_map/pallas_call | solution.py:310
  30.9 0.0 collective-permute-done.9.refs_3_
  30.9 1.7 %shard_map.74 = f32[2,768,1536]{2,1,0:T(8,128)} custom-call(bf16[2,64,768]{2,1,0:T(8,128)(2,1)S(1)} %get-tuple-element.26.refs_0_.refs_2_.refs_6_.refs_8_, bf16[1,64,768]{2,1,0:T(8,128)(2,1)S(1)} %get-tuple-element.30.refs_7_.refs_9_.refs_1_, bf16[2,64,768]{2,1,0:T(8,128)(2,1)S(1)} %collective-permute-done.8.refs_2_, ...), custom_call_target="tpu_custom_call", output_to_operand_aliasing={{}: (6, {})} | custom-call | flops 150994944 | bytes 2359296 | tf_op jit(solution)/shard_map/pallas_call | solution.py:310
  (14 shorter events, 0.1 us)
Async XLA Ops:
  0.0 9.6 %copy-start.1 = (f32[2,32,768]{2,1,0:T(8,128)S(1)}, f32[2,32,768]{2,1,0:T(8,128)}, u32[]{:S(2)}) copy-start(f32[2,32,768]{2,1,0:T(8,128)} %scale_ref.2) | copy-start | bytes 589828
  0.0 9.6 %copy-start = (bf16[2,4096,768]{2,1,0:T(8,128)(2,1)S(1)}, bf16[2,4096,768]{2,1,0:T(8,128)(2,1)}, u32[]{:S(2)}) copy-start(bf16[2,4096,768]{2,1,0:T(8,128)(2,1)} %codes_ref.2) | copy-start | bytes 37748740
  0.0 14.9 %slice-start = ((s8[12582912]{0:T(1024)(128)(4,1)}), s8[4194304]{0:T(1024)(128)(4,1)S(1)}, s32[]{:S(2)}) async-start(s8[12582912]{0:T(1024)(128)(4,1)} %bitcast), calls=%async_computation | async-start | bytes 8388608
  0.0 14.9 %slice-start.1 = ((s8[12582912]{0:T(1024)(128)(4,1)}), s8[4194304]{0:T(1024)(128)(4,1)S(1)}, s32[]{:S(2)}) async-start(s8[12582912]{0:T(1024)(128)(4,1)} %bitcast), calls=%async_computation.1 | async-start | bytes 8388608
  1.0 13.9 %slice-start.2 = ((s8[12582912]{0:T(1024)(128)(4,1)}), s8[4194304]{0:T(1024)(128)(4,1)S(1)}, s32[]{:S(2)}) async-start(s8[12582912]{0:T(1024)(128)(4,1)} %bitcast), calls=%async_computation.2 | async-start | bytes 8388608
  1.0 13.9 %copy-start.2 = (f32[2,32,768]{2,1,0:T(8,128)S(1)}, f32[2,32,768]{2,1,0:T(8,128)}, u32[]{:S(2)}) copy-start(f32[2,32,768]{2,1,0:T(8,128)} %scale_ref.3) | copy-start | bytes 589828
  1.0 11.0 %collective-permute-start = (bf16[8,4224]{1,0:T(8,128)(2,1)S(1)}, bf16[8,4224]{1,0:T(8,128)(2,1)S(1)}, u32[]{:S(2)}, u32[]{:S(2)}) collective-permute-start(bf16[8,4224]{1,0:T(8,128)(2,1)S(1)} %shard_map.64.refs_0_), channel_id=1, source_target_pairs={{0,4},{2,6},{4,8},{6,10},{8,12},{10,14},{12,0},{14,2},{1,5},{3,7},... | collective-permute-start | bytes 202760 | tf_op jit(solution)/shard_map/ppermute | solution.py:87
  4.1 7.9 %collective-permute-start.1 = (bf16[8,4224]{1,0:T(8,128)(2,1)S(1)}, bf16[8,4224]{1,0:T(8,128)(2,1)S(1)}, u32[]{:S(2)}, u32[]{:S(2)}) collective-permute-start(bf16[8,4224]{1,0:T(8,128)(2,1)S(1)} %shard_map.64.refs_0_), channel_id=1, source_target_pairs={{0,8},{2,10},{4,12},{6,14},{8,0},{10,2},{12,4},{14,6},{1,9},{3,11}... | collective-permute-start | bytes 202760 | tf_op jit(solution)/shard_map/ppermute | solution.py:87
  6.7 5.3 %collective-permute-start.2 = (bf16[8,4224]{1,0:T(8,128)(2,1)S(1)}, bf16[8,4224]{1,0:T(8,128)(2,1)S(1)}, u32[]{:S(2)}, u32[]{:S(2)}) collective-permute-start(bf16[8,4224]{1,0:T(8,128)(2,1)S(1)} %shard_map.64.refs_0_), channel_id=1, source_target_pairs={{0,12},{2,14},{4,0},{6,2},{8,4},{10,6},{12,8},{14,10},{1,13},{3,15... | collective-permute-start | bytes 202760 | tf_op jit(solution)/shard_map/ppermute | solution.py:87
  8.1 4.3 %collective-permute-start.3 = (bf16[8,4224]{1,0:T(8,128)(2,1)S(1)}, bf16[8,4224]{1,0:T(8,128)(2,1)S(1)}, u32[]{:S(2)}, u32[]{:S(2)}) collective-permute-start(bf16[8,4224]{1,0:T(8,128)(2,1)S(1)} %shard_map.64.refs_0_), channel_id=1, source_target_pairs={{0,1},{1,0},{2,3},{3,2},{4,5},{5,4},{6,7},{7,6},{8,9},{9,8},{10,11... | collective-permute-start | bytes 202760 | tf_op jit(solution)/shard_map/ppermute | solution.py:92
  12.4 1.7 %collective-permute-start.4 = (bf16[32,4224]{1,0:T(8,128)(2,1)S(1)}, bf16[32,4224]{1,0:T(8,128)(2,1)S(1)}, u32[]{:S(2)}, u32[]{:S(2)}) collective-permute-start(bf16[32,4224]{1,0:T(8,128)(2,1)S(1)} %get-tuple-element.21.mine_ref), channel_id=1, source_target_pairs={{0,2},{2,0},{4,6},{6,4},{8,10},{10,8},{12,14},{14,12},{1,3},{3,1},... | collective-permute-start | bytes 811016 | tf_op jit(solution)/shard_map/ppermute | solution.py:92
  12.5 6.3 %collective-permute-start.5 = (bf16[16,4224]{1,0:T(8,128)(2,1)S(1)}, bf16[16,4224]{1,0:T(8,128)(2,1)S(1)}, u32[]{:S(2)}, u32[]{:S(2)}) collective-permute-start(bf16[16,4224]{1,0:T(8,128)(2,1)S(1)} %shard_map.68), channel_id=1, source_target_pairs={{0,1},{1,0},{2,3},{3,2},{4,5},{5,4},{6,7},{7,6},{8,9},{9,8},{10,11... | collective-permute-start | bytes 405512 | tf_op jit(solution)/shard_map/ppermute | solution.py:92
  14.1 4.8 %collective-permute-start.6 = (bf16[8,4224]{1,0:T(8,128)(2,1)S(1)}, bf16[8,4224]{1,0:T(8,128)(2,1)S(1)}, u32[]{:S(2)}, u32[]{:S(2)}) collective-permute-start(bf16[8,4224]{1,0:T(8,128)(2,1)S(1)} %get-tuple-element.27.refs_0_), channel_id=1, source_target_pairs={{0,4},{2,6},{4,0},{6,2},{8,12},{10,14},{12,8},{14,10},{1,5},{3,7},... | collective-permute-start | bytes 202760 | tf_op jit(solution)/shard_map/ppermute | solution.py:92
  18.9 1.6 %collective-permute-start.7 = (bf16[32,4224]{1,0:T(8,128)(2,1)S(1)}, bf16[32,4224]{1,0:T(8,128)(2,1)S(1)}, u32[]{:S(2)}, u32[]{:S(2)}) collective-permute-start(bf16[32,4224]{1,0:T(8,128)(2,1)S(1)} %shard_map.69.mine_ref), channel_id=1, source_target_pairs={{0,2},{2,0},{4,6},{6,4},{8,10},{10,8},{12,14},{14,12},{1,3},{3,1},... | collective-permute-start | bytes 811016 | tf_op jit(solution)/shard_map/ppermute | solution.py:92
  19.0 10.2 %collective-permute-start.8 = (bf16[2,64,768]{2,1,0:T(8,128)(2,1)S(1)}, bf16[2,64,768]{2,1,0:T(8,128)(2,1)S(1)}, u32[]{:S(2)}, u32[]{:S(2)}) collective-permute-start(bf16[2,64,768]{2,1,0:T(8,128)(2,1)S(1)} %get-tuple-element.26.refs_0_.refs_2_.refs_6_.refs_8_), channel_id=1, source_target_pairs={{0,1},{1,0},{2,3},{3,2},{4,5},{5,4},{6,7},{7,6},{8,9},{9,8},{10,11... | collective-permute-start | bytes 589832 | tf_op jit(solution)/shard_map/ppermute | solution.py:92
  22.5 6.7 %collective-permute-start.10 = (bf16[1,64,768]{2,1,0:T(8,128)(2,1)S(1)}, bf16[1,64,768]{2,1,0:T(8,128)(2,1)S(1)}, u32[]{:S(2)}, u32[]{:S(2)}) collective-permute-start(bf16[1,64,768]{2,1,0:T(8,128)(2,1)S(1)} %get-tuple-element.33.refs_1_.refs_3_), channel_id=1, source_target_pairs={{0,1},{1,0},{2,3},{3,2},{4,5},{5,4},{6,7},{7,6},{8,9},{9,8},{10,11... | collective-permute-start | bytes 294920 | tf_op jit(solution)/shard_map/ppermute | solution.py:92
  25.9 4.9 %collective-permute-start.9 = (bf16[1,64,768]{2,1,0:T(8,128)(2,1)S(1)}, bf16[1,64,768]{2,1,0:T(8,128)(2,1)S(1)}, u32[]{:S(2)}, u32[]{:S(2)}) collective-permute-start(bf16[1,64,768]{2,1,0:T(8,128)(2,1)S(1)} %get-tuple-element.30.refs_7_.refs_9_.refs_1_), channel_id=1, source_target_pairs={{0,1},{1,0},{2,3},{3,2},{4,5},{5,4},{6,7},{7,6},{8,9},{9,8},{10,11... | collective-permute-start | bytes 294920 | tf_op jit(solution)/shard_map/ppermute | solution.py:92

commit v9 on v7

--- a/solution.py
+++ b/solution.py
@@ -9,6 +9,7 @@
 
 TOP = 8
 LANES = 128
+LABEL = 256
 NEAR_BLOCK = 768
 FAR_BLOCK = 128
 PARTS = 3
@@ -95,7 +96,7 @@
 def label_kernel(rows_ref, ids_ref, out_ref):
     depth = rows_ref.shape[1]
     ids = ids_ref[...].astype(F32).astype(BF16)
-    blank = jnp.full((ids.shape[0], LANES - ids.shape[1]), -1, BF16)
+    blank = jnp.full((ids.shape[0], LABEL - ids.shape[1]), -1, BF16)
     out_ref[:, :depth] = rows_ref[...]
     out_ref[:, depth:] = jnp.concatenate([ids, blank], axis=1)
 
@@ -105,7 +106,7 @@
     ids = pltpu.with_memory_space_constraint(ids, pltpu.HBM)
     return pl.pallas_call(
         label_kernel,
-        out_shape=jax.ShapeDtypeStruct((rows.shape[0], rows.shape[1] + LANES), BF16),
+        out_shape=jax.ShapeDtypeStruct((rows.shape[0], rows.shape[1] + LABEL), BF16),
         compiler_params=pltpu.CompilerParams(vmem_limit_bytes=2 << 20),
         cost_estimate=pl.CostEstimate(flops=cost, bytes_accessed=1 << 20, transcendentals=0),
     )(rows, ids)

time: 32.8 us -> 32.8 us (level)
  transfers between devices with their start and end apart: 11 -> 11, of which waited for: 1 -> 1; matrix products, arithmetic and copies ran while one was open for 0% -> 0% of each run, Pallas kernels for 45% -> 44%
where the time goes in v9:
time: 32.8 us; the launch traced here: 32.7 us
  Pallas kernels  17.2 us (52%)
  starting transfers between devices  14.9 us (45%)
  waiting for transfers between devices  0.39 us (1%)
    ppermute x8, starting transfers between devices, swap(): return lax.ppermute(x, axis, [(i, i ^ by) for i in range(n)])  7.84 us
    ppermute x3, starting transfers between devices, shift(): return lax.ppermute(x, axis, [(i, (i + by) % n) for i in range(n)])  7.03 us
    pallas_call x3, Pallas kernels, gram_blocks(): pl.pallas_call(functools.partial(gram_kernel, jobs), in_specs=[pl.BlockSp...  5.98 us
    pallas_call x1, Pallas kernels, near_units(): pl.pallas_call(functools.partial(near_kernel, owned), in_specs=[pl.BlockS...  3.95 us
    pallas_call x2, Pallas kernels, far_units(): pl.pallas_call(functools.partial(far_kernel, owned, expert), in_specs=[pl...  3.74 us
    pallas_call x1, Pallas kernels, weights(): pl.pallas_call(weights_kernel, in_specs=[pl.BlockSpec(memory_space=pltpu....  2.45 us
    pallas_call x1, Pallas kernels, label(): pl.pallas_call(label_kernel, out_shape=jax.ShapeDtypeStruct((rows.shape[0...  1 us
  transfers between devices with their start and end apart: 11, of which 1 were waited for; matrix products, arithmetic and copies ran while one was open for 0% of the time, Pallas kernels for 44%

profile of v9, /device:TPU:0, one launch (start us, length us, event | category | flops | bytes accessed | tf_op | source)
XLA Modules:
  0.0 32.7 jit_solution(5811218500755331385)
XLA Ops:
  0.0 1.0 %shard_map.64.refs_0_ = bf16[8,4352]{1,0:T(8,128)(2,1)S(1)} custom-call(bf16[8,4096]{1,0:T(8,128)(2,1)} %rows_ref.1, s32[8,8]{1,0:T(8,128)} %ids_ref.1), custom_call_target="tpu_custom_call" | custom-call | flops 17179869184 | bytes 1048576 | tf_op jit(solution)/shard_map/pallas_call | solution.py:107
  1.0 0.0 slice-start.2
  1.0 0.0 copy-start.2
  1.0 3.1 %collective-permute-start = (bf16[8,4352]{1,0:T(8,128)(2,1)S(1)}, bf16[8,4352]{1,0:T(8,128)(2,1)S(1)}, u32[]{:S(2)}, u32[]{:S(2)}) collective-permute-start(bf16[8,4352]{1,0:T(8,128)(2,1)S(1)} %shard_map.64.refs_0_), channel_id=1, source_target_pairs={{0,4},{2,6},{4,8},{6,10},{8,12},{10,14},{12,0},{14,2},{1,5},{3,7},... | collective-permute-start | bytes 208904 | tf_op jit(solution)/shard_map/ppermute | solution.py:88
  4.1 2.6 %collective-permute-start.1 = (bf16[8,4352]{1,0:T(8,128)(2,1)S(1)}, bf16[8,4352]{1,0:T(8,128)(2,1)S(1)}, u32[]{:S(2)}, u32[]{:S(2)}) collective-permute-start(bf16[8,4352]{1,0:T(8,128)(2,1)S(1)} %shard_map.64.refs_0_), channel_id=1, source_target_pairs={{0,8},{2,10},{4,12},{6,14},{8,0},{10,2},{12,4},{14,6},{1,9},{3,11}... | collective-permute-start | bytes 208904 | tf_op jit(solution)/shard_map/ppermute | solution.py:88
  6.7 1.3 %collective-permute-start.2 = (bf16[8,4352]{1,0:T(8,128)(2,1)S(1)}, bf16[8,4352]{1,0:T(8,128)(2,1)S(1)}, u32[]{:S(2)}, u32[]{:S(2)}) collective-permute-start(bf16[8,4352]{1,0:T(8,128)(2,1)S(1)} %shard_map.64.refs_0_), channel_id=1, source_target_pairs={{0,12},{2,14},{4,0},{6,2},{8,4},{10,6},{12,8},{14,10},{1,13},{3,15... | collective-permute-start | bytes 208904 | tf_op jit(solution)/shard_map/ppermute | solution.py:88
  8.1 1.5 %collective-permute-start.3 = (bf16[8,4352]{1,0:T(8,128)(2,1)S(1)}, bf16[8,4352]{1,0:T(8,128)(2,1)S(1)}, u32[]{:S(2)}, u32[]{:S(2)}) collective-permute-start(bf16[8,4352]{1,0:T(8,128)(2,1)S(1)} %shard_map.64.refs_0_), channel_id=1, source_target_pairs={{0,1},{1,0},{2,3},{3,2},{4,5},{5,4},{6,7},{7,6},{8,9},{9,8},{10,11... | collective-permute-start | bytes 208904 | tf_op jit(solution)/shard_map/ppermute | solution.py:93
  9.6 2.5 %shard_map.65 = (bf16[4096,768]{1,0:T(8,128)(2,1)S(1)}, bf16[4096,768]{1,0:T(8,128)(2,1)S(1)}, f32[16,128]{1,0:T(8,128)S(1)}) custom-call(bf16[2,4096,768]{2,1,0:T(8,128)(2,1)S(1)} %copy-done, f32[2,32,768]{2,1,0:T(8,128)S(1)} %copy-done.1), custom_call_target="tpu_custom_call" | custom-call | flops 8589934592 | bytes 25165824 | tf_op jit(solution)/shard_map/pallas_call | solution.py:165
  12.0 0.0 collective-permute-done.refs_1_.refs_0_
  12.0 0.0 collective-permute-done.1.refs_2_.refs_1_
  12.0 0.0 collective-permute-done.2.refs_3_.refs_2_
  12.1 0.3 collective-permute-done.3.refs_4_
  12.4 0.1 shard_map.66
  12.4 0.1 collective-permute-start.4
  12.6 1.6 %collective-permute-start.5 = (bf16[16,4352]{1,0:T(8,128)(2,1)S(1)}, bf16[16,4352]{1,0:T(8,128)(2,1)S(1)}, u32[]{:S(2)}, u32[]{:S(2)}) collective-permute-start(bf16[16,4352]{1,0:T(8,128)(2,1)S(1)} %shard_map.68), channel_id=1, source_target_pairs={{0,1},{1,0},{2,3},{3,2},{4,5},{5,4},{6,7},{7,6},{8,9},{9,8},{10,11... | collective-permute-start | bytes 417800 | tf_op jit(solution)/shard_map/ppermute | solution.py:93
  14.1 0.0 collective-permute-done.4.theirs_ref
  14.1 1.0 %collective-permute-start.6 = (bf16[8,4352]{1,0:T(8,128)(2,1)S(1)}, bf16[8,4352]{1,0:T(8,128)(2,1)S(1)}, u32[]{:S(2)}, u32[]{:S(2)}) collective-permute-start(bf16[8,4352]{1,0:T(8,128)(2,1)S(1)} %get-tuple-element.27.refs_0_), channel_id=1, source_target_pairs={{0,4},{2,6},{4,0},{6,2},{8,12},{10,14},{12,8},{14,10},{1,5},{3,7},... | collective-permute-start | bytes 208904 | tf_op jit(solution)/shard_map/ppermute | solution.py:93
  15.1 4.0 %shard_map.67 = (bf16[2,64,768]{2,1,0:T(8,128)(2,1)S(1)}, f32[2,32,128]{2,1,0:T(8,128)S(1)}, bf16[4096,768]{1,0:T(8,128)(2,1)S(1)}, bf16[4096,768]{1,0:T(8,128)(2,1)S(1)}) custom-call(bf16[32,4352]{1,0:T(8,128)(2,1)S(1)} %get-tuple-element.21.mine_ref, bf16[32,4352]{1,0:T(8,128)(2,1)S(1)} %collective-permute-done.4.theirs_ref, ...), custom_call_target="tpu_custom_call" | custom-call | flops 8589934592 | bytes 25165824 | tf_op jit(solution)/shard_map/pallas_call | solution.py:218
  19.1 0.0 collective-permute-done.5.refs_1_
  19.1 0.0 collective-permute-done.6.refs_2_
  19.1 0.1 collective-permute-start.7
  19.2 1.5 %collective-permute-start.8 = (bf16[2,64,768]{2,1,0:T(8,128)(2,1)S(1)}, bf16[2,64,768]{2,1,0:T(8,128)(2,1)S(1)}, u32[]{:S(2)}, u32[]{:S(2)}) collective-permute-start(bf16[2,64,768]{2,1,0:T(8,128)(2,1)S(1)} %get-tuple-element.26.refs_0_.refs_2_.refs_6_.refs_8_), channel_id=1, source_target_pairs={{0,1},{1,0},{2,3},{3,2},{4,5},{5,4},{6,7},{7,6},{8,9},{9,8},{10,11... | collective-permute-start | bytes 589832 | tf_op jit(solution)/shard_map/ppermute | solution.py:93
  20.7 0.0 collective-permute-done.7.theirs_ref
  20.8 1.9 %shard_map.71 = (bf16[1,64,768]{2,1,0:T(8,128)(2,1)S(1)}, f32[1,32,128]{2,1,0:T(8,128)S(1)}) custom-call(bf16[32,4352]{1,0:T(8,128)(2,1)S(1)} %shard_map.69.mine_ref, bf16[32,4352]{1,0:T(8,128)(2,1)S(1)} %collective-permute-done.7.theirs_ref, bf16[4096,768]{1,0:T(8,128)(2,1)S(1)} %get-tuple-element.24.refs_0_.gate_ref, ...), custom_call_target="tpu_custom_call" | custom-call | flops 805306368 | bytes 12582912 | tf_op jit(solution)/shard_map/pallas_call | solution.py:254
  22.6 1.5 %collective-permute-start.10 = (bf16[1,64,768]{2,1,0:T(8,128)(2,1)S(1)}, bf16[1,64,768]{2,1,0:T(8,128)(2,1)S(1)}, u32[]{:S(2)}, u32[]{:S(2)}) collective-permute-start(bf16[1,64,768]{2,1,0:T(8,128)(2,1)S(1)} %get-tuple-element.33.refs_1_.refs_3_), channel_id=1, source_target_pairs={{0,1},{1,0},{2,3},{3,2},{4,5},{5,4},{6,7},{7,6},{8,9},{9,8},{10,11... | collective-permute-start | bytes 294920 | tf_op jit(solution)/shard_map/ppermute | solution.py:93
  24.1 1.9 %shard_map.70 = (bf16[1,64,768]{2,1,0:T(8,128)(2,1)S(1)}, f32[1,32,128]{2,1,0:T(8,128)S(1)}) custom-call(bf16[32,4352]{1,0:T(8,128)(2,1)S(1)} %shard_map.69.mine_ref, bf16[32,4352]{1,0:T(8,128)(2,1)S(1)} %collective-permute-done.7.theirs_ref, bf16[4096,768]{1,0:T(8,128)(2,1)S(1)} %get-tuple-element.25.refs_1_.gate_ref, ...), custom_call_target="tpu_custom_call" | custom-call | flops 805306368 | bytes 12582912 | tf_op jit(solution)/shard_map/pallas_call | solution.py:254
  26.0 0.7 %collective-permute-start.9 = (bf16[1,64,768]{2,1,0:T(8,128)(2,1)S(1)}, bf16[1,64,768]{2,1,0:T(8,128)(2,1)S(1)}, u32[]{:S(2)}, u32[]{:S(2)}) collective-permute-start(bf16[1,64,768]{2,1,0:T(8,128)(2,1)S(1)} %get-tuple-element.30.refs_7_.refs_9_.refs_1_), channel_id=1, source_target_pairs={{0,1},{1,0},{2,3},{3,2},{4,5},{5,4},{6,7},{7,6},{8,9},{9,8},{10,11... | collective-permute-start | bytes 294920 | tf_op jit(solution)/shard_map/ppermute | solution.py:93
  26.7 2.5 %shard_map.72.refs_6_ = f32[2,768,1536]{2,1,0:T(8,128)} custom-call(bf16[2,64,768]{2,1,0:T(8,128)(2,1)S(1)} %get-tuple-element.26.refs_0_.refs_2_.refs_6_.refs_8_, bf16[1,64,768]{2,1,0:T(8,128)(2,1)S(1)} %get-tuple-element.33.refs_1_.refs_3_, bf16[2,64,768]{2,1,0:T(8,128)(2,1)S(1)} %get-tuple-element.26.refs_0_.refs_2_.refs_6_.refs_8_, ...), custom_call_target="tpu_custom_call" | custom-call | flops 301989888 | bytes 4718592 | tf_op jit(solution)/shard_map/pallas_call | solution.py:311
  29.2 0.0 collective-permute-done.8.refs_2_
  29.2 0.0 collective-permute-done.10.refs_3_
  29.2 1.7 %shard_map.73.refs_6_ = f32[2,768,1536]{2,1,0:T(8,128)} custom-call(bf16[2,64,768]{2,1,0:T(8,128)(2,1)S(1)} %get-tuple-element.26.refs_0_.refs_2_.refs_6_.refs_8_, bf16[1,64,768]{2,1,0:T(8,128)(2,1)S(1)} %get-tuple-element.33.refs_1_.refs_3_, bf16[2,64,768]{2,1,0:T(8,128)(2,1)S(1)} %collective-permute-done.8.refs_2_, ...), custom_call_target="tpu_custom_call", output_to_operand_aliasing={{}: (6, {})} | custom-call | flops 150994944 | bytes 2359296 | tf_op jit(solution)/shard_map/pallas_call | solution.py:311
  31.0 1.7 %shard_map.74 = f32[2,768,1536]{2,1,0:T(8,128)} custom-call(bf16[2,64,768]{2,1,0:T(8,128)(2,1)S(1)} %get-tuple-element.26.refs_0_.refs_2_.refs_6_.refs_8_, bf16[1,64,768]{2,1,0:T(8,128)(2,1)S(1)} %get-tuple-element.30.refs_7_.refs_9_.refs_1_, bf16[2,64,768]{2,1,0:T(8,128)(2,1)S(1)} %collective-permute-done.8.refs_2_, ...), custom_call_target="tpu_custom_call", output_to_operand_aliasing={{}: (6, {})} | custom-call | flops 150994944 | bytes 2359296 | tf_op jit(solution)/shard_map/pallas_call | solution.py:311
  (14 shorter events, 0.1 us)
Async XLA Ops:
  0.0 9.6 %copy-start.1 = (f32[2,32,768]{2,1,0:T(8,128)S(1)}, f32[2,32,768]{2,1,0:T(8,128)}, u32[]{:S(2)}) copy-start(f32[2,32,768]{2,1,0:T(8,128)} %scale_ref.2) | copy-start | bytes 589828
  0.0 9.6 %copy-start = (bf16[2,4096,768]{2,1,0:T(8,128)(2,1)S(1)}, bf16[2,4096,768]{2,1,0:T(8,128)(2,1)}, u32[]{:S(2)}) copy-start(bf16[2,4096,768]{2,1,0:T(8,128)(2,1)} %codes_ref.2) | copy-start | bytes 37748740
  0.0 15.1 %slice-start = ((s8[12582912]{0:T(1024)(128)(4,1)}), s8[4194304]{0:T(1024)(128)(4,1)S(1)}, s32[]{:S(2)}) async-start(s8[12582912]{0:T(1024)(128)(4,1)} %bitcast), calls=%async_computation | async-start | bytes 8388608
  0.0 15.1 %slice-start.1 = ((s8[12582912]{0:T(1024)(128)(4,1)}), s8[4194304]{0:T(1024)(128)(4,1)S(1)}, s32[]{:S(2)}) async-start(s8[12582912]{0:T(1024)(128)(4,1)} %bitcast), calls=%async_computation.1 | async-start | bytes 8388608
  1.0 14.1 %slice-start.2 = ((s8[12582912]{0:T(1024)(128)(4,1)}), s8[4194304]{0:T(1024)(128)(4,1)S(1)}, s32[]{:S(2)}) async-start(s8[12582912]{0:T(1024)(128)(4,1)} %bitcast), calls=%async_computation.2 | async-start | bytes 8388608
  1.0 14.1 %copy-start.2 = (f32[2,32,768]{2,1,0:T(8,128)S(1)}, f32[2,32,768]{2,1,0:T(8,128)}, u32[]{:S(2)}) copy-start(f32[2,32,768]{2,1,0:T(8,128)} %scale_ref.3) | copy-start | bytes 589828
  1.0 11.0 %collective-permute-start = (bf16[8,4352]{1,0:T(8,128)(2,1)S(1)}, bf16[8,4352]{1,0:T(8,128)(2,1)S(1)}, u32[]{:S(2)}, u32[]{:S(2)}) collective-permute-start(bf16[8,4352]{1,0:T(8,128)(2,1)S(1)} %shard_map.64.refs_0_), channel_id=1, source_target_pairs={{0,4},{2,6},{4,8},{6,10},{8,12},{10,14},{12,0},{14,2},{1,5},{3,7},... | collective-permute-start | bytes 208904 | tf_op jit(solution)/shard_map/ppermute | solution.py:88
  4.1 7.9 %collective-permute-start.1 = (bf16[8,4352]{1,0:T(8,128)(2,1)S(1)}, bf16[8,4352]{1,0:T(8,128)(2,1)S(1)}, u32[]{:S(2)}, u32[]{:S(2)}) collective-permute-start(bf16[8,4352]{1,0:T(8,128)(2,1)S(1)} %shard_map.64.refs_0_), channel_id=1, source_target_pairs={{0,8},{2,10},{4,12},{6,14},{8,0},{10,2},{12,4},{14,6},{1,9},{3,11}... | collective-permute-start | bytes 208904 | tf_op jit(solution)/shard_map/ppermute | solution.py:88
  6.7 5.3 %collective-permute-start.2 = (bf16[8,4352]{1,0:T(8,128)(2,1)S(1)}, bf16[8,4352]{1,0:T(8,128)(2,1)S(1)}, u32[]{:S(2)}, u32[]{:S(2)}) collective-permute-start(bf16[8,4352]{1,0:T(8,128)(2,1)S(1)} %shard_map.64.refs_0_), channel_id=1, source_target_pairs={{0,12},{2,14},{4,0},{6,2},{8,4},{10,6},{12,8},{14,10},{1,13},{3,15... | collective-permute-start | bytes 208904 | tf_op jit(solution)/shard_map/ppermute | solution.py:88
  8.1 4.3 %collective-permute-start.3 = (bf16[8,4352]{1,0:T(8,128)(2,1)S(1)}, bf16[8,4352]{1,0:T(8,128)(2,1)S(1)}, u32[]{:S(2)}, u32[]{:S(2)}) collective-permute-start(bf16[8,4352]{1,0:T(8,128)(2,1)S(1)} %shard_map.64.refs_0_), channel_id=1, source_target_pairs={{0,1},{1,0},{2,3},{3,2},{4,5},{5,4},{6,7},{7,6},{8,9},{9,8},{10,11... | collective-permute-start | bytes 208904 | tf_op jit(solution)/shard_map/ppermute | solution.py:93
  12.4 1.7 %collective-permute-start.4 = (bf16[32,4352]{1,0:T(8,128)(2,1)S(1)}, bf16[32,4352]{1,0:T(8,128)(2,1)S(1)}, u32[]{:S(2)}, u32[]{:S(2)}) collective-permute-start(bf16[32,4352]{1,0:T(8,128)(2,1)S(1)} %get-tuple-element.21.mine_ref), channel_id=1, source_target_pairs={{0,2},{2,0},{4,6},{6,4},{8,10},{10,8},{12,14},{14,12},{1,3},{3,1},... | collective-permute-start | bytes 835592 | tf_op jit(solution)/shard_map/ppermute | solution.py:93
  12.6 6.5 %collective-permute-start.5 = (bf16[16,4352]{1,0:T(8,128)(2,1)S(1)}, bf16[16,4352]{1,0:T(8,128)(2,1)S(1)}, u32[]{:S(2)}, u32[]{:S(2)}) collective-permute-start(bf16[16,4352]{1,0:T(8,128)(2,1)S(1)} %shard_map.68), channel_id=1, source_target_pairs={{0,1},{1,0},{2,3},{3,2},{4,5},{5,4},{6,7},{7,6},{8,9},{9,8},{10,11... | collective-permute-start | bytes 417800 | tf_op jit(solution)/shard_map/ppermute | solution.py:93
  14.1 5.0 %collective-permute-start.6 = (bf16[8,4352]{1,0:T(8,128)(2,1)S(1)}, bf16[8,4352]{1,0:T(8,128)(2,1)S(1)}, u32[]{:S(2)}, u32[]{:S(2)}) collective-permute-start(bf16[8,4352]{1,0:T(8,128)(2,1)S(1)} %get-tuple-element.27.refs_0_), channel_id=1, source_target_pairs={{0,4},{2,6},{4,0},{6,2},{8,12},{10,14},{12,8},{14,10},{1,5},{3,7},... | collective-permute-start | bytes 208904 | tf_op jit(solution)/shard_map/ppermute | solution.py:93
  19.1 1.6 %collective-permute-start.7 = (bf16[32,4352]{1,0:T(8,128)(2,1)S(1)}, bf16[32,4352]{1,0:T(8,128)(2,1)S(1)}, u32[]{:S(2)}, u32[]{:S(2)}) collective-permute-start(bf16[32,4352]{1,0:T(8,128)(2,1)S(1)} %shard_map.69.mine_ref), channel_id=1, source_target_pairs={{0,2},{2,0},{4,6},{6,4},{8,10},{10,8},{12,14},{14,12},{1,3},{3,1},... | collective-permute-start | bytes 835592 | tf_op jit(solution)/shard_map/ppermute | solution.py:93
  19.2 10.0 %collective-permute-start.8 = (bf16[2,64,768]{2,1,0:T(8,128)(2,1)S(1)}, bf16[2,64,768]{2,1,0:T(8,128)(2,1)S(1)}, u32[]{:S(2)}, u32[]{:S(2)}) collective-permute-start(bf16[2,64,768]{2,1,0:T(8,128)(2,1)S(1)} %get-tuple-element.26.refs_0_.refs_2_.refs_6_.refs_8_), channel_id=1, source_target_pairs={{0,1},{1,0},{2,3},{3,2},{4,5},{5,4},{6,7},{7,6},{8,9},{9,8},{10,11... | collective-permute-start | bytes 589832 | tf_op jit(solution)/shard_map/ppermute | solution.py:93
  22.6 6.6 %collective-permute-start.10 = (bf16[1,64,768]{2,1,0:T(8,128)(2,1)S(1)}, bf16[1,64,768]{2,1,0:T(8,128)(2,1)S(1)}, u32[]{:S(2)}, u32[]{:S(2)}) collective-permute-start(bf16[1,64,768]{2,1,0:T(8,128)(2,1)S(1)} %get-tuple-element.33.refs_1_.refs_3_), channel_id=1, source_target_pairs={{0,1},{1,0},{2,3},{3,2},{4,5},{5,4},{6,7},{7,6},{8,9},{9,8},{10,11... | collective-permute-start | bytes 294920 | tf_op jit(solution)/shard_map/ppermute | solution.py:93
  26.0 5.0 %collective-permute-start.9 = (bf16[1,64,768]{2,1,0:T(8,128)(2,1)S(1)}, bf16[1,64,768]{2,1,0:T(8,128)(2,1)S(1)}, u32[]{:S(2)}, u32[]{:S(2)}) collective-permute-start(bf16[1,64,768]{2,1,0:T(8,128)(2,1)S(1)} %get-tuple-element.30.refs_7_.refs_9_.refs_1_), channel_id=1, source_target_pairs={{0,1},{1,0},{2,3},{3,2},{4,5},{5,4},{6,7},{7,6},{8,9},{9,8},{10,11... | collective-permute-start | bytes 294920 | tf_op jit(solution)/shard_map/ppermute | solution.py:93
